TPU v7x, 512 devices: a whole 4x4x16 slice. The times are simulated.
512 devices in a mesh: ia: 8 (over y, core), wa: 8 (over z_lo), ao: 8 (over x, z_hi).
Axes of the slice: x: 4, y: 4, z: 16 (z_hi: 2, z_lo: 8; z = z_hi * 8 + z_lo), core: 2. Of those that a mesh axis runs over, the one named last changes fastest.
Arguments:
- tokens: bfloat16 [1024, 8192], P(('ia', 'ao'), 'wa'), may hold values from -6 to 6
- w_in: bfloat16 [8192, 16384], P('wa', ('ao', 'ia')), may hold values from -0.0625 to 0.0625
- w_out: bfloat16 [16384, 8192], P(('ao', 'ia'), 'wa'), may hold values from -0.046875 to 0.046875
- grad_out: bfloat16 [1024, 8192], P(('ia', 'ao'), 'wa'), may hold values from -6 to 6
Outputs:
- block_out: bfloat16 [1024, 8192], P(('ia', 'ao'), 'wa')
- grad_in: bfloat16 [1024, 8192], P(('ia', 'ao'), 'wa')
- grad_w_in: bfloat16 [8192, 16384], P('wa', ('ao', 'ia'))
- grad_w_out: bfloat16 [16384, 8192], P(('ao', 'ia'), 'wa')
All inputs are finite; a program needn't handle non-finite values.
Results may differ from a plain program's by a relative error of at most 0.0049.
Values may be sent and summed in bfloat16 or wider, within the bound.
No kernel may reach another device: no remote copies, remote signals or barrier semaphores. Data moves between devices by JAX's collectives and lax.ppermute only.
A program may use at most 64 MiB of HBM per device.

v0:
```python
import jax
import jax.numpy as jnp
from jax import lax
from jax.sharding import PartitionSpec as P

inv_root_two = 0.7071067811865476
inv_root_tau = 0.3989422804014327


def gelu_pair(hidden):
    normal_cdf = 0.5 * (1.0 + lax.erf(hidden * inv_root_two))
    density = jnp.exp(-0.5 * hidden * hidden) * inv_root_tau
    return (hidden * normal_cdf, normal_cdf + hidden * density)


def contract_last(left, right):
    return lax.dot_general(
        left, right, (((1,), (1,)), ((), ())), preferred_element_type=jnp.float32
    )


def contract_first(left, right):
    return lax.dot_general(
        left, right, (((0,), (0,)), ((), ())), preferred_element_type=jnp.float32
    )


def shards(tokens, w_in, w_out, grad_out):
    x_block, dy_block = (
        lax.all_gather(tokens, "ao", axis=0, tiled=True),
        lax.all_gather(grad_out, "ao", axis=0, tiled=True),
    )
    w_in_block, w_out_block = (
        lax.all_gather(w_in, "ia", axis=1, tiled=True),
        lax.all_gather(w_out, "ia", axis=0, tiled=True),
    )
    partial_value = jnp.dot(x_block, w_in_block, preferred_element_type=jnp.float32)
    hidden = lax.psum(partial_value, "wa")
    act_full, slope = gelu_pair(hidden)
    act = act_full.astype(jnp.bfloat16)
    out_partial = jnp.dot(act, w_out_block, preferred_element_type=jnp.float32)
    block_out = lax.psum_scatter(out_partial, "ao", scatter_dimension=0, tiled=True).astype(
        jnp.bfloat16
    )
    grad_partial = contract_last(dy_block, w_out_block)
    grad_act = lax.psum(grad_partial, "wa")
    grad_hidden = (grad_act * slope).astype(jnp.bfloat16)
    input_partial = contract_last(grad_hidden, w_in_block)
    grad_in = lax.psum_scatter(input_partial, "ao", scatter_dimension=0, tiled=True).astype(
        jnp.bfloat16
    )
    x_all, dy_all = (
        lax.all_gather(x_block, "ia", axis=0, tiled=True),
        lax.all_gather(dy_block, "ia", axis=0, tiled=True),
    )
    act_cols, grad_cols = (
        lax.all_to_all(act, "ia", split_axis=1, concat_axis=0, tiled=True),
        lax.all_to_all(grad_hidden, "ia", split_axis=1, concat_axis=0, tiled=True),
    )
    grad_w_in = contract_first(x_all, grad_cols).astype(jnp.bfloat16)
    grad_w_out = contract_first(act_cols, dy_all).astype(jnp.bfloat16)
    return (block_out, grad_in, grad_w_in, grad_w_out)


def solution(mesh):
    return jax.shard_map(
        shards,
        mesh=mesh,
        in_specs=(
            P(("ia", "ao"), "wa"),
            P("wa", ("ao", "ia")),
            P(("ao", "ia"), "wa"),
            P(("ia", "ao"), "wa"),
        ),
        out_specs=(
            P(("ia", "ao"), "wa"),
            P(("ia", "ao"), "wa"),
            P("wa", ("ao", "ia")),
            P(("ao", "ia"), "wa"),
        ),
        check_vma=False,
    )
```

profile of v0, /device:TPU:1, one launch (start us, length us, event | category | flops | bytes accessed | tf_op | source)
XLA Modules:
  0.0 596.5 jit_solution(10044472118763450671)
XLA Ops:
  7.2 0.7 all-gather.5.cloned.1.call-update
  7.9 0.7 all-gather.7.cloned.1.call-update
  8.7 65.3 %all_gather.18 = bf16[128,1024]{1,0:T(8,128)(2,1)S(1)} all-gather(bf16[16,1024]{1,0:T(8,128)(2,1)} %param.4), channel_id=1, replica_groups=mesh['ia'=8,'wa'=8,'ao'=8] {'ao'}, dimensions={0}, use_global_device_ids=true | all-gather | bytes 294912 | tf_op jit(solution)/shard_map/all_gather | solution.py:30
  74.0 64.1 %all_gather.21 = bf16[128,1024]{1,0:T(8,128)(2,1)S(1)} all-gather(bf16[16,1024]{1,0:T(8,128)(2,1)} %param.7), channel_id=1, replica_groups=mesh['ia'=8,'wa'=8,'ao'=8] {'ao'}, dimensions={0}, use_global_device_ids=true | all-gather | bytes 294912 | tf_op jit(solution)/shard_map/all_gather | solution.py:31
  138.1 4.0 fusion.7
  142.1 4.7 fusion.9
  148.0 142.7 %all-reduce.3.cloned.1.call-done = (f32[128,2048]{1,0:T(8,128)}, f32[128,2048]{1,0:T(8,128)}) async-done(((f32[128,2048]{1,0:T(8,128)}, f32[128,2048]{1,0:T(8,128)}), (f32[128,2048]{1,0:T(8,128)}, f32[128,2048]{1,0:T(8,128)})) %all-reduce.3.cloned.1.call-update) | async-done | bytes 2097168 | tf_op jit(solution)/shard_map/psum | solution.py:38
  290.7 2.0 fusion.6
  292.7 4.5 fusion.10
  297.3 0.8 copy.17
  298.1 9.4 %all-to-all-start = ((bf16[128,8,256]{2,0,1:T(8,128)(2,1)}), bf16[128,8,256]{2,0,1:T(8,128)(2,1)S(1)}, u32[]{:S(2)}, u32[]{:S(2)}) async-start(bf16[128,8,256]{2,0,1:T(8,128)(2,1)} %bitcast.27), calls=%async_computation.2 | async-start | bytes 1048576 | tf_op jit(solution)/shard_map/all_to_all | solution.py:58
  307.6 3.7 fusion.8
  311.3 0.8 copy.16
  312.1 6.5 %all-to-all-done = bf16[128,8,256]{2,0,1:T(8,128)(2,1)S(1)} async-done(((bf16[128,8,256]{2,0,1:T(8,128)(2,1)}), bf16[128,8,256]{2,0,1:T(8,128)(2,1)S(1)}, u32[]{:S(2)}, u32[]{:S(2)}) %all-to-all-start) | async-done | bytes 524320 | tf_op jit(solution)/shard_map/all_to_all | solution.py:58
  318.6 5.2 all-to-all-start.1
  323.8 5.2 all-gather.9.cloned.1.call-done
  329.0 2.3 fusion
  331.4 1.0 copy.11
  332.4 33.3 %all-gather.11.cloned.1.call-done = bf16[1024,1024]{1,0:T(8,128)(2,1)} async-done(((bf16[128,1024]{1,0:T(8,128)(2,1)}), bf16[1024,1024]{1,0:T(8,128)(2,1)}) %all-gather.11.cloned.1.call-update) | async-done | bytes 2097168 | tf_op jit(solution)/shard_map/all_gather | solution.py:54
  365.7 3.1 convolution_convert_fusion
  368.8 111.6 %reduce-scatter.5.cloned.1.call-done = f32[16,1024]{1,0:T(8,128)} async-done(((f32[128,1024]{1,0:T(8,128)}), f32[16,1024]{1,0:T(8,128)}) %reduce-scatter.5.cloned.1.call-update) | async-done | bytes 65552 | tf_op jit(solution)/shard_map/reduce_scatter | solution.py:49
  480.4 1.5 convert_element_type.24
  481.8 106.3 %reduce-scatter.3.cloned.1.call-done = f32[16,1024]{1,0:T(8,128)} async-done(((f32[128,1024]{1,0:T(8,128)}), f32[16,1024]{1,0:T(8,128)}) %reduce-scatter.3.cloned.1.call-update) | async-done | bytes 65552 | tf_op jit(solution)/shard_map/reduce_scatter | solution.py:42
  588.2 1.5 convert_element_type.22
  (19 shorter events, 1.4 us)
Async XLA Ops:
  7.2 130.9 %all-gather.5.cloned.1.call-start = ((), (), s32[]{:S(2)}) async-start(), calls=%async_computation.4 | async-start | bytes 4718592 | tf_op jit(solution)/shard_map/all_gather | solution.py:34
  7.9 134.2 %all-gather.7.cloned.1.call-start = ((), (), s32[]{:S(2)}) async-start(), calls=%async_computation.5 | async-start | bytes 4718592 | tf_op jit(solution)/shard_map/all_gather | solution.py:35
  8.6 282.0 %all-reduce.3.cloned.1.call-start = ((), (), s32[]{:S(2)}) async-start(), calls=%async_computation.10 | async-start | bytes 4194304 | tf_op jit(solution)/shard_map/psum | solution.py:38
  74.0 72.8 %copy-start.1 = (bf16[128,1024]{1,0:T(8,128)(2,1)}, bf16[128,1024]{1,0:T(8,128)(2,1)S(1)}, u32[]{:S(2)}) copy-start(bf16[128,1024]{1,0:T(8,128)(2,1)S(1)} %all_gather.18) | copy-start | bytes 786436
  138.1 8.7 %copy-start = (bf16[128,1024]{1,0:T(8,128)(2,1)}, bf16[128,1024]{1,0:T(8,128)(2,1)S(1)}, u32[]{:S(2)}) copy-start(bf16[128,1024]{1,0:T(8,128)(2,1)S(1)} %all_gather.21) | copy-start | bytes 786436
  146.8 182.2 %all-gather.9.cloned.1.call-start = ((), (), s32[]{:S(2)}) async-start(), calls=%async_computation.8 | async-start | bytes 2359296 | tf_op jit(solution)/shard_map/all_gather | solution.py:53
  147.4 218.3 %all-gather.11.cloned.1.call-start = ((), (), s32[]{:S(2)}) async-start(), calls=%async_computation.9 | async-start | bytes 2359296 | tf_op jit(solution)/shard_map/all_gather | solution.py:54
  148.0 332.4 %reduce-scatter.5.cloned.1.call-start = ((), (), s32[]{:S(2)}) async-start(), calls=%async_computation.7 | async-start | bytes 589824 | tf_op jit(solution)/shard_map/reduce_scatter | solution.py:49
  298.1 20.5 %all-to-all-start = ((bf16[128,8,256]{2,0,1:T(8,128)(2,1)}), bf16[128,8,256]{2,0,1:T(8,128)(2,1)S(1)}, u32[]{:S(2)}, u32[]{:S(2)}) async-start(bf16[128,8,256]{2,0,1:T(8,128)(2,1)} %bitcast.27), calls=%async_computation.2 | async-start | bytes 1048576 | tf_op jit(solution)/shard_map/all_to_all | solution.py:58
  307.5 280.6 %reduce-scatter.3.cloned.1.call-start = ((), (), s32[]{:S(2)}) async-start(), calls=%async_computation.6 | async-start | bytes 589824 | tf_op jit(solution)/shard_map/reduce_scatter | solution.py:42
  318.6 47.1 %all-to-all-start.1 = ((bf16[128,8,256]{2,0,1:T(8,128)(2,1)}), bf16[128,8,256]{2,0,1:T(8,128)(2,1)S(1)}, u32[]{:S(2)}, u32[]{:S(2)}) async-start(bf16[128,8,256]{2,0,1:T(8,128)(2,1)} %bitcast.26), calls=%async_computation.3 | async-start | bytes 1048576 | tf_op jit(solution)/shard_map/all_to_all | solution.py:57
Sparse Core Ops, SparseCore 0:
  10.1 49.4 all-gather.4
  61.8 40.8 all-gather.6
  146.9 143.7 all-reduce.2
  293.3 35.7 all-gather.8
  331.0 34.6 all-gather.10
  370.0 110.3 reduce-scatter.4
  485.5 102.6 reduce-scatter.2
where the time goes:
time: 598 us; the launch traced here: 596 us
  waiting for transfers between devices  408 us (68%)
  blocking collectives  129 us (22%)
  matrix products  22.3 us (4%)
  starting transfers between devices  14.9 us (2%)
  between operations  14.1 us (2%)
    psum x1, waiting for transfers between devices, shards(): hidden = lax.psum(partial_value, 'wa')  143 us
    reduce_scatter x1, waiting for transfers between devices, shards(): lax.psum_scatter(input_partial, 'ao', scatter_dimension=0, tiled=True)  112 us
    reduce_scatter x1, waiting for transfers between devices, shards(): lax.psum_scatter(out_partial, 'ao', scatter_dimension=0, tiled=True)  106 us
    all_gather x1, blocking collectives, shards(): lax.all_gather(tokens, 'ao', axis=0, tiled=True)  65.3 us
    all_gather x1, blocking collectives, shards(): lax.all_gather(grad_out, 'ao', axis=0, tiled=True)  64.1 us
    all_gather x1, waiting for transfers between devices, shards(): lax.all_gather(dy_block, 'ia', axis=0, tiled=True)  33.3 us
  transfers between devices with their start and end apart: 9, of which 6 were waited for; matrix products, arithmetic and copies ran while one was open for 4% of the time, Pallas kernels for 0%

commit v1 on v0

v1 whole, which is shorter than its diff:
```python
import jax
import jax.numpy as jnp
from jax import lax
from jax.sharding import Mesh, PartitionSpec as P

inv_root_two = 0.7071067811865476
inv_root_tau = 0.3989422804014327
bf16 = jnp.bfloat16
f32 = jnp.float32


def gelu_pair(hidden):
    normal_cdf = 0.5 * (1.0 + lax.erf(hidden * inv_root_two))
    density = jnp.exp(-0.5 * hidden * hidden) * inv_root_tau
    return (hidden * normal_cdf, normal_cdf + hidden * density)


def dot_nn(left, right):
    return jnp.dot(left, right, preferred_element_type=f32)


def dot_nt(left, right):
    return lax.dot_general(
        left, right, (((1,), (1,)), ((), ())), preferred_element_type=f32
    )


def dot_tn(left, right):
    return lax.dot_general(
        left, right, (((0,), (0,)), ((), ())), preferred_element_type=f32
    )


def swap(value, axis):
    return lax.ppermute(value, axis, [(0, 1), (1, 0)])


def exchange(value, axes):
    return lax.all_to_all(value, axes, 0, 0, tiled=True)


def gather_tokens(pair, which):
    copies = jnp.broadcast_to(pair[None], (16,) + pair.shape)
    return exchange(copies, ("y", "x")).reshape(512, pair.shape[1])


def sum_over_z(partial):
    parts = partial.astype(bf16).reshape(8, 64, 512)
    return jnp.sum(exchange(parts, "z").astype(f32), axis=0)


def gather_z(value):
    copies = jnp.broadcast_to(value[None], (8,) + value.shape)
    return exchange(copies, "z").reshape(512, 512)


def sum_tokens(partial):
    parts = partial.astype(bf16).reshape(16, 32, partial.shape[1])
    return jnp.sum(exchange(parts, ("y", "x")).astype(f32), axis=0)


def shards(tokens, w_in, w_out, grad_out):
    high = lax.axis_index("h") == 1
    w_in_b = swap(w_in, "c")
    w_out_b = swap(w_out, "c")
    both = jnp.stack([tokens, grad_out])
    other = swap(both, "h")
    low_rows = jnp.where(high, other, both)
    high_rows = jnp.where(high, both, other)
    pairs = jnp.concatenate([low_rows, high_rows], axis=1)
    x_half = gather_tokens(pairs[0], "x")
    dy_half = gather_tokens(pairs[1], "dy")
    x_other = swap(x_half, "c")
    dy_other = swap(dy_half, "c")

    hidden = sum_over_z(
        jnp.concatenate([dot_nn(x_half, w_in), dot_nn(x_half, w_in_b)], axis=1)
    )
    grad_act = sum_over_z(
        jnp.concatenate([dot_nt(dy_half, w_out), dot_nt(dy_half, w_out_b)], axis=1)
    )
    act_full, slope = gelu_pair(hidden)
    act = gather_z(act_full.astype(bf16))
    grad_hidden = gather_z((grad_act * slope).astype(bf16))

    out_part = sum_tokens(dot_nn(act[:, :256], w_out) + dot_nn(act[:, 256:], w_out_b))
    in_part = sum_tokens(
        dot_nt(grad_hidden[:, :256], w_in) + dot_nt(grad_hidden[:, 256:], w_in_b)
    )
    parts = jnp.stack([out_part, in_part])
    keep = jnp.where(high, parts[:, 16:], parts[:, :16])
    send = jnp.where(high, parts[:, :16], parts[:, 16:])
    outs = (keep + swap(send, "h")).astype(bf16)

    act_other = swap(act[:, 256:], "c")
    grad_other = swap(grad_hidden[:, 256:], "c")
    grad_w_in = dot_tn(x_half, grad_hidden[:, :256]) + dot_tn(x_other, grad_other)
    grad_w_out = dot_tn(act[:, :256], dy_half) + dot_tn(act_other, dy_other)
    return (outs[0], outs[1], grad_w_in.astype(bf16), grad_w_out.astype(bf16))


def solution(mesh):
    fine = Mesh(mesh.devices.reshape(4, 2, 8, 4, 2), ("y", "c", "z", "x", "h"))
    rows = P(("y", "c", "x", "h"), "z")
    w_in_spec = P("z", ("x", "h", "y", "c"))
    w_out_spec = P(("x", "h", "y", "c"), "z")
    return jax.shard_map(
        shards,
        mesh=fine,
        in_specs=(rows, w_in_spec, w_out_spec, rows),
        out_specs=(rows, rows, w_in_spec, w_out_spec),
        check_vma=False,
    )
```

time: 598 us -> 261 us (0.44)
  the two profiles are of different devices: /device:TPU:1 before, /device:TPU:8 now
where the time goes in v1:
time: 261 us; the launch traced here: 260 us
  waiting for transfers between devices  105 us (40%)
  starting transfers between devices  77 us (30%)
  blocking collectives  51.6 us (20%)
  matrix products  14.7 us (6%)
  other arithmetic  6.44 us (2%)
  local copies, waits for them, and re-layouts  3.9 us (1%)
    all_to_all x6, waiting for transfers between devices, exchange(): return lax.all_to_all(value, axes, 0, 0, tiled=True)  87 us
    all_to_all x2, blocking collectives, exchange(): return lax.all_to_all(value, axes, 0, 0, tiled=True)  51.6 us
    all_to_all x6, starting transfers between devices, exchange(): return lax.all_to_all(value, axes, 0, 0, tiled=True)  40.9 us
    ppermute x8, starting transfers between devices, swap(): return lax.ppermute(value, axis, [(0, 1), (1, 0)])  36.1 us
    ppermute x8, waiting for transfers between devices, swap(): return lax.ppermute(value, axis, [(0, 1), (1, 0)])  18.2 us
    dot_general x4, matrix products, dot_tn(): lax.dot_general(left, right, (((0,), (0,)), ((), ())), preferred_element_...  6.94 us
  transfers between devices with their start and end apart: 14, of which 10 were waited for; matrix products, arithmetic and copies ran while one was open for 7% of the time, Pallas kernels for 0%

profile of v1, /device:TPU:8, one launch (start us, length us, event | category | flops | bytes accessed | tf_op | source)
XLA Modules:
  0.0 259.8 jit_solution(1828969229426438324)
XLA Ops:
  1.4 15.7 %collective-permute-start = (bf16[2,16,1024]{2,1,0:T(8,128)(2,1)S(1)}, bf16[2,16,1024]{2,1,0:T(8,128)(2,1)S(1)}, u32[]{:S(2)}, u32[]{:S(2)}) collective-permute-start(bf16[2,16,1024]{2,1,0:T(8,128)(2,1)S(1)} %pad_maximum_fusion.4), channel_id=1, source_target_pairs={{0,1},{1,0},{2,3},{3,2},{4,5},{5,4},{6,7},{7,6},{8,9},{9,8},{10,11... | collective-permute-start | bytes 196616 | tf_op jit(solution)/shard_map/ppermute | solution.py:35
  17.1 4.2 %collective-permute-done = bf16[2,16,1024]{2,1,0:T(8,128)(2,1)S(1)} collective-permute-done((bf16[2,16,1024]{2,1,0:T(8,128)(2,1)S(1)}, bf16[2,16,1024]{2,1,0:T(8,128)(2,1)S(1)}, u32[]{:S(2)}, u32[]{:S(2)}) %collective-permute-start) | collective-permute-done | bytes 65568 | tf_op jit(solution)/shard_map/ppermute | solution.py:35
  22.3 19.6 %all_to_all.40 = bf16[16,32,1024]{2,1,0:T(8,128)(2,1)S(1)} all-to-all(bf16[16,32,1024]{2,1,0:T(8,128)(2,1)S(1)} %broadcast_in_dim.30), channel_id=1, replica_groups=mesh['y'=4,'c'=2,'z'=8,'x'=4,'h'=2] {'y','x'}, dimensions={0} | all-to-all | bytes 2097152 | tf_op jit(solution)/shard_map/all_to_all | solution.py:39
  43.0 5.7 %all-to-all-start = ((bf16[16,32,1024]{2,1,0:T(8,128)(2,1)}), bf16[16,32,1024]{2,1,0:T(8,128)(2,1)S(1)}, u32[]{:S(2)}, u32[]{:S(2)}) async-start(bf16[16,32,1024]{2,1,0:T(8,128)(2,1)} %broadcast_in_dim.13), calls=%async_computation | async-start | bytes 2097152 | tf_op jit(solution)/shard_map/all_to_all | solution.py:39
  54.1 6.3 %all-to-all-done = bf16[16,32,1024]{2,1,0:T(8,128)(2,1)S(1)} async-done(((bf16[16,32,1024]{2,1,0:T(8,128)(2,1)}), bf16[16,32,1024]{2,1,0:T(8,128)(2,1)S(1)}, u32[]{:S(2)}, u32[]{:S(2)}) %all-to-all-start) | async-done | bytes 1048608 | tf_op jit(solution)/shard_map/all_to_all | solution.py:39
  60.5 13.5 %all-to-all-start.5 = ((bf16[8,64,512]{2,1,0:T(8,128)(2,1)}), bf16[8,64,512]{2,1,0:T(8,128)(2,1)S(1)}, u32[]{:S(2)}, u32[]{:S(2)}) async-start(bf16[8,64,512]{2,1,0:T(8,128)(2,1)} %pad_maximum_fusion.1), calls=%async_computation.5 | async-start | bytes 1048576 | tf_op jit(solution)/shard_map/all_to_all | solution.py:39
  79.8 21.7 %all-to-all-done.5 = bf16[8,64,512]{2,1,0:T(8,128)(2,1)S(1)} async-done(((bf16[8,64,512]{2,1,0:T(8,128)(2,1)}), bf16[8,64,512]{2,1,0:T(8,128)(2,1)S(1)}, u32[]{:S(2)}, u32[]{:S(2)}) %all-to-all-start.5) | async-done | bytes 524320 | tf_op jit(solution)/shard_map/all_to_all | solution.py:39
  101.5 4.3 %all-to-all-start.1 = ((bf16[8,64,512]{2,1,0:T(8,128)(2,1)}), bf16[8,64,512]{2,1,0:T(8,128)(2,1)S(1)}, u32[]{:S(2)}, u32[]{:S(2)}) async-start(bf16[8,64,512]{2,1,0:T(8,128)(2,1)} %pad_maximum_fusion), calls=%async_computation.1 | async-start | bytes 1048576 | tf_op jit(solution)/shard_map/all_to_all | solution.py:39
  105.8 27.9 %all-to-all-done.1 = bf16[8,64,512]{2,1,0:T(8,128)(2,1)S(1)} async-done(((bf16[8,64,512]{2,1,0:T(8,128)(2,1)}), bf16[8,64,512]{2,1,0:T(8,128)(2,1)S(1)}, u32[]{:S(2)}, u32[]{:S(2)}) %all-to-all-start.1) | async-done | bytes 524320 | tf_op jit(solution)/shard_map/all_to_all | solution.py:39
  133.9 32.0 %all_to_all.41 = bf16[8,64,512]{2,1,0:T(8,128)(2,1)S(1)} all-to-all(bf16[8,64,512]{2,1,0:T(8,128)(2,1)S(1)} %broadcast_in_dim.28), channel_id=1, replica_groups=mesh['y'=4,'c'=2,'z'=8,'x'=4,'h'=2] {'z'}, dimensions={0} | all-to-all | bytes 1048576 | tf_op jit(solution)/shard_map/all_to_all | solution.py:39
  166.7 4.3 %all-to-all-start.6 = ((bf16[8,64,512]{2,1,0:T(8,128)(2,1)}), bf16[8,64,512]{2,1,0:T(8,128)(2,1)S(1)}, u32[]{:S(2)}, u32[]{:S(2)}) async-start(bf16[8,64,512]{2,1,0:T(8,128)(2,1)} %broadcast_in_dim.31), calls=%async_computation.6 | async-start | bytes 1048576 | tf_op jit(solution)/shard_map/all_to_all | solution.py:39
  174.0 25.3 %all-to-all-done.6 = bf16[8,64,512]{2,1,0:T(8,128)(2,1)S(1)} async-done(((bf16[8,64,512]{2,1,0:T(8,128)(2,1)}), bf16[8,64,512]{2,1,0:T(8,128)(2,1)S(1)}, u32[]{:S(2)}, u32[]{:S(2)}) %all-to-all-start.6) | async-done | bytes 524320 | tf_op jit(solution)/shard_map/all_to_all | solution.py:39
  199.3 6.5 %all-to-all-start.3 = ((bf16[16,32,1024]{2,1,0:T(8,128)(2,1)}), bf16[16,32,1024]{2,1,0:T(8,128)(2,1)}, u32[]{:S(2)}, u32[]{:S(2)}) async-start(bf16[16,32,1024]{2,1,0:T(8,128)(2,1)} %bitcast.63), calls=%async_computation.3 | async-start | bytes 2097152 | tf_op jit(solution)/shard_map/all_to_all | solution.py:39
  205.8 2.1 collective-permute-start.7
  207.9 2.4 collective-permute-start.4
  213.3 3.5 %all-to-all-done.3 = bf16[16,32,1024]{2,1,0:T(8,128)(2,1)} async-done(((bf16[16,32,1024]{2,1,0:T(8,128)(2,1)}), bf16[16,32,1024]{2,1,0:T(8,128)(2,1)}, u32[]{:S(2)}, u32[]{:S(2)}) %all-to-all-start.3) | async-done | bytes 1048608 | tf_op jit(solution)/shard_map/all_to_all | solution.py:39
  216.8 6.7 %all-to-all-start.7 = ((bf16[16,32,1024]{2,1,0:T(8,128)(2,1)}), bf16[16,32,1024]{2,1,0:T(8,128)(2,1)}, u32[]{:S(2)}, u32[]{:S(2)}) async-start(bf16[16,32,1024]{2,1,0:T(8,128)(2,1)} %bitcast.62), calls=%async_computation.7 | async-start | bytes 2097152 | tf_op jit(solution)/shard_map/all_to_all | solution.py:39
  223.9 1.9 collective-permute-start.6
  225.9 2.4 collective-permute-start.5
  229.8 2.5 fusion.1
  233.8 2.4 all-to-all-done.7
  237.6 7.8 %collective-permute-start.3 = (f32[2,16,1024]{2,1,0:T(8,128)S(1)}, f32[2,16,1024]{2,1,0:T(8,128)S(1)}, u32[]{:S(2)}, u32[]{:S(2)}) collective-permute-start(f32[2,16,1024]{2,1,0:T(8,128)S(1)} %broadcast_select_fusion), channel_id=1, source_target_pairs={{0,1},{1,0},{2,3},{3,2},{4,5},{5,4},{6,7},{7,6},{8,9},{9,8},{10,11... | collective-permute-start | bytes 393224 | tf_op jit(solution)/shard_map/ppermute | solution.py:35
  245.4 2.5 fusion
  247.9 11.2 %collective-permute-done.3 = f32[2,16,1024]{2,1,0:T(8,128)S(1)} collective-permute-done((f32[2,16,1024]{2,1,0:T(8,128)S(1)}, f32[2,16,1024]{2,1,0:T(8,128)S(1)}, u32[]{:S(2)}, u32[]{:S(2)}) %collective-permute-start.3) | collective-permute-done | bytes 131104 | tf_op jit(solution)/shard_map/ppermute | solution.py:35
  (51 shorter events, 26.8 us)
Async XLA Ops:
  1.4 19.9 %collective-permute-start = (bf16[2,16,1024]{2,1,0:T(8,128)(2,1)S(1)}, bf16[2,16,1024]{2,1,0:T(8,128)(2,1)S(1)}, u32[]{:S(2)}, u32[]{:S(2)}) collective-permute-start(bf16[2,16,1024]{2,1,0:T(8,128)(2,1)S(1)} %pad_maximum_fusion.4), channel_id=1, source_target_pairs={{0,1},{1,0},{2,3},{3,2},{4,5},{5,4},{6,7},{7,6},{8,9},{9,8},{10,11... | collective-permute-start | bytes 196616 | tf_op jit(solution)/shard_map/ppermute | solution.py:35
  41.9 6.8 %copy-start.5 = (bf16[256,1024]{1,0:T(8,128)(2,1)S(1)}, bf16[256,1024]{1,0:T(8,128)(2,1)}, u32[]{:S(2)}) copy-start(bf16[256,1024]{1,0:T(8,128)(2,1)} %param.6) | copy-start | bytes 1572868
  43.0 17.5 %all-to-all-start = ((bf16[16,32,1024]{2,1,0:T(8,128)(2,1)}), bf16[16,32,1024]{2,1,0:T(8,128)(2,1)S(1)}, u32[]{:S(2)}, u32[]{:S(2)}) async-start(bf16[16,32,1024]{2,1,0:T(8,128)(2,1)} %broadcast_in_dim.13), calls=%async_computation | async-start | bytes 2097152 | tf_op jit(solution)/shard_map/all_to_all | solution.py:39
  48.7 3.8 %collective-permute-start.2 = (bf16[256,1024]{1,0:T(8,128)(2,1)S(1)}, bf16[256,1024]{1,0:T(8,128)(2,1)S(1)}, u32[]{:S(2)}, u32[]{:S(2)}) collective-permute-start(bf16[256,1024]{1,0:T(8,128)(2,1)S(1)} %copy-done.5), channel_id=1, source_target_pairs={{0,64},{64,0},{1,65},{65,1},{2,66},{66,2},{3,67},{67,3},{4,68},{68... | collective-permute-start | bytes 1572872 | tf_op jit(solution)/shard_map/ppermute | solution.py:35
  51.1 22.8 %copy-start.6 = (bf16[1024,256]{1,0:T(8,128)(2,1)S(1)}, bf16[1024,256]{1,0:T(8,128)(2,1)}, u32[]{:S(2)}) copy-start(bf16[1024,256]{1,0:T(8,128)(2,1)} %param.5) | copy-start | bytes 1572868
  52.5 0.8 copy-start.1
  60.5 41.0 %all-to-all-start.5 = ((bf16[8,64,512]{2,1,0:T(8,128)(2,1)}), bf16[8,64,512]{2,1,0:T(8,128)(2,1)S(1)}, u32[]{:S(2)}, u32[]{:S(2)}) async-start(bf16[8,64,512]{2,1,0:T(8,128)(2,1)} %pad_maximum_fusion.1), calls=%async_computation.5 | async-start | bytes 1048576 | tf_op jit(solution)/shard_map/all_to_all | solution.py:39
  74.0 3.8 %collective-permute-start.1 = (bf16[1024,256]{1,0:T(8,128)(2,1)S(1)}, bf16[1024,256]{1,0:T(8,128)(2,1)S(1)}, u32[]{:S(2)}, u32[]{:S(2)}) collective-permute-start(bf16[1024,256]{1,0:T(8,128)(2,1)S(1)} %copy-done.6), channel_id=1, source_target_pairs={{0,64},{64,0},{1,65},{65,1},{2,66},{66,2},{3,67},{67,3},{4,68},{68... | collective-permute-start | bytes 1572872 | tf_op jit(solution)/shard_map/ppermute | solution.py:35
  77.8 0.8 copy-start.3
  101.5 32.2 %all-to-all-start.1 = ((bf16[8,64,512]{2,1,0:T(8,128)(2,1)}), bf16[8,64,512]{2,1,0:T(8,128)(2,1)S(1)}, u32[]{:S(2)}, u32[]{:S(2)}) async-start(bf16[8,64,512]{2,1,0:T(8,128)(2,1)} %pad_maximum_fusion), calls=%async_computation.1 | async-start | bytes 1048576 | tf_op jit(solution)/shard_map/all_to_all | solution.py:39
  166.7 32.6 %all-to-all-start.6 = ((bf16[8,64,512]{2,1,0:T(8,128)(2,1)}), bf16[8,64,512]{2,1,0:T(8,128)(2,1)S(1)}, u32[]{:S(2)}, u32[]{:S(2)}) async-start(bf16[8,64,512]{2,1,0:T(8,128)(2,1)} %broadcast_in_dim.31), calls=%async_computation.6 | async-start | bytes 1048576 | tf_op jit(solution)/shard_map/all_to_all | solution.py:39
  171.0 1.6 copy-start.2
  199.3 17.5 %all-to-all-start.3 = ((bf16[16,32,1024]{2,1,0:T(8,128)(2,1)}), bf16[16,32,1024]{2,1,0:T(8,128)(2,1)}, u32[]{:S(2)}, u32[]{:S(2)}) async-start(bf16[16,32,1024]{2,1,0:T(8,128)(2,1)} %bitcast.63), calls=%async_computation.3 | async-start | bytes 2097152 | tf_op jit(solution)/shard_map/all_to_all | solution.py:39
  205.8 6.0 %copy-start.4 = (bf16[1024,256]{1,0:T(8,128)(2,1)S(1)}, bf16[1024,256]{1,0:T(8,128)(2,1)}, u32[]{:S(2)}) copy-start(bf16[1024,256]{1,0:T(8,128)(2,1)} %copy-done.3) | copy-start | bytes 1572868
  205.8 24.0 %collective-permute-start.7 = (bf16[512,1024]{1,0:T(8,128)(2,1)S(1)}, bf16[512,1024]{1,0:T(8,128)(2,1)}, u32[]{:S(2)}, u32[]{:S(2)}) collective-permute-start(bf16[512,1024]{1,0:T(8,128)(2,1)S(1)} %bitcast.60), channel_id=1, source_target_pairs={{0,64},{64,0},{1,65},{65,1},{2,66},{66,2},{3,67},{67,3},{4,68},{68... | collective-permute-start | bytes 3145736 | tf_op jit(solution)/shard_map/ppermute | solution.py:35
  207.9 37.5 %collective-permute-start.4 = (bf16[512,1024]{1,0:T(8,128)(2,1)S(1)}, bf16[512,1024]{1,0:T(8,128)(2,1)}, u32[]{:S(2)}, u32[]{:S(2)}) collective-permute-start(bf16[512,1024]{1,0:T(8,128)(2,1)S(1)} %bitcast.56), channel_id=1, source_target_pairs={{0,64},{64,0},{1,65},{65,1},{2,66},{66,2},{3,67},{67,3},{4,68},{68... | collective-permute-start | bytes 3145736 | tf_op jit(solution)/shard_map/ppermute | solution.py:35
  216.8 19.4 %all-to-all-start.7 = ((bf16[16,32,1024]{2,1,0:T(8,128)(2,1)}), bf16[16,32,1024]{2,1,0:T(8,128)(2,1)}, u32[]{:S(2)}, u32[]{:S(2)}) async-start(bf16[16,32,1024]{2,1,0:T(8,128)(2,1)} %bitcast.62), calls=%async_computation.7 | async-start | bytes 2097152 | tf_op jit(solution)/shard_map/all_to_all | solution.py:39
  223.9 5.8 %collective-permute-start.6 = (bf16[512,256]{1,0:T(8,128)(2,1)S(1)}, bf16[512,256]{1,0:T(8,128)(2,1)S(1)}, u32[]{:S(2)}, u32[]{:S(2)}) collective-permute-start(bf16[512,256]{1,0:T(8,128)(2,1)S(1)} %slice.49), channel_id=1, source_target_pairs={{0,64},{64,0},{1,65},{65,1},{2,66},{66,2},{3,67},{67,3},{4,68},{68... | collective-permute-start | bytes 786440 | tf_op jit(solution)/shard_map/ppermute | solution.py:35
  225.9 19.5 %collective-permute-start.5 = (bf16[512,256]{1,0:T(8,128)(2,1)S(1)}, bf16[512,256]{1,0:T(8,128)(2,1)S(1)}, u32[]{:S(2)}, u32[]{:S(2)}) collective-permute-start(bf16[512,256]{1,0:T(8,128)(2,1)S(1)} %slice.51), channel_id=1, source_target_pairs={{0,64},{64,0},{1,65},{65,1},{2,66},{66,2},{3,67},{67,3},{4,68},{68... | collective-permute-start | bytes 786440 | tf_op jit(solution)/shard_map/ppermute | solution.py:35
  232.3 13.2 %copy-start = (f32[1024,256]{1,0:T(8,128)S(1)}, f32[1024,256]{1,0:T(8,128)}, u32[]{:S(2)}) copy-start(f32[1024,256]{1,0:T(8,128)} %fusion.6) | copy-start | bytes 3145732
  237.6 21.5 %collective-permute-start.3 = (f32[2,16,1024]{2,1,0:T(8,128)S(1)}, f32[2,16,1024]{2,1,0:T(8,128)S(1)}, u32[]{:S(2)}, u32[]{:S(2)}) collective-permute-start(f32[2,16,1024]{2,1,0:T(8,128)S(1)} %broadcast_select_fusion), channel_id=1, source_target_pairs={{0,1},{1,0},{2,3},{3,2},{4,5},{5,4},{6,7},{7,6},{8,9},{9,8},{10,11... | collective-permute-start | bytes 393224 | tf_op jit(solution)/shard_map/ppermute | solution.py:35

commit v2 on v1

v2 whole, which is shorter than its diff:
```python
import jax
import jax.numpy as jnp
from jax import lax
from jax.sharding import Mesh, PartitionSpec as P

inv_root_two = 0.7071067811865476
inv_root_tau = 0.3989422804014327
bf16 = jnp.bfloat16
f32 = jnp.float32


def gelu_pair(hidden):
    normal_cdf = 0.5 * (1.0 + lax.erf(hidden * inv_root_two))
    density = jnp.exp(-0.5 * hidden * hidden) * inv_root_tau
    return (hidden * normal_cdf, normal_cdf + hidden * density)


def dot_nn(left, right):
    return jnp.dot(left, right, preferred_element_type=f32)


def dot_nt(left, right):
    return lax.dot_general(
        left, right, (((1,), (1,)), ((), ())), preferred_element_type=f32
    )


def dot_tn(left, right):
    return lax.dot_general(
        left, right, (((0,), (0,)), ((), ())), preferred_element_type=f32
    )


def swap(value, axis):
    return lax.ppermute(value, axis, [(0, 1), (1, 0)])


def flip(value, stride):
    return lax.ppermute(value, "z", [(i, i ^ stride) for i in range(8)])


def exchange(value):
    return lax.all_to_all(value, ("y", "x"), 0, 0, tiled=True)


def gather_rows(own):
    return exchange(jnp.broadcast_to(own[None], (16,) + own.shape))


def scatter_sum(first, second):
    width = first.shape[1]
    parts = jnp.stack(
        [first.astype(bf16).reshape(16, 16, width), second.astype(bf16).reshape(16, 16, width)],
        axis=1,
    )
    return jnp.sum(exchange(parts).astype(f32), axis=0)


def sum_quarter(partial):
    place = lax.axis_index("z")
    for stride in (1, 2):
        bit = (place // stride) % 2
        half = partial.shape[0] // 2
        send = lax.dynamic_slice_in_dim(partial, (1 - bit) * half, half).astype(bf16)
        keep = lax.dynamic_slice_in_dim(partial, bit * half, half)
        partial = keep + flip(send, stride).astype(f32)
    return partial + flip(partial.astype(bf16), 4).astype(f32)


def gather_quarters(value):
    place = lax.axis_index("z")
    for stride in (2, 1):
        upper = (place // stride) % 2 == 1
        other = flip(value, stride)
        value = jnp.concatenate(
            [jnp.where(upper, other, value), jnp.where(upper, value, other)]
        )
    return value


def shards(tokens, w_in, w_out, grad_out):
    n = tokens.shape[1]
    u = w_in.shape[1]
    own = jnp.stack([tokens, grad_out])
    near = gather_rows(own)
    far = gather_rows(swap(own, "h"))
    w_in_b = swap(w_in, "c")
    w_out_b = swap(w_out, "c")

    def front(rows):
        x = rows[:, 0].reshape(256, n)
        dy = rows[:, 1].reshape(256, n)
        partial = jnp.concatenate(
            [dot_nn(x, w_in), dot_nn(x, w_in_b), dot_nt(dy, w_out), dot_nt(dy, w_out_b)],
            axis=1,
        )
        total = sum_quarter(partial)
        act, slope = gelu_pair(total[:, : 2 * u])
        grad_hidden = total[:, 2 * u :] * slope
        return x, dy, jnp.concatenate([act.astype(bf16), grad_hidden.astype(bf16)], axis=1)

    def back(mid):
        out_part = dot_nn(mid[:, :u], w_out) + dot_nn(mid[:, u : 2 * u], w_out_b)
        in_part = dot_nt(mid[:, 2 * u : 3 * u], w_in) + dot_nt(mid[:, 3 * u :], w_in_b)
        return scatter_sum(out_part, in_part)

    x_near, dy_near, mid_near = front(near)
    x_far, dy_far, mid_far = front(far)
    mid_near = gather_quarters(mid_near)
    mid_far = gather_quarters(mid_far)
    far_sum = back(mid_far)
    near_sum = back(mid_near)
    outs = (near_sum + swap(far_sum, "h")).astype(bf16)

    def theirs(mid):
        return swap(jnp.concatenate([mid[:, u : 2 * u], mid[:, 3 * u :]], axis=1), "c")

    near_c, far_c = swap(near, "c"), swap(far, "c")
    x_all = jnp.concatenate(
        [x_near, x_far, near_c[:, 0].reshape(256, n), far_c[:, 0].reshape(256, n)]
    )
    dy_all = jnp.concatenate(
        [dy_near, dy_far, near_c[:, 1].reshape(256, n), far_c[:, 1].reshape(256, n)]
    )
    mids = (theirs(mid_near), theirs(mid_far))
    act_all = jnp.concatenate(
        [mid_near[:, :u], mid_far[:, :u]] + [m[:, :u] for m in mids]
    )
    grad_all = jnp.concatenate(
        [mid_near[:, 2 * u : 3 * u], mid_far[:, 2 * u : 3 * u]] + [m[:, u:] for m in mids]
    )
    grad_w_in = dot_tn(x_all, grad_all).astype(bf16)
    grad_w_out = dot_tn(act_all, dy_all).astype(bf16)
    return (outs[0], outs[1], grad_w_in, grad_w_out)


def solution(mesh):
    fine = Mesh(mesh.devices.reshape(4, 2, 8, 4, 2), ("y", "c", "z", "x", "h"))
    rows = P(("y", "c", "x", "h"), "z")
    w_in_spec = P("z", ("x", "h", "y", "c"))
    w_out_spec = P(("x", "h", "y", "c"), "z")
    return jax.shard_map(
        shards,
        mesh=fine,
        in_specs=(rows, w_in_spec, w_out_spec, rows),
        out_specs=(rows, rows, w_in_spec, w_out_spec),
        check_vma=False,
    )
```

time: 261 us -> 197 us (0.75)
  the two profiles are of different devices: /device:TPU:8 before, /device:TPU:2 now
where the time goes in v2:
time: 197 us; the launch traced here: 196 us
  starting transfers between devices  104 us (53%)
  waiting for transfers between devices  55 us (28%)
  local copies, waits for them, and re-layouts  15.5 us (8%)
  other arithmetic  10.4 us (5%)
  matrix products  9.43 us (5%)
    ppermute x10, starting transfers between devices, flip(): return lax.ppermute(value, 'z', [(i, i ^ stride) for i in range(8)])  36.9 us
    ppermute x8, starting transfers between devices, swap(): return lax.ppermute(value, axis, [(0, 1), (1, 0)])  35 us
    all_to_all x4, starting transfers between devices, exchange(): return lax.all_to_all(value, ('y', 'x'), 0, 0, tiled=True)  32.1 us
    ppermute x10, waiting for transfers between devices, flip(): return lax.ppermute(value, 'z', [(i, i ^ stride) for i in range(8)])  23.7 us
    all_to_all x4, waiting for transfers between devices, exchange(): return lax.all_to_all(value, ('y', 'x'), 0, 0, tiled=True)  17.2 us
    ppermute x8, waiting for transfers between devices, swap(): return lax.ppermute(value, axis, [(0, 1), (1, 0)])  14.1 us
    dot_general x2, matrix products, dot_tn(): lax.dot_general(left, right, (((0,), (0,)), ((), ())), preferred_element_...  4.32 us
  transfers between devices with their start and end apart: 22, of which 9 were waited for; matrix products, arithmetic and copies ran while one was open for 15% of the time, Pallas kernels for 0%

profile of v2, /device:TPU:2, one launch (start us, length us, event | category | flops | bytes accessed | tf_op | source)
XLA Modules:
  0.0 195.8 jit_solution(568313377959084164)
XLA Ops:
  2.5 9.5 %all-to-all-start = ((bf16[16,2,16,1024]{3,2,1,0:T(8,128)(2,1)}), bf16[16,2,16,1024]{3,2,1,0:T(8,128)(2,1)S(1)}, u32[]{:S(2)}, u32[]{:S(2)}) async-start(bf16[16,2,16,1024]{3,2,1,0:T(8,128)(2,1)} %broadcast_in_dim.4), calls=%async_computation | async-start | bytes 2097152 | tf_op jit(solution)/shard_map/all_to_all | solution.py:43
  12.0 13.8 %collective-permute-start.7 = (bf16[2,16,1024]{2,1,0:T(8,128)(2,1)S(1)}, bf16[2,16,1024]{2,1,0:T(8,128)(2,1)S(1)}, u32[]{:S(2)}, u32[]{:S(2)}) collective-permute-start(bf16[2,16,1024]{2,1,0:T(8,128)(2,1)S(1)} %pad_maximum_fusion.12), channel_id=1, source_target_pairs={{0,1},{1,0},{2,3},{3,2},{4,5},{5,4},{6,7},{7,6},{8,9},{9,8},{10,11... | collective-permute-start | bytes 196616 | tf_op jit(solution)/shard_map/ppermute | solution.py:35
  27.8 2.4 %collective-permute-start.1 = (bf16[256,1024]{1,0:T(8,128)(2,1)S(1)}, bf16[256,1024]{1,0:T(8,128)(2,1)S(1)}, u32[]{:S(2)}, u32[]{:S(2)}) collective-permute-start(bf16[256,1024]{1,0:T(8,128)(2,1)S(1)} %copy-done), channel_id=1, source_target_pairs={{0,64},{64,0},{1,65},{65,1},{2,66},{66,2},{3,67},{67,3},{4,68},{68... | collective-permute-start | bytes 1572872 | tf_op jit(solution)/shard_map/ppermute | solution.py:35
  31.6 7.2 %all-to-all-start.2 = ((bf16[16,2,16,1024]{3,2,1,0:T(8,128)(2,1)}), bf16[16,2,16,1024]{3,2,1,0:T(8,128)(2,1)}, u32[]{:S(2)}, u32[]{:S(2)}) async-start(bf16[16,2,16,1024]{3,2,1,0:T(8,128)(2,1)} %broadcast_in_dim.5), calls=%async_computation.2 | async-start | bytes 2097152 | tf_op jit(solution)/shard_map/all_to_all | solution.py:43
  43.4 2.9 %collective-permute-start.2 = (bf16[128,1024]{1,0:T(8,128)(2,1)}, bf16[128,1024]{1,0:T(8,128)(2,1)S(1)}, u32[]{:S(2)}, u32[]{:S(2)}) collective-permute-start(bf16[128,1024]{1,0:T(8,128)(2,1)} %dynamic-slice_convert_fusion.1), channel_id=1, source_target_pairs={{0,8},{8,0},{16,24},{24,16},{32,40},{40,32},{48,56},{56,48},{1,9},... | collective-permute-start | bytes 786440 | tf_op jit(solution)/shard_map/ppermute | solution.py:39
  46.3 8.7 %all-to-all-done.2 = bf16[16,2,16,1024]{3,2,1,0:T(8,128)(2,1)} async-done(((bf16[16,2,16,1024]{3,2,1,0:T(8,128)(2,1)}), bf16[16,2,16,1024]{3,2,1,0:T(8,128)(2,1)}, u32[]{:S(2)}, u32[]{:S(2)}) %all-to-all-start.2) | async-done | bytes 1048608 | tf_op jit(solution)/shard_map/all_to_all | solution.py:43
  57.9 3.1 %collective-permute-start.8 = (bf16[128,1024]{1,0:T(8,128)(2,1)S(1)}, bf16[128,1024]{1,0:T(8,128)(2,1)S(1)}, u32[]{:S(2)}, u32[]{:S(2)}) collective-permute-start(bf16[128,1024]{1,0:T(8,128)(2,1)S(1)} %dynamic-slice_convert_fusion), channel_id=1, source_target_pairs={{0,8},{8,0},{16,24},{24,16},{32,40},{40,32},{48,56},{56,48},{1,9},... | collective-permute-start | bytes 786440 | tf_op jit(solution)/shard_map/ppermute | solution.py:39
  61.1 3.4 %collective-permute-start.3 = (bf16[64,1024]{1,0:T(8,128)(2,1)S(1)}, bf16[64,1024]{1,0:T(8,128)(2,1)S(1)}, u32[]{:S(2)}, u32[]{:S(2)}) collective-permute-start(bf16[64,1024]{1,0:T(8,128)(2,1)S(1)} %dynamic-slice_convert_fusion.3), channel_id=1, source_target_pairs={{0,16},{8,24},{16,0},{24,8},{32,48},{40,56},{48,32},{56,40},{1,17}... | collective-permute-start | bytes 393224 | tf_op jit(solution)/shard_map/ppermute | solution.py:39
  64.5 5.1 %collective-permute-done.8 = bf16[128,1024]{1,0:T(8,128)(2,1)S(1)} collective-permute-done((bf16[128,1024]{1,0:T(8,128)(2,1)S(1)}, bf16[128,1024]{1,0:T(8,128)(2,1)S(1)}, u32[]{:S(2)}, u32[]{:S(2)}) %collective-permute-start.8) | collective-permute-done | bytes 262176 | tf_op jit(solution)/shard_map/ppermute | solution.py:39
  71.7 8.1 %collective-permute-start.4 = (bf16[64,1024]{1,0:T(8,128)(2,1)S(1)}, bf16[64,1024]{1,0:T(8,128)(2,1)S(1)}, u32[]{:S(2)}, u32[]{:S(2)}) collective-permute-start(bf16[64,1024]{1,0:T(8,128)(2,1)S(1)} %fusion.40), channel_id=1, source_target_pairs={{0,32},{8,40},{16,48},{24,56},{32,0},{40,8},{48,16},{56,24},{1,33}... | collective-permute-start | bytes 393224 | tf_op jit(solution)/shard_map/ppermute | solution.py:39
  80.7 6.9 %collective-permute-start.10 = (bf16[64,1024]{1,0:T(8,128)(2,1)S(1)}, bf16[64,1024]{1,0:T(8,128)(2,1)S(1)}, u32[]{:S(2)}, u32[]{:S(2)}) collective-permute-start(bf16[64,1024]{1,0:T(8,128)(2,1)S(1)} %fusion.41), channel_id=1, source_target_pairs={{0,32},{8,40},{16,48},{24,56},{32,0},{40,8},{48,16},{56,24},{1,33}... | collective-permute-start | bytes 393224 | tf_op jit(solution)/shard_map/ppermute | solution.py:39
  87.6 7.8 %collective-permute-done.4 = bf16[64,1024]{1,0:T(8,128)(2,1)S(1)} collective-permute-done((bf16[64,1024]{1,0:T(8,128)(2,1)S(1)}, bf16[64,1024]{1,0:T(8,128)(2,1)S(1)}, u32[]{:S(2)}, u32[]{:S(2)}) %collective-permute-start.4) | collective-permute-done | bytes 131104 | tf_op jit(solution)/shard_map/ppermute | solution.py:39
  99.5 2.9 %collective-permute-start.11 = (bf16[64,1024]{1,0:T(8,128)(2,1)S(1)}, bf16[64,1024]{1,0:T(8,128)(2,1)S(1)}, u32[]{:S(2)}, u32[]{:S(2)}) collective-permute-start(bf16[64,1024]{1,0:T(8,128)(2,1)S(1)} %pad_maximum_fusion.11), channel_id=1, source_target_pairs={{0,16},{8,24},{16,0},{24,8},{32,48},{40,56},{48,32},{56,40},{1,17}... | collective-permute-start | bytes 393224 | tf_op jit(solution)/shard_map/ppermute | solution.py:39
  102.4 5.5 %collective-permute-done.5 = bf16[64,1024]{1,0:T(8,128)(2,1)S(1)} collective-permute-done((bf16[64,1024]{1,0:T(8,128)(2,1)S(1)}, bf16[64,1024]{1,0:T(8,128)(2,1)S(1)}, u32[]{:S(2)}, u32[]{:S(2)}) %collective-permute-start.5) | collective-permute-done | bytes 131104 | tf_op jit(solution)/shard_map/ppermute | solution.py:39
  112.0 3.9 %collective-permute-start.12 = (bf16[128,1024]{1,0:T(8,128)(2,1)}, bf16[128,1024]{1,0:T(8,128)(2,1)}, u32[]{:S(2)}, u32[]{:S(2)}) collective-permute-start(bf16[128,1024]{1,0:T(8,128)(2,1)} %pad_maximum_fusion.5), channel_id=1, source_target_pairs={{0,8},{8,0},{16,24},{24,16},{32,40},{40,32},{48,56},{56,48},{1,9},... | collective-permute-start | bytes 786440 | tf_op jit(solution)/shard_map/ppermute | solution.py:39
  117.9 2.4 %collective-permute-start.15 = (bf16[16,2,16,1024]{3,2,1,0:T(8,128)(2,1)}, bf16[16,2,16,1024]{3,2,1,0:T(8,128)(2,1)}, u32[]{:S(2)}, u32[]{:S(2)}) collective-permute-start(bf16[16,2,16,1024]{3,2,1,0:T(8,128)(2,1)} %all-to-all-done.2), channel_id=1, source_target_pairs={{0,64},{64,0},{1,65},{65,1},{2,66},{66,2},{3,67},{67,3},{4,68},{68... | collective-permute-start | bytes 3145736 | tf_op jit(solution)/shard_map/ppermute | solution.py:35
  120.3 2.6 %collective-permute-done.12 = bf16[128,1024]{1,0:T(8,128)(2,1)} collective-permute-done((bf16[128,1024]{1,0:T(8,128)(2,1)}, bf16[128,1024]{1,0:T(8,128)(2,1)}, u32[]{:S(2)}, u32[]{:S(2)}) %collective-permute-start.12) | collective-permute-done | bytes 262176 | tf_op jit(solution)/shard_map/ppermute | solution.py:39
  128.4 2.4 %collective-permute-start.17 = (bf16[256,512]{1,0:T(8,128)(2,1)}, bf16[256,512]{1,0:T(8,128)(2,1)}, u32[]{:S(2)}, u32[]{:S(2)}) collective-permute-start(bf16[256,512]{1,0:T(8,128)(2,1)} %pad_maximum_fusion.7), channel_id=1, source_target_pairs={{0,64},{64,0},{1,65},{65,1},{2,66},{66,2},{3,67},{67,3},{4,68},{68... | collective-permute-start | bytes 786440 | tf_op jit(solution)/shard_map/ppermute | solution.py:35
  133.2 9.9 %all-to-all-start.3 = ((bf16[16,2,16,1024]{3,2,1,0:T(8,128)(2,1)}), bf16[16,2,16,1024]{3,2,1,0:T(8,128)(2,1)}, u32[]{:S(2)}, u32[]{:S(2)}) async-start(bf16[16,2,16,1024]{3,2,1,0:T(8,128)(2,1)} %pad_maximum_fusion.3), calls=%async_computation.3 | async-start | bytes 2097152 | tf_op jit(solution)/shard_map/all_to_all | solution.py:43
  150.7 8.5 %all-to-all-done.3 = bf16[16,2,16,1024]{3,2,1,0:T(8,128)(2,1)} async-done(((bf16[16,2,16,1024]{3,2,1,0:T(8,128)(2,1)}), bf16[16,2,16,1024]{3,2,1,0:T(8,128)(2,1)}, u32[]{:S(2)}, u32[]{:S(2)}) %all-to-all-start.3) | async-done | bytes 1048608 | tf_op jit(solution)/shard_map/all_to_all | solution.py:43
  159.2 5.5 %all-to-all-start.1 = ((bf16[16,2,16,1024]{3,2,1,0:T(8,128)(2,1)}), bf16[16,2,16,1024]{3,2,1,0:T(8,128)(2,1)S(1)}, u32[]{:S(2)}, u32[]{:S(2)}) async-start(bf16[16,2,16,1024]{3,2,1,0:T(8,128)(2,1)} %pad_maximum_fusion.1), calls=%async_computation.1 | async-start | bytes 2097152 | tf_op jit(solution)/shard_map/all_to_all | solution.py:43
  166.8 2.8 %fusion.16 = bf16[256,1024]{1,0:T(8,128)(2,1)} fusion(bf16[256,1024]{1,0:T(8,128)(2,1)} %bitcast.77, bf16[256,1024]{1,0:T(8,128)(2,1)S(1)} %bitcast.76, bf16[256,1024]{1,0:T(8,128)(2,1)S(1)} %bitcast.69, bf16[256,1024]{1,0:T(8,128)(2,1)S(1)} %bitcast.63, bf16[256,256]{1,0:T(8,128)(2,1)S(1)} %get-tuple-element.26, ...), kind=kOutput, calls=%fused_computation.22 | convolution fusion | flops 547618816 | bytes 3145728 | tf_op jit(solution)/shard_map/dot_general | solution.py:29
  172.6 8.2 %collective-permute-start.13 = (f32[2,16,1024]{2,1,0:T(8,128)S(1)}, f32[2,16,1024]{2,1,0:T(8,128)S(1)}, u32[]{:S(2)}, u32[]{:S(2)}) collective-permute-start(f32[2,16,1024]{2,1,0:T(8,128)S(1)} %convert_reduce_fusion), channel_id=1, source_target_pairs={{0,1},{1,0},{2,3},{3,2},{4,5},{5,4},{6,7},{7,6},{8,9},{9,8},{10,11... | collective-permute-start | bytes 393224 | tf_op jit(solution)/shard_map/ppermute | solution.py:35
  181.0 14.1 %collective-permute-done.13 = f32[2,16,1024]{2,1,0:T(8,128)S(1)} collective-permute-done((f32[2,16,1024]{2,1,0:T(8,128)S(1)}, f32[2,16,1024]{2,1,0:T(8,128)S(1)}, u32[]{:S(2)}, u32[]{:S(2)}) %collective-permute-start.13) | collective-permute-done | bytes 131104 | tf_op jit(solution)/shard_map/ppermute | solution.py:35
  (114 shorter events, 47.0 us)
Async XLA Ops:
  2.5 23.3 %copy-start.1 = (bf16[1024,256]{1,0:T(8,128)(2,1)S(1)}, bf16[1024,256]{1,0:T(8,128)(2,1)}, u32[]{:S(2)}) copy-start(bf16[1024,256]{1,0:T(8,128)(2,1)} %param.5) | copy-start | bytes 1572868
  2.5 25.3 %copy-start = (bf16[256,1024]{1,0:T(8,128)(2,1)S(1)}, bf16[256,1024]{1,0:T(8,128)(2,1)}, u32[]{:S(2)}) copy-start(bf16[256,1024]{1,0:T(8,128)(2,1)} %param.6) | copy-start | bytes 1572868
  2.5 27.8 %all-to-all-start = ((bf16[16,2,16,1024]{3,2,1,0:T(8,128)(2,1)}), bf16[16,2,16,1024]{3,2,1,0:T(8,128)(2,1)S(1)}, u32[]{:S(2)}, u32[]{:S(2)}) async-start(bf16[16,2,16,1024]{3,2,1,0:T(8,128)(2,1)} %broadcast_in_dim.4), calls=%async_computation | async-start | bytes 2097152 | tf_op jit(solution)/shard_map/all_to_all | solution.py:43
  12.0 18.3 %collective-permute-start.7 = (bf16[2,16,1024]{2,1,0:T(8,128)(2,1)S(1)}, bf16[2,16,1024]{2,1,0:T(8,128)(2,1)S(1)}, u32[]{:S(2)}, u32[]{:S(2)}) collective-permute-start(bf16[2,16,1024]{2,1,0:T(8,128)(2,1)S(1)} %pad_maximum_fusion.12), channel_id=1, source_target_pairs={{0,1},{1,0},{2,3},{3,2},{4,5},{5,4},{6,7},{7,6},{8,9},{9,8},{10,11... | collective-permute-start | bytes 196616 | tf_op jit(solution)/shard_map/ppermute | solution.py:35
  25.9 15.0 %collective-permute-start = (bf16[1024,256]{1,0:T(8,128)(2,1)S(1)}, bf16[1024,256]{1,0:T(8,128)(2,1)S(1)}, u32[]{:S(2)}, u32[]{:S(2)}) collective-permute-start(bf16[1024,256]{1,0:T(8,128)(2,1)S(1)} %copy-done.1), channel_id=1, source_target_pairs={{0,64},{64,0},{1,65},{65,1},{2,66},{66,2},{3,67},{67,3},{4,68},{68... | collective-permute-start | bytes 1572872 | tf_op jit(solution)/shard_map/ppermute | solution.py:35
  27.8 13.3 %collective-permute-start.1 = (bf16[256,1024]{1,0:T(8,128)(2,1)S(1)}, bf16[256,1024]{1,0:T(8,128)(2,1)S(1)}, u32[]{:S(2)}, u32[]{:S(2)}) collective-permute-start(bf16[256,1024]{1,0:T(8,128)(2,1)S(1)} %copy-done), channel_id=1, source_target_pairs={{0,64},{64,0},{1,65},{65,1},{2,66},{66,2},{3,67},{67,3},{4,68},{68... | collective-permute-start | bytes 1572872 | tf_op jit(solution)/shard_map/ppermute | solution.py:35
  31.6 23.3 %all-to-all-start.2 = ((bf16[16,2,16,1024]{3,2,1,0:T(8,128)(2,1)}), bf16[16,2,16,1024]{3,2,1,0:T(8,128)(2,1)}, u32[]{:S(2)}, u32[]{:S(2)}) async-start(bf16[16,2,16,1024]{3,2,1,0:T(8,128)(2,1)} %broadcast_in_dim.5), calls=%async_computation.2 | async-start | bytes 2097152 | tf_op jit(solution)/shard_map/all_to_all | solution.py:43
  43.4 17.6 %collective-permute-start.2 = (bf16[128,1024]{1,0:T(8,128)(2,1)}, bf16[128,1024]{1,0:T(8,128)(2,1)S(1)}, u32[]{:S(2)}, u32[]{:S(2)}) collective-permute-start(bf16[128,1024]{1,0:T(8,128)(2,1)} %dynamic-slice_convert_fusion.1), channel_id=1, source_target_pairs={{0,8},{8,0},{16,24},{24,16},{32,40},{40,32},{48,56},{56,48},{1,9},... | collective-permute-start | bytes 786440 | tf_op jit(solution)/shard_map/ppermute | solution.py:39
  57.9 11.6 %collective-permute-start.8 = (bf16[128,1024]{1,0:T(8,128)(2,1)S(1)}, bf16[128,1024]{1,0:T(8,128)(2,1)S(1)}, u32[]{:S(2)}, u32[]{:S(2)}) collective-permute-start(bf16[128,1024]{1,0:T(8,128)(2,1)S(1)} %dynamic-slice_convert_fusion), channel_id=1, source_target_pairs={{0,8},{8,0},{16,24},{24,16},{32,40},{40,32},{48,56},{56,48},{1,9},... | collective-permute-start | bytes 786440 | tf_op jit(solution)/shard_map/ppermute | solution.py:39
  61.1 10.5 %collective-permute-start.3 = (bf16[64,1024]{1,0:T(8,128)(2,1)S(1)}, bf16[64,1024]{1,0:T(8,128)(2,1)S(1)}, u32[]{:S(2)}, u32[]{:S(2)}) collective-permute-start(bf16[64,1024]{1,0:T(8,128)(2,1)S(1)} %dynamic-slice_convert_fusion.3), channel_id=1, source_target_pairs={{0,16},{8,24},{16,0},{24,8},{32,48},{40,56},{48,32},{56,40},{1,17}... | collective-permute-start | bytes 393224 | tf_op jit(solution)/shard_map/ppermute | solution.py:39
  69.7 11.0 %collective-permute-start.9 = (bf16[64,1024]{1,0:T(8,128)(2,1)S(1)}, bf16[64,1024]{1,0:T(8,128)(2,1)S(1)}, u32[]{:S(2)}, u32[]{:S(2)}) collective-permute-start(bf16[64,1024]{1,0:T(8,128)(2,1)S(1)} %dynamic-slice_convert_fusion.2), channel_id=1, source_target_pairs={{0,16},{8,24},{16,0},{24,8},{32,48},{40,56},{48,32},{56,40},{1,17}... | collective-permute-start | bytes 393224 | tf_op jit(solution)/shard_map/ppermute | solution.py:39
  71.7 23.7 %collective-permute-start.4 = (bf16[64,1024]{1,0:T(8,128)(2,1)S(1)}, bf16[64,1024]{1,0:T(8,128)(2,1)S(1)}, u32[]{:S(2)}, u32[]{:S(2)}) collective-permute-start(bf16[64,1024]{1,0:T(8,128)(2,1)S(1)} %fusion.40), channel_id=1, source_target_pairs={{0,32},{8,40},{16,48},{24,56},{32,0},{40,8},{48,16},{56,24},{1,33}... | collective-permute-start | bytes 393224 | tf_op jit(solution)/shard_map/ppermute | solution.py:39
  80.7 18.7 %collective-permute-start.10 = (bf16[64,1024]{1,0:T(8,128)(2,1)S(1)}, bf16[64,1024]{1,0:T(8,128)(2,1)S(1)}, u32[]{:S(2)}, u32[]{:S(2)}) collective-permute-start(bf16[64,1024]{1,0:T(8,128)(2,1)S(1)} %fusion.41), channel_id=1, source_target_pairs={{0,32},{8,40},{16,48},{24,56},{32,0},{40,8},{48,16},{56,24},{1,33}... | collective-permute-start | bytes 393224 | tf_op jit(solution)/shard_map/ppermute | solution.py:39
  95.5 12.4 %collective-permute-start.5 = (bf16[64,1024]{1,0:T(8,128)(2,1)S(1)}, bf16[64,1024]{1,0:T(8,128)(2,1)S(1)}, u32[]{:S(2)}, u32[]{:S(2)}) collective-permute-start(bf16[64,1024]{1,0:T(8,128)(2,1)S(1)} %pad_maximum_fusion.10), channel_id=1, source_target_pairs={{0,16},{8,24},{16,0},{24,8},{32,48},{40,56},{48,32},{56,40},{1,17}... | collective-permute-start | bytes 393224 | tf_op jit(solution)/shard_map/ppermute | solution.py:39
  99.5 11.1 %collective-permute-start.11 = (bf16[64,1024]{1,0:T(8,128)(2,1)S(1)}, bf16[64,1024]{1,0:T(8,128)(2,1)S(1)}, u32[]{:S(2)}, u32[]{:S(2)}) collective-permute-start(bf16[64,1024]{1,0:T(8,128)(2,1)S(1)} %pad_maximum_fusion.11), channel_id=1, source_target_pairs={{0,16},{8,24},{16,0},{24,8},{32,48},{40,56},{48,32},{56,40},{1,17}... | collective-permute-start | bytes 393224 | tf_op jit(solution)/shard_map/ppermute | solution.py:39
  108.7 11.6 %collective-permute-start.6 = (bf16[128,1024]{1,0:T(8,128)(2,1)}, bf16[128,1024]{1,0:T(8,128)(2,1)}, u32[]{:S(2)}, u32[]{:S(2)}) collective-permute-start(bf16[128,1024]{1,0:T(8,128)(2,1)} %pad_maximum_fusion.4), channel_id=1, source_target_pairs={{0,8},{8,0},{16,24},{24,16},{32,40},{40,32},{48,56},{56,48},{1,9},... | collective-permute-start | bytes 786440 | tf_op jit(solution)/shard_map/ppermute | solution.py:39
  112.0 10.8 %collective-permute-start.12 = (bf16[128,1024]{1,0:T(8,128)(2,1)}, bf16[128,1024]{1,0:T(8,128)(2,1)}, u32[]{:S(2)}, u32[]{:S(2)}) collective-permute-start(bf16[128,1024]{1,0:T(8,128)(2,1)} %pad_maximum_fusion.5), channel_id=1, source_target_pairs={{0,8},{8,0},{16,24},{24,16},{32,40},{40,32},{48,56},{56,48},{1,9},... | collective-permute-start | bytes 786440 | tf_op jit(solution)/shard_map/ppermute | solution.py:39
  115.9 30.1 %collective-permute-start.14 = (bf16[16,2,16,1024]{3,2,1,0:T(8,128)(2,1)}, bf16[16,2,16,1024]{3,2,1,0:T(8,128)(2,1)}, u32[]{:S(2)}, u32[]{:S(2)}) collective-permute-start(bf16[16,2,16,1024]{3,2,1,0:T(8,128)(2,1)} %copy-done.6), channel_id=1, source_target_pairs={{0,64},{64,0},{1,65},{65,1},{2,66},{66,2},{3,67},{67,3},{4,68},{68... | collective-permute-start | bytes 3145736 | tf_op jit(solution)/shard_map/ppermute | solution.py:35
  117.9 30.5 %collective-permute-start.15 = (bf16[16,2,16,1024]{3,2,1,0:T(8,128)(2,1)}, bf16[16,2,16,1024]{3,2,1,0:T(8,128)(2,1)}, u32[]{:S(2)}, u32[]{:S(2)}) collective-permute-start(bf16[16,2,16,1024]{3,2,1,0:T(8,128)(2,1)} %all-to-all-done.2), channel_id=1, source_target_pairs={{0,64},{64,0},{1,65},{65,1},{2,66},{66,2},{3,67},{67,3},{4,68},{68... | collective-permute-start | bytes 3145736 | tf_op jit(solution)/shard_map/ppermute | solution.py:35
  125.6 39.1 %collective-permute-start.16 = (bf16[256,512]{1,0:T(8,128)(2,1)}, bf16[256,512]{1,0:T(8,128)(2,1)}, u32[]{:S(2)}, u32[]{:S(2)}) collective-permute-start(bf16[256,512]{1,0:T(8,128)(2,1)} %pad_maximum_fusion.6), channel_id=1, source_target_pairs={{0,64},{64,0},{1,65},{65,1},{2,66},{66,2},{3,67},{67,3},{4,68},{68... | collective-permute-start | bytes 786440 | tf_op jit(solution)/shard_map/ppermute | solution.py:35
  128.4 37.4 %collective-permute-start.17 = (bf16[256,512]{1,0:T(8,128)(2,1)}, bf16[256,512]{1,0:T(8,128)(2,1)}, u32[]{:S(2)}, u32[]{:S(2)}) collective-permute-start(bf16[256,512]{1,0:T(8,128)(2,1)} %pad_maximum_fusion.7), channel_id=1, source_target_pairs={{0,64},{64,0},{1,65},{65,1},{2,66},{66,2},{3,67},{67,3},{4,68},{68... | collective-permute-start | bytes 786440 | tf_op jit(solution)/shard_map/ppermute | solution.py:35
  133.2 26.0 %all-to-all-start.3 = ((bf16[16,2,16,1024]{3,2,1,0:T(8,128)(2,1)}), bf16[16,2,16,1024]{3,2,1,0:T(8,128)(2,1)}, u32[]{:S(2)}, u32[]{:S(2)}) async-start(bf16[16,2,16,1024]{3,2,1,0:T(8,128)(2,1)} %pad_maximum_fusion.3), calls=%async_computation.3 | async-start | bytes 2097152 | tf_op jit(solution)/shard_map/all_to_all | solution.py:43
  159.2 21.7 %all-to-all-start.1 = ((bf16[16,2,16,1024]{3,2,1,0:T(8,128)(2,1)}), bf16[16,2,16,1024]{3,2,1,0:T(8,128)(2,1)S(1)}, u32[]{:S(2)}, u32[]{:S(2)}) async-start(bf16[16,2,16,1024]{3,2,1,0:T(8,128)(2,1)} %pad_maximum_fusion.1), calls=%async_computation.1 | async-start | bytes 2097152 | tf_op jit(solution)/shard_map/all_to_all | solution.py:43
  172.6 22.5 %collective-permute-start.13 = (f32[2,16,1024]{2,1,0:T(8,128)S(1)}, f32[2,16,1024]{2,1,0:T(8,128)S(1)}, u32[]{:S(2)}, u32[]{:S(2)}) collective-permute-start(f32[2,16,1024]{2,1,0:T(8,128)S(1)} %convert_reduce_fusion), channel_id=1, source_target_pairs={{0,1},{1,0},{2,3},{3,2},{4,5},{5,4},{6,7},{7,6},{8,9},{9,8},{10,11... | collective-permute-start | bytes 393224 | tf_op jit(solution)/shard_map/ppermute | solution.py:35
  (16 other events, 39.7 us)

commit v3 on v1

v3 whole, which is shorter than its diff:
```python
import jax
import jax.numpy as jnp
from jax import lax
from jax.experimental import pallas as pl
from jax.experimental.pallas import tpu as pltpu
from jax.sharding import Mesh, PartitionSpec as P

inv_root_two = 0.7071067811865476
inv_root_tau = 0.3989422804014327
bf16 = jnp.bfloat16
f32 = jnp.float32


def gelu_pair(hidden):
    normal_cdf = 0.5 * (1.0 + lax.erf(hidden * inv_root_two))
    density = jnp.exp(-0.5 * hidden * hidden) * inv_root_tau
    return (hidden * normal_cdf, normal_cdf + hidden * density)


def dot_nn(left, right):
    return jnp.dot(left, right, preferred_element_type=f32)


def dot_nt(left, right):
    return lax.dot_general(
        left, right, (((1,), (1,)), ((), ())), preferred_element_type=f32
    )


def dot_tn(left, right):
    return lax.dot_general(
        left, right, (((0,), (0,)), ((), ())), preferred_element_type=f32
    )


def swap(value, axis):
    return lax.ppermute(value, axis, [(0, 1), (1, 0)])


def exchange(value, axes=("y", "x")):
    return lax.all_to_all(value, axes, 0, 0, tiled=True)


def gather_rows(own):
    return exchange(jnp.broadcast_to(own[None], (16,) + own.shape))


def after(value, *others):
    return lax.optimization_barrier((value,) + others)[0]


def cross(value):
    return value + swap(value.astype(bf16), "zq").astype(f32)


def gather_four(value):
    copies = jnp.broadcast_to(value[None], (4,) + value.shape)
    return exchange(copies, ("zr",)).reshape(256, value.shape[1])


def halve(partial, stride, axis):
    bit = (lax.axis_index("zr") // stride) % 2
    send = lax.dynamic_index_in_dim(partial, 1 - bit, axis, keepdims=False)
    kept = lax.dynamic_index_in_dim(partial, bit, axis, keepdims=False)
    other = lax.ppermute(send.astype(bf16), "zr", [(i, i ^ stride) for i in range(4)])
    return kept + other.astype(f32)


def double(value, stride, axis):
    upper = (lax.axis_index("zr") // stride) % 2 == 1
    other = lax.ppermute(value, "zr", [(i, i ^ stride) for i in range(4)])
    return jnp.stack(
        [jnp.where(upper, other, value), jnp.where(upper, value, other)], axis=axis
    )


def front_kernel(rows, in_a, in_b, out_a, out_b, result):
    n, u = in_a.shape
    x = rows[:, 0].reshape(256, n)
    dy = rows[:, 1].reshape(256, n)
    for c, (w, v) in enumerate(((in_a, out_a), (in_b, out_b))):
        result[:, 2 * c * u : (2 * c + 1) * u] = dot_nn(x, w[...]).astype(result.dtype)
        result[:, (2 * c + 1) * u : (2 * c + 2) * u] = dot_nt(dy, v[...]).astype(
            result.dtype
        )


def back_kernel(mid, in_a, in_b, out_a, out_b, result):
    n, u = in_a.shape
    out_part = dot_nn(mid[:, :u], out_a[...]) + dot_nn(mid[:, 2 * u : 3 * u], out_b[...])
    result[:, 0] = out_part.astype(bf16).reshape(16, 16, n)
    in_part = dot_nt(mid[:, u : 2 * u], in_a[...]) + dot_nt(mid[:, 3 * u :], in_b[...])
    result[:, 1] = in_part.astype(bf16).reshape(16, 16, n)


def run(kernel, left, weights, shape, dtype):
    n, u = weights[0].shape
    result = jax.ShapeDtypeStruct(shape, dtype)
    return pl.pallas_call(
        kernel,
        out_shape=result,
        in_specs=[pl.BlockSpec(memory_space=pltpu.VMEM)] * 5,
        out_specs=pl.BlockSpec(memory_space=pltpu.VMEM),
        compiler_params=pltpu.CompilerParams(vmem_limit_bytes=32 * 1024 * 1024),
        cost_estimate=pl.CostEstimate(
            flops=2048 * n * u,
            bytes_accessed=2 * left.size + 8 * n * u + result.size * result.dtype.itemsize,
            transcendentals=0,
        ),
    )(left, *weights)


def both(*values):
    return lax.optimization_barrier(values)


def shards(tokens, w_in, w_out, grad_out):
    n = tokens.shape[1]
    u = w_in.shape[1]
    own = jnp.stack([tokens, grad_out])
    near = gather_rows(own)
    other_rows = swap(own, "h")
    weights = (w_in, swap(w_in, "c"), w_out, swap(w_out, "c"))

    def middle(total):
        parts = []
        for i in (0, 2 * u):
            act, slope = gelu_pair(total[:, i : i + u])
            grad_hidden = total[:, i + u : i + 2 * u] * slope
            parts += [act.astype(bf16), grad_hidden.astype(bf16)]
        return jnp.concatenate(parts, axis=1)

    def last(mid):
        return run(back_kernel, mid, weights, (16, 2, 16, n), bf16)

    def total_of(parts):
        return jnp.sum(exchange(parts).astype(f32), axis=0)

    far = gather_rows(after(other_rows, near))
    near_1 = run(front_kernel, near, weights, (256, 4 * u), f32)
    near_4 = halve(halve(near_1.reshape(2, 2, 64, 4 * u), 1, 1), 2, 0)
    far_1 = run(front_kernel, far, weights, (256, 4 * u), bf16)
    near_c = swap(near, "c")
    near_4, far_1 = both(near_4, far_1)
    far_4 = jnp.sum(
        exchange(far_1.reshape(4, 64, 4 * u), ("zr",)).astype(f32), axis=0
    )
    far_c = swap(far, "c")
    near_8, far_4, near_c = both(cross(near_4), far_4, near_c)
    far_8, mid_near, far_c = both(cross(far_4), double(middle(near_8), 2, 0), far_c)
    mid_far, mid_near = both(gather_four(middle(far_8)), double(mid_near, 1, 1))
    mid_near = mid_near.reshape(256, 4 * u)
    parts_far = last(mid_far)
    far_sum = total_of(parts_far)
    parts_near = last(mid_near)

    x_all = jnp.concatenate([r[:, 0].reshape(256, n) for r in (near, far, near_c, far_c)])
    dy_all = jnp.concatenate([r[:, 1].reshape(256, n) for r in (near, far, near_c, far_c)])
    far_sum, parts_near, mid_near, mid_far, x_all, dy_all = both(
        far_sum, parts_near, mid_near, mid_far, x_all, dy_all
    )
    mids = jnp.concatenate([mid_near, mid_far])
    theirs = swap(mids[:, 2 * u :], "c")
    act_all = jnp.concatenate([mids[:, :u], theirs[:, :u]])
    grad_all = jnp.concatenate([mids[:, u : 2 * u], theirs[:, u:]])
    grad_w_in = dot_tn(x_all, grad_all).astype(bf16)
    grad_w_out = dot_tn(act_all, dy_all).astype(bf16)
    near_sum = total_of(parts_near)
    outs = (near_sum + swap(far_sum, "h")).astype(bf16)
    return (outs[0], outs[1], grad_w_in, grad_w_out)


def solution(mesh):
    fine = Mesh(mesh.devices.reshape(4, 2, 2, 4, 4, 2), ("y", "c", "zq", "zr", "x", "h"))
    rows = P(("y", "c", "x", "h"), ("zq", "zr"))
    w_in_spec = P(("zq", "zr"), ("x", "h", "y", "c"))
    w_out_spec = P(("x", "h", "y", "c"), ("zq", "zr"))
    return jax.shard_map(
        shards,
        mesh=fine,
        in_specs=(rows, w_in_spec, w_out_spec, rows),
        out_specs=(rows, rows, w_in_spec, w_out_spec),
        check_vma=False,
    )
```

time: 261 us -> 196 us (0.75)
  the two profiles are of different devices: /device:TPU:8 before, /device:TPU:1 now
where the time goes in v3:
time: 196 us; the launch traced here: 195 us
  starting transfers between devices  105 us (54%)
  waiting for transfers between devices  47.9 us (24%)
  local copies, waits for them, and re-layouts  19.4 us (10%)
  other arithmetic  13.2 us (7%)
  Pallas kernels  4.89 us (2%)
  matrix products  3.08 us (2%)
    ppermute x9, starting transfers between devices, swap(): return lax.ppermute(value, axis, [(0, 1), (1, 0)])  49.7 us
    all_to_all x6, starting transfers between devices, exchange(): return lax.all_to_all(value, axes, 0, 0, tiled=True)  42 us
    all_to_all x6, waiting for transfers between devices, exchange(): return lax.all_to_all(value, axes, 0, 0, tiled=True)  20.3 us
    ppermute x2, waiting for transfers between devices, double(): other = lax.ppermute(value, 'zr', [(i, i ^ stride) for i in range(4)])  10.7 us
    ppermute x9, waiting for transfers between devices, swap(): return lax.ppermute(value, axis, [(0, 1), (1, 0)])  9.44 us
    ppermute x2, starting transfers between devices, double(): other = lax.ppermute(value, 'zr', [(i, i ^ stride) for i in range(4)])  7.76 us
    ppermute x2, waiting for transfers between devices, halve(): lax.ppermute(send.astype(bf16), 'zr', [(i, i ^ stride) for i in range(4)])  7.4 us
    unnamed x39, local copies, waits for them, and re-layouts  6.89 us
  transfers between devices with their start and end apart: 19, of which 7 were waited for; matrix products, arithmetic and copies ran while one was open for 11% of the time, Pallas kernels for 1%

profile of v3, /device:TPU:1, one launch (start us, length us, event | category | flops | bytes accessed | tf_op | source)
XLA Modules:
  0.0 194.8 jit_solution(3683351807888725764)
XLA Ops:
  2.7 7.6 %all-to-all-start = ((bf16[16,2,16,1024]{3,2,1,0:T(8,128)(2,1)}), bf16[16,2,16,1024]{3,2,1,0:T(8,128)(2,1)S(1)}, u32[]{:S(2)}, u32[]{:S(2)}) async-start(bf16[16,2,16,1024]{3,2,1,0:T(8,128)(2,1)} %broadcast_in_dim.6), calls=%async_computation | async-start | bytes 2097152 | tf_op jit(solution)/shard_map/all_to_all | solution.py:41
  10.3 4.9 %collective-permute-start = (bf16[1024,256]{1,0:T(8,128)(2,1)S(1)}, bf16[1024,256]{1,0:T(8,128)(2,1)S(1)}, u32[]{:S(2)}, u32[]{:S(2)}) collective-permute-start(bf16[1024,256]{1,0:T(8,128)(2,1)S(1)} %copy-done), channel_id=1, source_target_pairs={{0,64},{64,0},{1,65},{65,1},{2,66},{66,2},{3,67},{67,3},{4,68},{68... | collective-permute-start | bytes 1572872 | tf_op jit(solution)/shard_map/ppermute | solution.py:37
  17.1 13.5 %collective-permute-start.4 = (bf16[2,16,1024]{2,1,0:T(8,128)(2,1)S(1)}, bf16[2,16,1024]{2,1,0:T(8,128)(2,1)S(1)}, u32[]{:S(2)}, u32[]{:S(2)}) collective-permute-start(bf16[2,16,1024]{2,1,0:T(8,128)(2,1)S(1)} %pad_maximum_fusion.6), channel_id=1, source_target_pairs={{0,1},{1,0},{2,3},{3,2},{4,5},{5,4},{6,7},{7,6},{8,9},{9,8},{10,11... | collective-permute-start | bytes 196616 | tf_op jit(solution)/shard_map/ppermute | solution.py:37
  33.3 2.6 %collective-permute-start.2 = (bf16[2,64,1024]{2,1,0:T(8,128)(2,1)}, bf16[2,64,1024]{2,1,0:T(8,128)(2,1)S(1)}, u32[]{:S(2)}, u32[]{:S(2)}) collective-permute-start(bf16[2,64,1024]{2,1,0:T(8,128)(2,1)} %fusion.6), channel_id=1, source_target_pairs={{0,8},{8,0},{16,24},{24,16},{1,9},{9,1},{17,25},{25,17},{2,10},{10... | collective-permute-start | bytes 786440 | tf_op jit(solution)/shard_map/ppermute | solution.py:65
  37.1 6.9 %all-to-all-start.1 = ((bf16[16,2,16,1024]{3,2,1,0:T(8,128)(2,1)}), bf16[16,2,16,1024]{3,2,1,0:T(8,128)(2,1)S(1)}, u32[]{:S(2)}, u32[]{:S(2)}) async-start(bf16[16,2,16,1024]{3,2,1,0:T(8,128)(2,1)} %broadcast_in_dim.7), calls=%async_computation.1 | async-start | bytes 2097152 | tf_op jit(solution)/shard_map/all_to_all | solution.py:41
  46.0 3.1 %collective-permute-start.3 = (bf16[64,1024]{1,0:T(8,128)(2,1)S(1)}, bf16[64,1024]{1,0:T(8,128)(2,1)S(1)}, u32[]{:S(2)}, u32[]{:S(2)}) collective-permute-start(bf16[64,1024]{1,0:T(8,128)(2,1)S(1)} %fusion.7), channel_id=1, source_target_pairs={{0,16},{8,24},{16,0},{24,8},{1,17},{9,25},{17,1},{25,9},{2,18},{10... | collective-permute-start | bytes 393224 | tf_op jit(solution)/shard_map/ppermute | solution.py:65
  49.1 7.4 %collective-permute-done.3 = bf16[64,1024]{1,0:T(8,128)(2,1)S(1)} collective-permute-done((bf16[64,1024]{1,0:T(8,128)(2,1)S(1)}, bf16[64,1024]{1,0:T(8,128)(2,1)S(1)}, u32[]{:S(2)}, u32[]{:S(2)}) %collective-permute-start.3) | collective-permute-done | bytes 131104 | tf_op jit(solution)/shard_map/ppermute | solution.py:65
  63.2 4.1 %all-to-all-start.2 = ((bf16[4,64,1024]{2,1,0:T(8,128)(2,1)}), bf16[4,64,1024]{2,1,0:T(8,128)(2,1)}, u32[]{:S(2)}, u32[]{:S(2)}) async-start(bf16[4,64,1024]{2,1,0:T(8,128)(2,1)} %bitcast.46), calls=%async_computation.2 | async-start | bytes 1048576 | tf_op jit(solution)/shard_map/all_to_all | solution.py:41
  67.3 4.8 %collective-permute-start.6 = (bf16[16,2,16,1024]{3,2,1,0:T(8,128)(2,1)S(1)}, bf16[16,2,16,1024]{3,2,1,0:T(8,128)(2,1)}, u32[]{:S(2)}, u32[]{:S(2)}) collective-permute-start(bf16[16,2,16,1024]{3,2,1,0:T(8,128)(2,1)S(1)} %all-to-all-done.rows), channel_id=1, source_target_pairs={{0,64},{64,0},{1,65},{65,1},{2,66},{66,2},{3,67},{67,3},{4,68},{68... | collective-permute-start | bytes 3145736 | tf_op jit(solution)/shard_map/ppermute | solution.py:37
  72.2 6.3 %collective-permute-start.5 = (bf16[64,1024]{1,0:T(8,128)(2,1)S(1)}, bf16[64,1024]{1,0:T(8,128)(2,1)S(1)}, u32[]{:S(2)}, u32[]{:S(2)}) collective-permute-start(bf16[64,1024]{1,0:T(8,128)(2,1)S(1)} %convert_element_type.78), channel_id=1, source_target_pairs={{0,32},{32,0},{1,33},{33,1},{2,34},{34,2},{3,35},{35,3},{4,36},{36... | collective-permute-start | bytes 393224 | tf_op jit(solution)/shard_map/ppermute | solution.py:37
  78.5 2.2 %collective-permute-start.9 = (bf16[16,2,16,1024]{3,2,1,0:T(8,128)(2,1)S(1)}, bf16[16,2,16,1024]{3,2,1,0:T(8,128)(2,1)}, u32[]{:S(2)}, u32[]{:S(2)}) collective-permute-start(bf16[16,2,16,1024]{3,2,1,0:T(8,128)(2,1)S(1)} %all-to-all-done.1.rows), channel_id=1, source_target_pairs={{0,64},{64,0},{1,65},{65,1},{2,66},{66,2},{3,67},{67,3},{4,68},{68... | collective-permute-start | bytes 3145736 | tf_op jit(solution)/shard_map/ppermute | solution.py:37
  80.8 7.9 %collective-permute-done.5 = bf16[64,1024]{1,0:T(8,128)(2,1)S(1)} collective-permute-done((bf16[64,1024]{1,0:T(8,128)(2,1)S(1)}, bf16[64,1024]{1,0:T(8,128)(2,1)S(1)}, u32[]{:S(2)}, u32[]{:S(2)}) %collective-permute-start.5) | collective-permute-done | bytes 131104 | tf_op jit(solution)/shard_map/ppermute | solution.py:37
  92.3 4.3 %collective-permute-start.8 = (bf16[64,1024]{1,0:T(8,128)(2,1)}, bf16[64,1024]{1,0:T(8,128)(2,1)}, u32[]{:S(2)}, u32[]{:S(2)}) collective-permute-start(bf16[64,1024]{1,0:T(8,128)(2,1)} %pad_maximum_fusion.4), channel_id=1, source_target_pairs={{0,16},{8,24},{16,0},{24,8},{1,17},{9,25},{17,1},{25,9},{2,18},{10... | collective-permute-start | bytes 393224 | tf_op jit(solution)/shard_map/ppermute | solution.py:71
  96.6 6.9 %collective-permute-start.7 = (bf16[64,1024]{1,0:T(8,128)(2,1)S(1)}, bf16[64,1024]{1,0:T(8,128)(2,1)S(1)}, u32[]{:S(2)}, u32[]{:S(2)}) collective-permute-start(bf16[64,1024]{1,0:T(8,128)(2,1)S(1)} %convert_element_type.81), channel_id=1, source_target_pairs={{0,32},{32,0},{1,33},{33,1},{2,34},{34,2},{3,35},{35,3},{4,36},{36... | collective-permute-start | bytes 393224 | tf_op jit(solution)/shard_map/ppermute | solution.py:37
  107.8 11.6 %all-to-all-start.3 = ((bf16[4,64,1024]{2,1,0:T(8,128)(2,1)}), bf16[4,64,1024]{2,1,0:T(8,128)(2,1)}, u32[]{:S(2)}, u32[]{:S(2)}) async-start(bf16[4,64,1024]{2,1,0:T(8,128)(2,1)} %broadcast_in_dim.8), calls=%async_computation.3 | async-start | bytes 1048576 | tf_op jit(solution)/shard_map/all_to_all | solution.py:41
  119.3 3.4 %collective-permute-start.10 = (bf16[2,64,1024]{2,1,0:T(8,128)(2,1)S(1)}, bf16[2,64,1024]{2,1,0:T(8,128)(2,1)S(1)}, u32[]{:S(2)}, u32[]{:S(2)}) collective-permute-start(bf16[2,64,1024]{2,1,0:T(8,128)(2,1)S(1)} %copy-done.18), channel_id=1, source_target_pairs={{0,8},{8,0},{16,24},{24,16},{1,9},{9,1},{17,25},{25,17},{2,10},{10... | collective-permute-start | bytes 786440 | tf_op jit(solution)/shard_map/ppermute | solution.py:71
  123.9 10.7 %collective-permute-done.10 = bf16[2,64,1024]{2,1,0:T(8,128)(2,1)S(1)} collective-permute-done((bf16[2,64,1024]{2,1,0:T(8,128)(2,1)S(1)}, bf16[2,64,1024]{2,1,0:T(8,128)(2,1)S(1)}, u32[]{:S(2)}, u32[]{:S(2)}) %collective-permute-start.10) | collective-permute-done | bytes 262176 | tf_op jit(solution)/shard_map/ppermute | solution.py:71
  138.2 8.1 %all-to-all-start.4 = ((bf16[16,2,16,1024]{3,2,1,0:T(8,128)(2,1)}), bf16[16,2,16,1024]{3,2,1,0:T(8,128)(2,1)}, u32[]{:S(2)}, u32[]{:S(2)}) async-start(bf16[16,2,16,1024]{3,2,1,0:T(8,128)(2,1)} %copy-done.9), calls=%async_computation.4 | async-start | bytes 2097152 | tf_op jit(solution)/shard_map/all_to_all | solution.py:41
  149.2 2.3 %pad_maximum_fusion = (bf16[1024,1024]{1,0:T(8,128)(2,1)}, bf16[1024,1024]{1,0:T(8,128)(2,1)}) fusion(bf16[256,1024]{1,0:T(8,128)(2,1)S(1)} %bitcast.54, bf16[256,1024]{1,0:T(8,128)(2,1)S(1)} %bitcast.52, bf16[256,1024]{1,0:T(8,128)(2,1)S(1)} %bitcast.50, bf16[256,1024]{1,0:T(8,128)(2,1)S(1)} %bitcast.48, bf16[256,1024]{1,0:T(8,128)(2,1)S(1)} %bitcast.53, ...), kind=kLoop, calls=%fused_computation | loop fusion | flops 16777216 | bytes 8388608 | tf_op jit(solution)/shard_map/concatenate | solution.py:157
  153.2 8.5 %all-to-all-done.4 = bf16[16,2,16,1024]{3,2,1,0:T(8,128)(2,1)} async-done(((bf16[16,2,16,1024]{3,2,1,0:T(8,128)(2,1)}), bf16[16,2,16,1024]{3,2,1,0:T(8,128)(2,1)}, u32[]{:S(2)}, u32[]{:S(2)}) %all-to-all-start.4) | async-done | bytes 1048608 | tf_op jit(solution)/shard_map/all_to_all | solution.py:41
  166.0 5.1 %collective-permute-start.12 = (bf16[512,512]{1,0:T(8,128)(2,1)}, bf16[512,512]{1,0:T(8,128)(2,1)}, u32[]{:S(2)}, u32[]{:S(2)}) collective-permute-start(bf16[512,512]{1,0:T(8,128)(2,1)} %slice.99), channel_id=1, source_target_pairs={{0,64},{64,0},{1,65},{65,1},{2,66},{66,2},{3,67},{67,3},{4,68},{68... | collective-permute-start | bytes 1572872 | tf_op jit(solution)/shard_map/ppermute | solution.py:37
  171.1 3.7 %all-to-all-start.5 = ((bf16[16,2,16,1024]{3,2,1,0:T(8,128)(2,1)}), bf16[16,2,16,1024]{3,2,1,0:T(8,128)(2,1)S(1)}, u32[]{:S(2)}, u32[]{:S(2)}) async-start(bf16[16,2,16,1024]{3,2,1,0:T(8,128)(2,1)} %shard_map.78), calls=%async_computation.5 | async-start | bytes 2097152 | tf_op jit(solution)/shard_map/all_to_all | solution.py:41
  174.8 4.0 %collective-permute-start.11 = (f32[2,16,1024]{2,1,0:T(8,128)S(1)}, f32[2,16,1024]{2,1,0:T(8,128)S(1)}, u32[]{:S(2)}, u32[]{:S(2)}) collective-permute-start(f32[2,16,1024]{2,1,0:T(8,128)S(1)} %convert_reduce_fusion.1), channel_id=1, source_target_pairs={{0,1},{1,0},{2,3},{3,2},{4,5},{5,4},{6,7},{7,6},{8,9},{9,8},{10,11... | collective-permute-start | bytes 393224 | tf_op jit(solution)/shard_map/ppermute | solution.py:37
  184.3 9.7 %all-to-all-done.5 = bf16[16,2,16,1024]{3,2,1,0:T(8,128)(2,1)S(1)} async-done(((bf16[16,2,16,1024]{3,2,1,0:T(8,128)(2,1)}), bf16[16,2,16,1024]{3,2,1,0:T(8,128)(2,1)S(1)}, u32[]{:S(2)}, u32[]{:S(2)}) %all-to-all-start.5) | async-done | bytes 1048608 | tf_op jit(solution)/shard_map/all_to_all | solution.py:41
  (93 shorter events, 43.8 us)
Async XLA Ops:
  0.6 14.5 %copy-start.1 = (bf16[256,1024]{1,0:T(8,128)(2,1)S(1)}, bf16[256,1024]{1,0:T(8,128)(2,1)}, u32[]{:S(2)}) copy-start(bf16[256,1024]{1,0:T(8,128)(2,1)} %out_a.7) | copy-start | bytes 1572868
  2.7 27.9 %all-to-all-start = ((bf16[16,2,16,1024]{3,2,1,0:T(8,128)(2,1)}), bf16[16,2,16,1024]{3,2,1,0:T(8,128)(2,1)S(1)}, u32[]{:S(2)}, u32[]{:S(2)}) async-start(bf16[16,2,16,1024]{3,2,1,0:T(8,128)(2,1)} %broadcast_in_dim.6), calls=%async_computation | async-start | bytes 2097152 | tf_op jit(solution)/shard_map/all_to_all | solution.py:41
  10.3 20.3 %collective-permute-start = (bf16[1024,256]{1,0:T(8,128)(2,1)S(1)}, bf16[1024,256]{1,0:T(8,128)(2,1)S(1)}, u32[]{:S(2)}, u32[]{:S(2)}) collective-permute-start(bf16[1024,256]{1,0:T(8,128)(2,1)S(1)} %copy-done), channel_id=1, source_target_pairs={{0,64},{64,0},{1,65},{65,1},{2,66},{66,2},{3,67},{67,3},{4,68},{68... | collective-permute-start | bytes 1572872 | tf_op jit(solution)/shard_map/ppermute | solution.py:37
  15.1 15.4 %collective-permute-start.1 = (bf16[256,1024]{1,0:T(8,128)(2,1)S(1)}, bf16[256,1024]{1,0:T(8,128)(2,1)S(1)}, u32[]{:S(2)}, u32[]{:S(2)}) collective-permute-start(bf16[256,1024]{1,0:T(8,128)(2,1)S(1)} %copy-done.1), channel_id=1, source_target_pairs={{0,64},{64,0},{1,65},{65,1},{2,66},{66,2},{3,67},{67,3},{4,68},{68... | collective-permute-start | bytes 1572872 | tf_op jit(solution)/shard_map/ppermute | solution.py:37
  17.1 18.9 %collective-permute-start.4 = (bf16[2,16,1024]{2,1,0:T(8,128)(2,1)S(1)}, bf16[2,16,1024]{2,1,0:T(8,128)(2,1)S(1)}, u32[]{:S(2)}, u32[]{:S(2)}) collective-permute-start(bf16[2,16,1024]{2,1,0:T(8,128)(2,1)S(1)} %pad_maximum_fusion.6), channel_id=1, source_target_pairs={{0,1},{1,0},{2,3},{3,2},{4,5},{5,4},{6,7},{7,6},{8,9},{9,8},{10,11... | collective-permute-start | bytes 196616 | tf_op jit(solution)/shard_map/ppermute | solution.py:37
  33.3 10.8 %collective-permute-start.2 = (bf16[2,64,1024]{2,1,0:T(8,128)(2,1)}, bf16[2,64,1024]{2,1,0:T(8,128)(2,1)S(1)}, u32[]{:S(2)}, u32[]{:S(2)}) collective-permute-start(bf16[2,64,1024]{2,1,0:T(8,128)(2,1)} %fusion.6), channel_id=1, source_target_pairs={{0,8},{8,0},{16,24},{24,16},{1,9},{9,1},{17,25},{25,17},{2,10},{10... | collective-permute-start | bytes 786440 | tf_op jit(solution)/shard_map/ppermute | solution.py:65
  37.1 22.5 %all-to-all-start.1 = ((bf16[16,2,16,1024]{3,2,1,0:T(8,128)(2,1)}), bf16[16,2,16,1024]{3,2,1,0:T(8,128)(2,1)S(1)}, u32[]{:S(2)}, u32[]{:S(2)}) async-start(bf16[16,2,16,1024]{3,2,1,0:T(8,128)(2,1)} %broadcast_in_dim.7), calls=%async_computation.1 | async-start | bytes 2097152 | tf_op jit(solution)/shard_map/all_to_all | solution.py:41
  46.0 10.5 %collective-permute-start.3 = (bf16[64,1024]{1,0:T(8,128)(2,1)S(1)}, bf16[64,1024]{1,0:T(8,128)(2,1)S(1)}, u32[]{:S(2)}, u32[]{:S(2)}) collective-permute-start(bf16[64,1024]{1,0:T(8,128)(2,1)S(1)} %fusion.7), channel_id=1, source_target_pairs={{0,16},{8,24},{16,0},{24,8},{1,17},{9,25},{17,1},{25,9},{2,18},{10... | collective-permute-start | bytes 393224 | tf_op jit(solution)/shard_map/ppermute | solution.py:65
  63.2 26.2 %all-to-all-start.2 = ((bf16[4,64,1024]{2,1,0:T(8,128)(2,1)}), bf16[4,64,1024]{2,1,0:T(8,128)(2,1)}, u32[]{:S(2)}, u32[]{:S(2)}) async-start(bf16[4,64,1024]{2,1,0:T(8,128)(2,1)} %bitcast.46), calls=%async_computation.2 | async-start | bytes 1048576 | tf_op jit(solution)/shard_map/all_to_all | solution.py:41
  67.3 23.2 %collective-permute-start.6 = (bf16[16,2,16,1024]{3,2,1,0:T(8,128)(2,1)S(1)}, bf16[16,2,16,1024]{3,2,1,0:T(8,128)(2,1)}, u32[]{:S(2)}, u32[]{:S(2)}) collective-permute-start(bf16[16,2,16,1024]{3,2,1,0:T(8,128)(2,1)S(1)} %all-to-all-done.rows), channel_id=1, source_target_pairs={{0,64},{64,0},{1,65},{65,1},{2,66},{66,2},{3,67},{67,3},{4,68},{68... | collective-permute-start | bytes 3145736 | tf_op jit(solution)/shard_map/ppermute | solution.py:37
  72.2 16.5 %collective-permute-start.5 = (bf16[64,1024]{1,0:T(8,128)(2,1)S(1)}, bf16[64,1024]{1,0:T(8,128)(2,1)S(1)}, u32[]{:S(2)}, u32[]{:S(2)}) collective-permute-start(bf16[64,1024]{1,0:T(8,128)(2,1)S(1)} %convert_element_type.78), channel_id=1, source_target_pairs={{0,32},{32,0},{1,33},{33,1},{2,34},{34,2},{3,35},{35,3},{4,36},{36... | collective-permute-start | bytes 393224 | tf_op jit(solution)/shard_map/ppermute | solution.py:37
  78.5 28.3 %collective-permute-start.9 = (bf16[16,2,16,1024]{3,2,1,0:T(8,128)(2,1)S(1)}, bf16[16,2,16,1024]{3,2,1,0:T(8,128)(2,1)}, u32[]{:S(2)}, u32[]{:S(2)}) collective-permute-start(bf16[16,2,16,1024]{3,2,1,0:T(8,128)(2,1)S(1)} %all-to-all-done.1.rows), channel_id=1, source_target_pairs={{0,64},{64,0},{1,65},{65,1},{2,66},{66,2},{3,67},{67,3},{4,68},{68... | collective-permute-start | bytes 3145736 | tf_op jit(solution)/shard_map/ppermute | solution.py:37
  92.3 11.3 %collective-permute-start.8 = (bf16[64,1024]{1,0:T(8,128)(2,1)}, bf16[64,1024]{1,0:T(8,128)(2,1)}, u32[]{:S(2)}, u32[]{:S(2)}) collective-permute-start(bf16[64,1024]{1,0:T(8,128)(2,1)} %pad_maximum_fusion.4), channel_id=1, source_target_pairs={{0,16},{8,24},{16,0},{24,8},{1,17},{9,25},{17,1},{25,9},{2,18},{10... | collective-permute-start | bytes 393224 | tf_op jit(solution)/shard_map/ppermute | solution.py:71
  96.6 10.1 %collective-permute-start.7 = (bf16[64,1024]{1,0:T(8,128)(2,1)S(1)}, bf16[64,1024]{1,0:T(8,128)(2,1)S(1)}, u32[]{:S(2)}, u32[]{:S(2)}) collective-permute-start(bf16[64,1024]{1,0:T(8,128)(2,1)S(1)} %convert_element_type.81), channel_id=1, source_target_pairs={{0,32},{32,0},{1,33},{33,1},{2,34},{34,2},{3,35},{35,3},{4,36},{36... | collective-permute-start | bytes 393224 | tf_op jit(solution)/shard_map/ppermute | solution.py:37
  106.8 12.5 %copy-start.18 = (bf16[2,64,1024]{2,1,0:T(8,128)(2,1)S(1)}, bf16[2,64,1024]{2,1,0:T(8,128)(2,1)}, u32[]{:S(2)}) copy-start(bf16[2,64,1024]{2,1,0:T(8,128)(2,1)} %pad_maximum_fusion.3) | copy-start | bytes 786436
  107.8 27.7 %all-to-all-start.3 = ((bf16[4,64,1024]{2,1,0:T(8,128)(2,1)}), bf16[4,64,1024]{2,1,0:T(8,128)(2,1)}, u32[]{:S(2)}, u32[]{:S(2)}) async-start(bf16[4,64,1024]{2,1,0:T(8,128)(2,1)} %broadcast_in_dim.8), calls=%async_computation.3 | async-start | bytes 1048576 | tf_op jit(solution)/shard_map/all_to_all | solution.py:41
  119.3 15.3 %collective-permute-start.10 = (bf16[2,64,1024]{2,1,0:T(8,128)(2,1)S(1)}, bf16[2,64,1024]{2,1,0:T(8,128)(2,1)S(1)}, u32[]{:S(2)}, u32[]{:S(2)}) collective-permute-start(bf16[2,64,1024]{2,1,0:T(8,128)(2,1)S(1)} %copy-done.18), channel_id=1, source_target_pairs={{0,8},{8,0},{16,24},{24,16},{1,9},{9,1},{17,25},{25,17},{2,10},{10... | collective-permute-start | bytes 786440 | tf_op jit(solution)/shard_map/ppermute | solution.py:71
  123.9 11.6 %copy-start.4 = (bf16[1024,256]{1,0:T(8,128)(2,1)S(1)}, bf16[1024,256]{1,0:T(8,128)(2,1)}, u32[]{:S(2)}) copy-start(bf16[1024,256]{1,0:T(8,128)(2,1)} %copy-done.2) | copy-start | bytes 1572868
  123.9 11.6 %copy-start.7 = (bf16[256,1024]{1,0:T(8,128)(2,1)S(1)}, bf16[256,1024]{1,0:T(8,128)(2,1)}, u32[]{:S(2)}) copy-start(bf16[256,1024]{1,0:T(8,128)(2,1)} %copy-done.5) | copy-start | bytes 1572868
  138.2 23.5 %all-to-all-start.4 = ((bf16[16,2,16,1024]{3,2,1,0:T(8,128)(2,1)}), bf16[16,2,16,1024]{3,2,1,0:T(8,128)(2,1)}, u32[]{:S(2)}, u32[]{:S(2)}) async-start(bf16[16,2,16,1024]{3,2,1,0:T(8,128)(2,1)} %copy-done.9), calls=%async_computation.4 | async-start | bytes 2097152 | tf_op jit(solution)/shard_map/all_to_all | solution.py:41
  166.0 15.1 %copy-start.12 = (bf16[1024,1024]{1,0:T(8,128)(2,1)S(1)}, bf16[1024,1024]{1,0:T(8,128)(2,1)}, u32[]{:S(2)}) copy-start(bf16[1024,1024]{1,0:T(8,128)(2,1)} %get-tuple-element.37) | copy-start | bytes 6291460
  166.0 13.9 %collective-permute-start.12 = (bf16[512,512]{1,0:T(8,128)(2,1)}, bf16[512,512]{1,0:T(8,128)(2,1)}, u32[]{:S(2)}, u32[]{:S(2)}) collective-permute-start(bf16[512,512]{1,0:T(8,128)(2,1)} %slice.99), channel_id=1, source_target_pairs={{0,64},{64,0},{1,65},{65,1},{2,66},{66,2},{3,67},{67,3},{4,68},{68... | collective-permute-start | bytes 1572872 | tf_op jit(solution)/shard_map/ppermute | solution.py:37
  171.1 22.8 %all-to-all-start.5 = ((bf16[16,2,16,1024]{3,2,1,0:T(8,128)(2,1)}), bf16[16,2,16,1024]{3,2,1,0:T(8,128)(2,1)S(1)}, u32[]{:S(2)}, u32[]{:S(2)}) async-start(bf16[16,2,16,1024]{3,2,1,0:T(8,128)(2,1)} %shard_map.78), calls=%async_computation.5 | async-start | bytes 2097152 | tf_op jit(solution)/shard_map/all_to_all | solution.py:41
  174.8 19.3 %collective-permute-start.11 = (f32[2,16,1024]{2,1,0:T(8,128)S(1)}, f32[2,16,1024]{2,1,0:T(8,128)S(1)}, u32[]{:S(2)}, u32[]{:S(2)}) collective-permute-start(f32[2,16,1024]{2,1,0:T(8,128)S(1)} %convert_reduce_fusion.1), channel_id=1, source_target_pairs={{0,1},{1,0},{2,3},{3,2},{4,5},{5,4},{6,7},{7,6},{8,9},{9,8},{10,11... | collective-permute-start | bytes 393224 | tf_op jit(solution)/shard_map/ppermute | solution.py:37
  (14 other events, 28.5 us)

commit v4 on v3

--- a/solution.py
+++ b/solution.py
@@ -139,16 +139,16 @@
     far = gather_rows(after(other_rows, near))
     near_1 = run(front_kernel, near, weights, (256, 4 * u), f32)
     near_4 = halve(halve(near_1.reshape(2, 2, 64, 4 * u), 1, 1), 2, 0)
+    near_4, far = both(near_4, far)
     far_1 = run(front_kernel, far, weights, (256, 4 * u), bf16)
     near_c = swap(near, "c")
-    near_4, far_1 = both(near_4, far_1)
     far_4 = jnp.sum(
         exchange(far_1.reshape(4, 64, 4 * u), ("zr",)).astype(f32), axis=0
     )
     far_c = swap(far, "c")
-    near_8, far_4, near_c = both(cross(near_4), far_4, near_c)
-    far_8, mid_near, far_c = both(cross(far_4), double(middle(near_8), 2, 0), far_c)
-    mid_far, mid_near = both(gather_four(middle(far_8)), double(mid_near, 1, 1))
+    mid_near, far_4, near_c = both(double(middle(cross(near_4)), 2, 0), far_4, near_c)
+    far_8, mid_near, far_c = both(cross(far_4), double(mid_near, 1, 1), far_c)
+    mid_far = gather_four(middle(far_8))
     mid_near = mid_near.reshape(256, 4 * u)
     parts_far = last(mid_far)
     far_sum = total_of(parts_far)
@@ -156,17 +156,18 @@
 
     x_all = jnp.concatenate([r[:, 0].reshape(256, n) for r in (near, far, near_c, far_c)])
     dy_all = jnp.concatenate([r[:, 1].reshape(256, n) for r in (near, far, near_c, far_c)])
-    far_sum, parts_near, mid_near, mid_far, x_all, dy_all = both(
-        far_sum, parts_near, mid_near, mid_far, x_all, dy_all
-    )
-    mids = jnp.concatenate([mid_near, mid_far])
-    theirs = swap(mids[:, 2 * u :], "c")
+    theirs_near = swap(mid_near[:, 2 * u :], "c")
+    late_far, x_all, dy_all = both(mid_far, x_all, dy_all)
+    theirs_far = swap(late_far[:, 2 * u :], "c")
+    mids = jnp.concatenate([mid_near[:, : 2 * u], mid_far[:, : 2 * u]])
+    theirs = jnp.concatenate([theirs_near, theirs_far])
+    far_sum, parts_near, mids, theirs = both(far_sum, parts_near, mids, theirs)
     act_all = jnp.concatenate([mids[:, :u], theirs[:, :u]])
     grad_all = jnp.concatenate([mids[:, u : 2 * u], theirs[:, u:]])
     grad_w_in = dot_tn(x_all, grad_all).astype(bf16)
     grad_w_out = dot_tn(act_all, dy_all).astype(bf16)
     near_sum = total_of(parts_near)
-    outs = (near_sum + swap(far_sum, "h")).astype(bf16)
+    outs = (near_sum + swap(far_sum.astype(bf16), "h").astype(f32)).astype(bf16)
     return (outs[0], outs[1], grad_w_in, grad_w_out)
 
 

time: 196 us -> 188 us (0.959)
  waiting for transfers between devices: 47.9 us -> 29.6 us
  starting transfers between devices: 105 us -> 111 us
  local copies, waits for them, and re-layouts: 19.4 us -> 21.7 us
    ppermute x2, waiting for transfers between devices: 10.7 us -> 0.01 us  [double(): other = lax.ppermute(value, 'zr', [(i, i ^ stride) for i in range(4)])]
    all_to_all x6, waiting for transfers between devices: 20.3 us -> 10.5 us  [exchange(): return lax.all_to_all(value, axes, 0, 0, tiled=True)]
    ppermute x2, starting transfers between devices: 7.76 us -> 16.2 us  [double(): other = lax.ppermute(value, 'zr', [(i, i ^ stride) for i in range(4)])]
    all_to_all x6, starting transfers between devices: 42 us -> 34 us  [exchange(): return lax.all_to_all(value, axes, 0, 0, tiled=True)]
    ppermute x9 -> x10, starting transfers between devices: 49.7 us -> 55.4 us  [swap(): return lax.ppermute(value, axis, [(0, 1), (1, 0)])]
    concatenate x0 -> x2, other arithmetic: none -> 2.61 us  [the longest x1 1.78 us: shards(): theirs = jnp.concatenate([theirs_near, theirs_far])]
    ppermute x9 -> x10, waiting for transfers between devices: 9.44 us -> 11.6 us  [swap(): return lax.ppermute(value, axis, [(0, 1), (1, 0)])]
    slice x4, local copies, waits for them, and re-layouts: 3.86 us -> 6 us  [shards(): r[:, 1].reshape(256, n)]
  transfers between devices with their start and end apart: 19 -> 20, of which waited for: 7 -> 6; matrix products, arithmetic and copies ran while one was open for 11% -> 15% of each run, Pallas kernels for 1% -> 2%
where the time goes in v4:
time: 188 us; the launch traced here: 187 us
  starting transfers between devices  111 us (59%)
  waiting for transfers between devices  29.6 us (16%)
  local copies, waits for them, and re-layouts  21.7 us (12%)
  other arithmetic  15.1 us (8%)
  Pallas kernels  4.88 us (3%)
  matrix products  3.07 us (2%)
    ppermute x10, starting transfers between devices, swap(): return lax.ppermute(value, axis, [(0, 1), (1, 0)])  55.4 us
    all_to_all x6, starting transfers between devices, exchange(): return lax.all_to_all(value, axes, 0, 0, tiled=True)  34 us
    ppermute x2, starting transfers between devices, double(): other = lax.ppermute(value, 'zr', [(i, i ^ stride) for i in range(4)])  16.2 us
    ppermute x10, waiting for transfers between devices, swap(): return lax.ppermute(value, axis, [(0, 1), (1, 0)])  11.6 us
    all_to_all x6, waiting for transfers between devices, exchange(): return lax.all_to_all(value, axes, 0, 0, tiled=True)  10.5 us
    ppermute x2, waiting for transfers between devices, halve(): lax.ppermute(send.astype(bf16), 'zr', [(i, i ^ stride) for i in range(4)])  7.4 us
    unnamed x40, local copies, waits for them, and re-layouts  6.24 us
    slice x4, local copies, waits for them, and re-layouts, shards(): r[:, 1].reshape(256, n)  6 us
  transfers between devices with their start and end apart: 20, of which 6 were waited for; matrix products, arithmetic and copies ran while one was open for 15% of the time, Pallas kernels for 2%

profile of v4, /device:TPU:1, one launch (start us, length us, event | category | flops | bytes accessed | tf_op | source)
XLA Modules:
  0.0 186.8 jit_solution(6713310934312640301)
XLA Ops:
  2.6 7.6 %all-to-all-start = ((bf16[16,2,16,1024]{3,2,1,0:T(8,128)(2,1)}), bf16[16,2,16,1024]{3,2,1,0:T(8,128)(2,1)S(1)}, u32[]{:S(2)}, u32[]{:S(2)}) async-start(bf16[16,2,16,1024]{3,2,1,0:T(8,128)(2,1)} %broadcast_in_dim.6), calls=%async_computation | async-start | bytes 2097152 | tf_op jit(solution)/shard_map/all_to_all | solution.py:41
  10.2 4.9 %collective-permute-start = (bf16[1024,256]{1,0:T(8,128)(2,1)S(1)}, bf16[1024,256]{1,0:T(8,128)(2,1)S(1)}, u32[]{:S(2)}, u32[]{:S(2)}) collective-permute-start(bf16[1024,256]{1,0:T(8,128)(2,1)S(1)} %copy-done), channel_id=1, source_target_pairs={{0,64},{64,0},{1,65},{65,1},{2,66},{66,2},{3,67},{67,3},{4,68},{68... | collective-permute-start | bytes 1572872 | tf_op jit(solution)/shard_map/ppermute | solution.py:37
  17.0 13.5 %collective-permute-start.4 = (bf16[2,16,1024]{2,1,0:T(8,128)(2,1)S(1)}, bf16[2,16,1024]{2,1,0:T(8,128)(2,1)S(1)}, u32[]{:S(2)}, u32[]{:S(2)}) collective-permute-start(bf16[2,16,1024]{2,1,0:T(8,128)(2,1)S(1)} %pad_maximum_fusion.8), channel_id=1, source_target_pairs={{0,1},{1,0},{2,3},{3,2},{4,5},{5,4},{6,7},{7,6},{8,9},{9,8},{10,11... | collective-permute-start | bytes 196616 | tf_op jit(solution)/shard_map/ppermute | solution.py:37
  33.2 2.6 %collective-permute-start.2 = (bf16[2,64,1024]{2,1,0:T(8,128)(2,1)}, bf16[2,64,1024]{2,1,0:T(8,128)(2,1)S(1)}, u32[]{:S(2)}, u32[]{:S(2)}) collective-permute-start(bf16[2,64,1024]{2,1,0:T(8,128)(2,1)} %fusion.6), channel_id=1, source_target_pairs={{0,8},{8,0},{16,24},{24,16},{1,9},{9,1},{17,25},{25,17},{2,10},{10... | collective-permute-start | bytes 786440 | tf_op jit(solution)/shard_map/ppermute | solution.py:65
  37.0 6.9 %all-to-all-start.1 = ((bf16[16,2,16,1024]{3,2,1,0:T(8,128)(2,1)}), bf16[16,2,16,1024]{3,2,1,0:T(8,128)(2,1)S(1)}, u32[]{:S(2)}, u32[]{:S(2)}) async-start(bf16[16,2,16,1024]{3,2,1,0:T(8,128)(2,1)} %broadcast_in_dim.7), calls=%async_computation.1 | async-start | bytes 2097152 | tf_op jit(solution)/shard_map/all_to_all | solution.py:41
  45.9 3.1 %collective-permute-start.3 = (bf16[64,1024]{1,0:T(8,128)(2,1)S(1)}, bf16[64,1024]{1,0:T(8,128)(2,1)S(1)}, u32[]{:S(2)}, u32[]{:S(2)}) collective-permute-start(bf16[64,1024]{1,0:T(8,128)(2,1)S(1)} %fusion.7), channel_id=1, source_target_pairs={{0,16},{8,24},{16,0},{24,8},{1,17},{9,25},{17,1},{25,9},{2,18},{10... | collective-permute-start | bytes 393224 | tf_op jit(solution)/shard_map/ppermute | solution.py:65
  49.0 7.4 %collective-permute-done.3 = bf16[64,1024]{1,0:T(8,128)(2,1)S(1)} collective-permute-done((bf16[64,1024]{1,0:T(8,128)(2,1)S(1)}, bf16[64,1024]{1,0:T(8,128)(2,1)S(1)}, u32[]{:S(2)}, u32[]{:S(2)}) %collective-permute-start.3) | collective-permute-done | bytes 131104 | tf_op jit(solution)/shard_map/ppermute | solution.py:65
  57.4 2.1 %all-to-all-done.1.rows = bf16[16,2,16,1024]{3,2,1,0:T(8,128)(2,1)S(1)} async-done(((bf16[16,2,16,1024]{3,2,1,0:T(8,128)(2,1)}), bf16[16,2,16,1024]{3,2,1,0:T(8,128)(2,1)S(1)}, u32[]{:S(2)}, u32[]{:S(2)}) %all-to-all-start.1) | async-done | bytes 1048608 | tf_op jit(solution)/shard_map/all_to_all | solution.py:41
  63.2 4.2 %all-to-all-start.2 = ((bf16[4,64,1024]{2,1,0:T(8,128)(2,1)}), bf16[4,64,1024]{2,1,0:T(8,128)(2,1)}, u32[]{:S(2)}, u32[]{:S(2)}) async-start(bf16[4,64,1024]{2,1,0:T(8,128)(2,1)} %bitcast.46), calls=%async_computation.2 | async-start | bytes 1048576 | tf_op jit(solution)/shard_map/all_to_all | solution.py:41
  67.3 6.4 %collective-permute-start.5 = (bf16[64,1024]{1,0:T(8,128)(2,1)S(1)}, bf16[64,1024]{1,0:T(8,128)(2,1)S(1)}, u32[]{:S(2)}, u32[]{:S(2)}) collective-permute-start(bf16[64,1024]{1,0:T(8,128)(2,1)S(1)} %convert_element_type.84), channel_id=1, source_target_pairs={{0,32},{32,0},{1,33},{33,1},{2,34},{34,2},{3,35},{35,3},{4,36},{36... | collective-permute-start | bytes 393224 | tf_op jit(solution)/shard_map/ppermute | solution.py:37
  73.7 5.1 %collective-permute-start.7 = (bf16[16,2,16,1024]{3,2,1,0:T(8,128)(2,1)S(1)}, bf16[16,2,16,1024]{3,2,1,0:T(8,128)(2,1)}, u32[]{:S(2)}, u32[]{:S(2)}) collective-permute-start(bf16[16,2,16,1024]{3,2,1,0:T(8,128)(2,1)S(1)} %all-to-all-done.rows), channel_id=1, source_target_pairs={{0,64},{64,0},{1,65},{65,1},{2,66},{66,2},{3,67},{67,3},{4,68},{68... | collective-permute-start | bytes 3145736 | tf_op jit(solution)/shard_map/ppermute | solution.py:37
  79.0 14.2 %collective-permute-start.6 = (bf16[64,1024]{1,0:T(8,128)(2,1)S(1)}, bf16[64,1024]{1,0:T(8,128)(2,1)S(1)}, u32[]{:S(2)}, u32[]{:S(2)}) collective-permute-start(bf16[64,1024]{1,0:T(8,128)(2,1)S(1)} %pad_maximum_fusion.6), channel_id=1, source_target_pairs={{0,16},{8,24},{16,0},{24,8},{1,17},{9,25},{17,1},{25,9},{2,18},{10... | collective-permute-start | bytes 393224 | tf_op jit(solution)/shard_map/ppermute | solution.py:71
  93.2 4.5 %collective-permute-start.10 = (bf16[16,2,16,1024]{3,2,1,0:T(8,128)(2,1)S(1)}, bf16[16,2,16,1024]{3,2,1,0:T(8,128)(2,1)}, u32[]{:S(2)}, u32[]{:S(2)}) collective-permute-start(bf16[16,2,16,1024]{3,2,1,0:T(8,128)(2,1)S(1)} %all-to-all-done.1.rows), channel_id=1, source_target_pairs={{0,64},{64,0},{1,65},{65,1},{2,66},{66,2},{3,67},{67,3},{4,68},{68... | collective-permute-start | bytes 3145736 | tf_op jit(solution)/shard_map/ppermute | solution.py:37
  100.4 2.7 %collective-permute-start.8 = (bf16[64,1024]{1,0:T(8,128)(2,1)}, bf16[64,1024]{1,0:T(8,128)(2,1)S(1)}, u32[]{:S(2)}, u32[]{:S(2)}) collective-permute-start(bf16[64,1024]{1,0:T(8,128)(2,1)} %convert_element_type.91), channel_id=1, source_target_pairs={{0,32},{32,0},{1,33},{33,1},{2,34},{34,2},{3,35},{35,3},{4,36},{36... | collective-permute-start | bytes 393224 | tf_op jit(solution)/shard_map/ppermute | solution.py:37
  105.0 11.6 %collective-permute-done.8 = bf16[64,1024]{1,0:T(8,128)(2,1)S(1)} collective-permute-done((bf16[64,1024]{1,0:T(8,128)(2,1)}, bf16[64,1024]{1,0:T(8,128)(2,1)S(1)}, u32[]{:S(2)}, u32[]{:S(2)}) %collective-permute-start.8) | collective-permute-done | bytes 131104 | tf_op jit(solution)/shard_map/ppermute | solution.py:37
  119.5 4.9 %all-to-all-start.3 = ((bf16[4,64,1024]{2,1,0:T(8,128)(2,1)}), bf16[4,64,1024]{2,1,0:T(8,128)(2,1)}, u32[]{:S(2)}, u32[]{:S(2)}) async-start(bf16[4,64,1024]{2,1,0:T(8,128)(2,1)} %broadcast_in_dim.8), calls=%async_computation.3 | async-start | bytes 1048576 | tf_op jit(solution)/shard_map/all_to_all | solution.py:41
  126.6 2.4 %fusion.36 = (bf16[16,1,16,1024]{3,2,1,0:T(8,128)(2,1)}, bf16[16,1,16,1024]{3,2,1,0:T(8,128)(2,1)}) fusion(bf16[16,2,16,1024]{3,2,1,0:T(8,128)(2,1)} %collective-permute-done.7), kind=kLoop, calls=%fused_computation.75 | loop fusion | bytes 2097152 | tf_op jit(solution)/shard_map/slice | solution.py:158
  129.7 3.9 %collective-permute-start.11 = (bf16[256,512]{1,0:T(8,128)(2,1)}, bf16[256,512]{1,0:T(8,128)(2,1)}, u32[]{:S(2)}, u32[]{:S(2)}) collective-permute-start(bf16[256,512]{1,0:T(8,128)(2,1)} %get-tuple-element.48), channel_id=1, source_target_pairs={{0,64},{64,0},{1,65},{65,1},{2,66},{66,2},{3,67},{67,3},{4,68},{68... | collective-permute-start | bytes 786440 | tf_op jit(solution)/shard_map/ppermute | solution.py:37
  133.6 5.9 %all-to-all-done.3 = bf16[4,64,1024]{2,1,0:T(8,128)(2,1)} async-done(((bf16[4,64,1024]{2,1,0:T(8,128)(2,1)}), bf16[4,64,1024]{2,1,0:T(8,128)(2,1)}, u32[]{:S(2)}, u32[]{:S(2)}) %all-to-all-start.3) | async-done | bytes 524320 | tf_op jit(solution)/shard_map/all_to_all | solution.py:41
  142.2 4.6 %all-to-all-start.4 = ((bf16[16,2,16,1024]{3,2,1,0:T(8,128)(2,1)}), bf16[16,2,16,1024]{3,2,1,0:T(8,128)(2,1)}, u32[]{:S(2)}, u32[]{:S(2)}) async-start(bf16[16,2,16,1024]{3,2,1,0:T(8,128)(2,1)} %copy-done.9), calls=%async_computation.4 | async-start | bytes 2097152 | tf_op jit(solution)/shard_map/all_to_all | solution.py:41
  148.7 3.2 %pad_maximum_fusion = (bf16[1024,1024]{1,0:T(8,128)(2,1)}, bf16[1024,1024]{1,0:T(8,128)(2,1)}) fusion(bf16[256,1024]{1,0:T(8,128)(2,1)S(1)} %bitcast.54, bf16[256,1024]{1,0:T(8,128)(2,1)} %bitcast.52, bf16[256,1024]{1,0:T(8,128)(2,1)S(1)} %bitcast.50, bf16[256,1024]{1,0:T(8,128)(2,1)S(1)} %bitcast.48, bf16[256,1024]{1,0:T(8,128)(2,1)S(1)} %bitcast.53, ...), kind=kLoop, calls=%fused_computation | loop fusion | flops 16777216 | bytes 8388608 | tf_op jit(solution)/shard_map/concatenate | solution.py:157
  152.9 3.1 %collective-permute-start.12 = (bf16[256,512]{1,0:T(8,128)(2,1)S(1)}, bf16[256,512]{1,0:T(8,128)(2,1)S(1)}, u32[]{:S(2)}, u32[]{:S(2)}) collective-permute-start(bf16[256,512]{1,0:T(8,128)(2,1)S(1)} %slice.97), channel_id=1, source_target_pairs={{0,64},{64,0},{1,65},{65,1},{2,66},{66,2},{3,67},{67,3},{4,68},{68... | collective-permute-start | bytes 786440 | tf_op jit(solution)/shard_map/ppermute | solution.py:37
  164.0 5.8 %all-to-all-start.5 = ((bf16[16,2,16,1024]{3,2,1,0:T(8,128)(2,1)}), bf16[16,2,16,1024]{3,2,1,0:T(8,128)(2,1)S(1)}, u32[]{:S(2)}, u32[]{:S(2)}) async-start(bf16[16,2,16,1024]{3,2,1,0:T(8,128)(2,1)} %shard_map.78), calls=%async_computation.5 | async-start | bytes 2097152 | tf_op jit(solution)/shard_map/all_to_all | solution.py:41
  169.8 9.5 %collective-permute-start.13 = (bf16[2,16,1024]{2,1,0:T(8,128)(2,1)S(1)}, bf16[2,16,1024]{2,1,0:T(8,128)(2,1)S(1)}, u32[]{:S(2)}, u32[]{:S(2)}) collective-permute-start(bf16[2,16,1024]{2,1,0:T(8,128)(2,1)S(1)} %convert_reduce_fusion.1), channel_id=1, source_target_pairs={{0,1},{1,0},{2,3},{3,2},{4,5},{5,4},{6,7},{7,6},{8,9},{9,8},{10,11... | collective-permute-start | bytes 196616 | tf_op jit(solution)/shard_map/ppermute | solution.py:37
  (99 shorter events, 45.5 us)
Async XLA Ops:
  0.6 14.5 %copy-start.1 = (bf16[256,1024]{1,0:T(8,128)(2,1)S(1)}, bf16[256,1024]{1,0:T(8,128)(2,1)}, u32[]{:S(2)}) copy-start(bf16[256,1024]{1,0:T(8,128)(2,1)} %out_a.7) | copy-start | bytes 1572868
  2.6 27.9 %all-to-all-start = ((bf16[16,2,16,1024]{3,2,1,0:T(8,128)(2,1)}), bf16[16,2,16,1024]{3,2,1,0:T(8,128)(2,1)S(1)}, u32[]{:S(2)}, u32[]{:S(2)}) async-start(bf16[16,2,16,1024]{3,2,1,0:T(8,128)(2,1)} %broadcast_in_dim.6), calls=%async_computation | async-start | bytes 2097152 | tf_op jit(solution)/shard_map/all_to_all | solution.py:41
  10.2 20.3 %collective-permute-start = (bf16[1024,256]{1,0:T(8,128)(2,1)S(1)}, bf16[1024,256]{1,0:T(8,128)(2,1)S(1)}, u32[]{:S(2)}, u32[]{:S(2)}) collective-permute-start(bf16[1024,256]{1,0:T(8,128)(2,1)S(1)} %copy-done), channel_id=1, source_target_pairs={{0,64},{64,0},{1,65},{65,1},{2,66},{66,2},{3,67},{67,3},{4,68},{68... | collective-permute-start | bytes 1572872 | tf_op jit(solution)/shard_map/ppermute | solution.py:37
  15.1 15.4 %collective-permute-start.1 = (bf16[256,1024]{1,0:T(8,128)(2,1)S(1)}, bf16[256,1024]{1,0:T(8,128)(2,1)S(1)}, u32[]{:S(2)}, u32[]{:S(2)}) collective-permute-start(bf16[256,1024]{1,0:T(8,128)(2,1)S(1)} %copy-done.1), channel_id=1, source_target_pairs={{0,64},{64,0},{1,65},{65,1},{2,66},{66,2},{3,67},{67,3},{4,68},{68... | collective-permute-start | bytes 1572872 | tf_op jit(solution)/shard_map/ppermute | solution.py:37
  17.0 18.8 %collective-permute-start.4 = (bf16[2,16,1024]{2,1,0:T(8,128)(2,1)S(1)}, bf16[2,16,1024]{2,1,0:T(8,128)(2,1)S(1)}, u32[]{:S(2)}, u32[]{:S(2)}) collective-permute-start(bf16[2,16,1024]{2,1,0:T(8,128)(2,1)S(1)} %pad_maximum_fusion.8), channel_id=1, source_target_pairs={{0,1},{1,0},{2,3},{3,2},{4,5},{5,4},{6,7},{7,6},{8,9},{9,8},{10,11... | collective-permute-start | bytes 196616 | tf_op jit(solution)/shard_map/ppermute | solution.py:37
  33.2 10.8 %collective-permute-start.2 = (bf16[2,64,1024]{2,1,0:T(8,128)(2,1)}, bf16[2,64,1024]{2,1,0:T(8,128)(2,1)S(1)}, u32[]{:S(2)}, u32[]{:S(2)}) collective-permute-start(bf16[2,64,1024]{2,1,0:T(8,128)(2,1)} %fusion.6), channel_id=1, source_target_pairs={{0,8},{8,0},{16,24},{24,16},{1,9},{9,1},{17,25},{25,17},{2,10},{10... | collective-permute-start | bytes 786440 | tf_op jit(solution)/shard_map/ppermute | solution.py:65
  37.0 22.5 %all-to-all-start.1 = ((bf16[16,2,16,1024]{3,2,1,0:T(8,128)(2,1)}), bf16[16,2,16,1024]{3,2,1,0:T(8,128)(2,1)S(1)}, u32[]{:S(2)}, u32[]{:S(2)}) async-start(bf16[16,2,16,1024]{3,2,1,0:T(8,128)(2,1)} %broadcast_in_dim.7), calls=%async_computation.1 | async-start | bytes 2097152 | tf_op jit(solution)/shard_map/all_to_all | solution.py:41
  45.9 10.5 %collective-permute-start.3 = (bf16[64,1024]{1,0:T(8,128)(2,1)S(1)}, bf16[64,1024]{1,0:T(8,128)(2,1)S(1)}, u32[]{:S(2)}, u32[]{:S(2)}) collective-permute-start(bf16[64,1024]{1,0:T(8,128)(2,1)S(1)} %fusion.7), channel_id=1, source_target_pairs={{0,16},{8,24},{16,0},{24,8},{1,17},{9,25},{17,1},{25,9},{2,18},{10... | collective-permute-start | bytes 393224 | tf_op jit(solution)/shard_map/ppermute | solution.py:65
  63.2 35.4 %all-to-all-start.2 = ((bf16[4,64,1024]{2,1,0:T(8,128)(2,1)}), bf16[4,64,1024]{2,1,0:T(8,128)(2,1)}, u32[]{:S(2)}, u32[]{:S(2)}) async-start(bf16[4,64,1024]{2,1,0:T(8,128)(2,1)} %bitcast.46), calls=%async_computation.2 | async-start | bytes 1048576 | tf_op jit(solution)/shard_map/all_to_all | solution.py:41
  67.3 11.5 %collective-permute-start.5 = (bf16[64,1024]{1,0:T(8,128)(2,1)S(1)}, bf16[64,1024]{1,0:T(8,128)(2,1)S(1)}, u32[]{:S(2)}, u32[]{:S(2)}) collective-permute-start(bf16[64,1024]{1,0:T(8,128)(2,1)S(1)} %convert_element_type.84), channel_id=1, source_target_pairs={{0,32},{32,0},{1,33},{33,1},{2,34},{34,2},{3,35},{35,3},{4,36},{36... | collective-permute-start | bytes 393224 | tf_op jit(solution)/shard_map/ppermute | solution.py:37
  73.7 26.0 %collective-permute-start.7 = (bf16[16,2,16,1024]{3,2,1,0:T(8,128)(2,1)S(1)}, bf16[16,2,16,1024]{3,2,1,0:T(8,128)(2,1)}, u32[]{:S(2)}, u32[]{:S(2)}) collective-permute-start(bf16[16,2,16,1024]{3,2,1,0:T(8,128)(2,1)S(1)} %all-to-all-done.rows), channel_id=1, source_target_pairs={{0,64},{64,0},{1,65},{65,1},{2,66},{66,2},{3,67},{67,3},{4,68},{68... | collective-permute-start | bytes 3145736 | tf_op jit(solution)/shard_map/ppermute | solution.py:37
  79.0 18.8 %collective-permute-start.6 = (bf16[64,1024]{1,0:T(8,128)(2,1)S(1)}, bf16[64,1024]{1,0:T(8,128)(2,1)S(1)}, u32[]{:S(2)}, u32[]{:S(2)}) collective-permute-start(bf16[64,1024]{1,0:T(8,128)(2,1)S(1)} %pad_maximum_fusion.6), channel_id=1, source_target_pairs={{0,16},{8,24},{16,0},{24,8},{1,17},{9,25},{17,1},{25,9},{2,18},{10... | collective-permute-start | bytes 393224 | tf_op jit(solution)/shard_map/ppermute | solution.py:71
  93.2 25.3 %collective-permute-start.10 = (bf16[16,2,16,1024]{3,2,1,0:T(8,128)(2,1)S(1)}, bf16[16,2,16,1024]{3,2,1,0:T(8,128)(2,1)}, u32[]{:S(2)}, u32[]{:S(2)}) collective-permute-start(bf16[16,2,16,1024]{3,2,1,0:T(8,128)(2,1)S(1)} %all-to-all-done.1.rows), channel_id=1, source_target_pairs={{0,64},{64,0},{1,65},{65,1},{2,66},{66,2},{3,67},{67,3},{4,68},{68... | collective-permute-start | bytes 3145736 | tf_op jit(solution)/shard_map/ppermute | solution.py:37
  100.4 16.2 %collective-permute-start.8 = (bf16[64,1024]{1,0:T(8,128)(2,1)}, bf16[64,1024]{1,0:T(8,128)(2,1)S(1)}, u32[]{:S(2)}, u32[]{:S(2)}) collective-permute-start(bf16[64,1024]{1,0:T(8,128)(2,1)} %convert_element_type.91), channel_id=1, source_target_pairs={{0,32},{32,0},{1,33},{33,1},{2,34},{34,2},{3,35},{35,3},{4,36},{36... | collective-permute-start | bytes 393224 | tf_op jit(solution)/shard_map/ppermute | solution.py:37
  103.0 13.6 %collective-permute-start.9 = (bf16[2,64,1024]{2,1,0:T(8,128)(2,1)}, bf16[2,64,1024]{2,1,0:T(8,128)(2,1)}, u32[]{:S(2)}, u32[]{:S(2)}) collective-permute-start(bf16[2,64,1024]{2,1,0:T(8,128)(2,1)} %pad_maximum_fusion.5), channel_id=1, source_target_pairs={{0,8},{8,0},{16,24},{24,16},{1,9},{9,1},{17,25},{25,17},{2,10},{10... | collective-permute-start | bytes 786440 | tf_op jit(solution)/shard_map/ppermute | solution.py:71
  119.5 20.0 %all-to-all-start.3 = ((bf16[4,64,1024]{2,1,0:T(8,128)(2,1)}), bf16[4,64,1024]{2,1,0:T(8,128)(2,1)}, u32[]{:S(2)}, u32[]{:S(2)}) async-start(bf16[4,64,1024]{2,1,0:T(8,128)(2,1)} %broadcast_in_dim.8), calls=%async_computation.3 | async-start | bytes 1048576 | tf_op jit(solution)/shard_map/all_to_all | solution.py:41
  126.6 12.9 %copy-start.4 = (bf16[1024,256]{1,0:T(8,128)(2,1)S(1)}, bf16[1024,256]{1,0:T(8,128)(2,1)}, u32[]{:S(2)}) copy-start(bf16[1024,256]{1,0:T(8,128)(2,1)} %copy-done.2) | copy-start | bytes 1572868
  126.6 12.9 %copy-start.7 = (bf16[256,1024]{1,0:T(8,128)(2,1)S(1)}, bf16[256,1024]{1,0:T(8,128)(2,1)}, u32[]{:S(2)}) copy-start(bf16[256,1024]{1,0:T(8,128)(2,1)} %copy-done.5) | copy-start | bytes 1572868
  129.7 29.8 %collective-permute-start.11 = (bf16[256,512]{1,0:T(8,128)(2,1)}, bf16[256,512]{1,0:T(8,128)(2,1)}, u32[]{:S(2)}, u32[]{:S(2)}) collective-permute-start(bf16[256,512]{1,0:T(8,128)(2,1)} %get-tuple-element.48), channel_id=1, source_target_pairs={{0,64},{64,0},{1,65},{65,1},{2,66},{66,2},{3,67},{67,3},{4,68},{68... | collective-permute-start | bytes 786440 | tf_op jit(solution)/shard_map/ppermute | solution.py:37
  142.2 20.4 %all-to-all-start.4 = ((bf16[16,2,16,1024]{3,2,1,0:T(8,128)(2,1)}), bf16[16,2,16,1024]{3,2,1,0:T(8,128)(2,1)}, u32[]{:S(2)}, u32[]{:S(2)}) async-start(bf16[16,2,16,1024]{3,2,1,0:T(8,128)(2,1)} %copy-done.9), calls=%async_computation.4 | async-start | bytes 2097152 | tf_op jit(solution)/shard_map/all_to_all | solution.py:41
  152.9 6.7 %collective-permute-start.12 = (bf16[256,512]{1,0:T(8,128)(2,1)S(1)}, bf16[256,512]{1,0:T(8,128)(2,1)S(1)}, u32[]{:S(2)}, u32[]{:S(2)}) collective-permute-start(bf16[256,512]{1,0:T(8,128)(2,1)S(1)} %slice.97), channel_id=1, source_target_pairs={{0,64},{64,0},{1,65},{65,1},{2,66},{66,2},{3,67},{67,3},{4,68},{68... | collective-permute-start | bytes 786440 | tf_op jit(solution)/shard_map/ppermute | solution.py:37
  164.0 17.6 %copy-start.12 = (bf16[1024,1024]{1,0:T(8,128)(2,1)S(1)}, bf16[1024,1024]{1,0:T(8,128)(2,1)}, u32[]{:S(2)}) copy-start(bf16[1024,1024]{1,0:T(8,128)(2,1)} %get-tuple-element.35) | copy-start | bytes 6291460
  164.0 21.9 %all-to-all-start.5 = ((bf16[16,2,16,1024]{3,2,1,0:T(8,128)(2,1)}), bf16[16,2,16,1024]{3,2,1,0:T(8,128)(2,1)S(1)}, u32[]{:S(2)}, u32[]{:S(2)}) async-start(bf16[16,2,16,1024]{3,2,1,0:T(8,128)(2,1)} %shard_map.78), calls=%async_computation.5 | async-start | bytes 2097152 | tf_op jit(solution)/shard_map/all_to_all | solution.py:41
  169.8 16.3 %collective-permute-start.13 = (bf16[2,16,1024]{2,1,0:T(8,128)(2,1)S(1)}, bf16[2,16,1024]{2,1,0:T(8,128)(2,1)S(1)}, u32[]{:S(2)}, u32[]{:S(2)}) collective-permute-start(bf16[2,16,1024]{2,1,0:T(8,128)(2,1)S(1)} %convert_reduce_fusion.1), channel_id=1, source_target_pairs={{0,1},{1,0},{2,3},{3,2},{4,5},{5,4},{6,7},{7,6},{8,9},{9,8},{10,11... | collective-permute-start | bytes 196616 | tf_op jit(solution)/shard_map/ppermute | solution.py:37
  (16 other events, 35.8 us)

commit v5 on v3

--- a/solution.py
+++ b/solution.py
@@ -66,12 +66,19 @@
     return kept + other.astype(f32)
 
 
-def double(value, stride, axis):
+def partner(value, stride):
+    return lax.ppermute(value, "zr", [(i, i ^ stride) for i in range(4)])
+
+
+def joined(value, other, stride, axis):
     upper = (lax.axis_index("zr") // stride) % 2 == 1
-    other = lax.ppermute(value, "zr", [(i, i ^ stride) for i in range(4)])
     return jnp.stack(
         [jnp.where(upper, other, value), jnp.where(upper, value, other)], axis=axis
     )
+
+
+def double(value, stride, axis):
+    return joined(value, partner(value, stride), stride, axis)
 
 
 def front_kernel(rows, in_a, in_b, out_a, out_b, result):
@@ -139,34 +146,36 @@
     far = gather_rows(after(other_rows, near))
     near_1 = run(front_kernel, near, weights, (256, 4 * u), f32)
     near_4 = halve(halve(near_1.reshape(2, 2, 64, 4 * u), 1, 1), 2, 0)
+    near_4, far = both(near_4, far)
     far_1 = run(front_kernel, far, weights, (256, 4 * u), bf16)
     near_c = swap(near, "c")
-    near_4, far_1 = both(near_4, far_1)
     far_4 = jnp.sum(
         exchange(far_1.reshape(4, 64, 4 * u), ("zr",)).astype(f32), axis=0
     )
     far_c = swap(far, "c")
-    near_8, far_4, near_c = both(cross(near_4), far_4, near_c)
-    far_8, mid_near, far_c = both(cross(far_4), double(middle(near_8), 2, 0), far_c)
+    near_8, far_4, near_c, far_c = both(cross(near_4), far_4, near_c, far_c)
+    x_all = jnp.concatenate([r[:, 0].reshape(256, n) for r in (near, far, near_c, far_c)])
+    dy_all = jnp.concatenate([r[:, 1].reshape(256, n) for r in (near, far, near_c, far_c)])
+    mid_near = middle(near_8)
+    far_8, mid_near, other, x_all, dy_all = both(
+        cross(far_4), mid_near, partner(mid_near, 2), x_all, dy_all
+    )
+    mid_near = joined(mid_near, other, 2, 0)
     mid_far, mid_near = both(gather_four(middle(far_8)), double(mid_near, 1, 1))
+    parts_far = last(mid_far)
     mid_near = mid_near.reshape(256, 4 * u)
-    parts_far = last(mid_far)
     far_sum = total_of(parts_far)
     parts_near = last(mid_near)
 
-    x_all = jnp.concatenate([r[:, 0].reshape(256, n) for r in (near, far, near_c, far_c)])
-    dy_all = jnp.concatenate([r[:, 1].reshape(256, n) for r in (near, far, near_c, far_c)])
-    far_sum, parts_near, mid_near, mid_far, x_all, dy_all = both(
-        far_sum, parts_near, mid_near, mid_far, x_all, dy_all
-    )
     mids = jnp.concatenate([mid_near, mid_far])
     theirs = swap(mids[:, 2 * u :], "c")
+    far_sum, parts_near, mids, theirs = both(far_sum, parts_near, mids, theirs)
     act_all = jnp.concatenate([mids[:, :u], theirs[:, :u]])
     grad_all = jnp.concatenate([mids[:, u : 2 * u], theirs[:, u:]])
     grad_w_in = dot_tn(x_all, grad_all).astype(bf16)
     grad_w_out = dot_tn(act_all, dy_all).astype(bf16)
     near_sum = total_of(parts_near)
-    outs = (near_sum + swap(far_sum, "h")).astype(bf16)
+    outs = (near_sum + swap(far_sum.astype(bf16), "h").astype(f32)).astype(bf16)
     return (outs[0], outs[1], grad_w_in, grad_w_out)
 
 

time: 196 us -> 181 us (0.923)
  waiting for transfers between devices: 47.9 us -> 36.4 us
  Pallas kernels: 4.89 us -> 2.85 us
    all_to_all x6, starting transfers between devices: 42 us -> 34 us  [exchange(): return lax.all_to_all(value, axes, 0, 0, tiled=True)]
    all_to_all x6, waiting for transfers between devices: 20.3 us -> 12.8 us  [exchange(): return lax.all_to_all(value, axes, 0, 0, tiled=True)]
    ppermute x2, starting transfers between devices: 7.76 us -> 14.8 us  [partner(): return lax.ppermute(value, 'zr', [(i, i ^ stride) for i in range(4)])]
    ppermute x9, waiting for transfers between devices: 9.44 us -> 3.33 us  [swap(): return lax.ppermute(value, axis, [(0, 1), (1, 0)])]
    concatenate x0 -> x3, other arithmetic: none -> 3.46 us  [the longest x2 1.95 us: shards(): mids = jnp.concatenate([mid_near, mid_far])]
    another operation x4, other arithmetic: 2.56 us -> 0.14 us  [joined(): jnp.stack([jnp.where(upper, other, value), jnp.where(upper, value, other)...]
    ppermute x2, waiting for transfers between devices: 10.7 us -> 12.9 us  [partner(): return lax.ppermute(value, 'zr', [(i, i ^ stride) for i in range(4)])]
    pallas_call x4, Pallas kernels: 4.89 us -> 2.85 us  [run(): pl.pallas_call(kernel, out_shape=result, in_specs=[pl.BlockSpec(memory_sp...]
  transfers between devices with their start and end apart: 19 -> 19, of which waited for: 7 -> 6; matrix products, arithmetic and copies ran while one was open for 11% -> 13% of each run, Pallas kernels for 1% -> 1%
where the time goes in v5:
time: 181 us; the launch traced here: 179 us
  starting transfers between devices  105 us (58%)
  waiting for transfers between devices  36.4 us (20%)
  local copies, waits for them, and re-layouts  17.6 us (10%)
  other arithmetic  12.7 us (7%)
  matrix products  3.07 us (2%)
  Pallas kernels  2.85 us (2%)
    ppermute x9, starting transfers between devices, swap(): return lax.ppermute(value, axis, [(0, 1), (1, 0)])  50.6 us
    all_to_all x6, starting transfers between devices, exchange(): return lax.all_to_all(value, axes, 0, 0, tiled=True)  34 us
    ppermute x2, starting transfers between devices, partner(): return lax.ppermute(value, 'zr', [(i, i ^ stride) for i in range(4)])  14.8 us
    ppermute x2, waiting for transfers between devices, partner(): return lax.ppermute(value, 'zr', [(i, i ^ stride) for i in range(4)])  12.9 us
    all_to_all x6, waiting for transfers between devices, exchange(): return lax.all_to_all(value, axes, 0, 0, tiled=True)  12.8 us
    ppermute x2, waiting for transfers between devices, halve(): lax.ppermute(send.astype(bf16), 'zr', [(i, i ^ stride) for i in range(4)])  7.4 us
    unnamed x38, local copies, waits for them, and re-layouts  6.87 us
    ppermute x2, starting transfers between devices, halve(): lax.ppermute(send.astype(bf16), 'zr', [(i, i ^ stride) for i in range(4)])  5.74 us
  transfers between devices with their start and end apart: 19, of which 6 were waited for; matrix products, arithmetic and copies ran while one was open for 13% of the time, Pallas kernels for 1%

profile of v5, /device:TPU:1, one launch (start us, length us, event | category | flops | bytes accessed | tf_op | source)
XLA Modules:
  0.0 179.0 jit_solution(9904952125857032081)
XLA Ops:
  2.6 7.6 %all-to-all-start = ((bf16[16,2,16,1024]{3,2,1,0:T(8,128)(2,1)}), bf16[16,2,16,1024]{3,2,1,0:T(8,128)(2,1)S(1)}, u32[]{:S(2)}, u32[]{:S(2)}) async-start(bf16[16,2,16,1024]{3,2,1,0:T(8,128)(2,1)} %broadcast_in_dim.6), calls=%async_computation | async-start | bytes 2097152 | tf_op jit(solution)/shard_map/all_to_all | solution.py:41
  10.2 4.9 %collective-permute-start = (bf16[1024,256]{1,0:T(8,128)(2,1)S(1)}, bf16[1024,256]{1,0:T(8,128)(2,1)S(1)}, u32[]{:S(2)}, u32[]{:S(2)}) collective-permute-start(bf16[1024,256]{1,0:T(8,128)(2,1)S(1)} %copy-done), channel_id=1, source_target_pairs={{0,64},{64,0},{1,65},{65,1},{2,66},{66,2},{3,67},{67,3},{4,68},{68... | collective-permute-start | bytes 1572872 | tf_op jit(solution)/shard_map/ppermute | solution.py:37
  15.1 1.9 %collective-permute-start.1 = (bf16[256,1024]{1,0:T(8,128)(2,1)S(1)}, bf16[256,1024]{1,0:T(8,128)(2,1)S(1)}, u32[]{:S(2)}, u32[]{:S(2)}) collective-permute-start(bf16[256,1024]{1,0:T(8,128)(2,1)S(1)} %copy-done.1), channel_id=1, source_target_pairs={{0,64},{64,0},{1,65},{65,1},{2,66},{66,2},{3,67},{67,3},{4,68},{68... | collective-permute-start | bytes 1572872 | tf_op jit(solution)/shard_map/ppermute | solution.py:37
  17.1 13.5 %collective-permute-start.4 = (bf16[2,16,1024]{2,1,0:T(8,128)(2,1)S(1)}, bf16[2,16,1024]{2,1,0:T(8,128)(2,1)S(1)}, u32[]{:S(2)}, u32[]{:S(2)}) collective-permute-start(bf16[2,16,1024]{2,1,0:T(8,128)(2,1)S(1)} %pad_maximum_fusion.7), channel_id=1, source_target_pairs={{0,1},{1,0},{2,3},{3,2},{4,5},{5,4},{6,7},{7,6},{8,9},{9,8},{10,11... | collective-permute-start | bytes 196616 | tf_op jit(solution)/shard_map/ppermute | solution.py:37
  33.2 2.6 %collective-permute-start.2 = (bf16[2,64,1024]{2,1,0:T(8,128)(2,1)}, bf16[2,64,1024]{2,1,0:T(8,128)(2,1)S(1)}, u32[]{:S(2)}, u32[]{:S(2)}) collective-permute-start(bf16[2,64,1024]{2,1,0:T(8,128)(2,1)} %fusion.7), channel_id=1, source_target_pairs={{0,8},{8,0},{16,24},{24,16},{1,9},{9,1},{17,25},{25,17},{2,10},{10... | collective-permute-start | bytes 786440 | tf_op jit(solution)/shard_map/ppermute | solution.py:65
  37.0 6.9 %all-to-all-start.1 = ((bf16[16,2,16,1024]{3,2,1,0:T(8,128)(2,1)}), bf16[16,2,16,1024]{3,2,1,0:T(8,128)(2,1)S(1)}, u32[]{:S(2)}, u32[]{:S(2)}) async-start(bf16[16,2,16,1024]{3,2,1,0:T(8,128)(2,1)} %broadcast_in_dim.7), calls=%async_computation.1 | async-start | bytes 2097152 | tf_op jit(solution)/shard_map/all_to_all | solution.py:41
  45.9 3.1 %collective-permute-start.3 = (bf16[64,1024]{1,0:T(8,128)(2,1)S(1)}, bf16[64,1024]{1,0:T(8,128)(2,1)S(1)}, u32[]{:S(2)}, u32[]{:S(2)}) collective-permute-start(bf16[64,1024]{1,0:T(8,128)(2,1)S(1)} %fusion.8), channel_id=1, source_target_pairs={{0,16},{8,24},{16,0},{24,8},{1,17},{9,25},{17,1},{25,9},{2,18},{10... | collective-permute-start | bytes 393224 | tf_op jit(solution)/shard_map/ppermute | solution.py:65
  49.0 7.4 %collective-permute-done.3 = bf16[64,1024]{1,0:T(8,128)(2,1)S(1)} collective-permute-done((bf16[64,1024]{1,0:T(8,128)(2,1)S(1)}, bf16[64,1024]{1,0:T(8,128)(2,1)S(1)}, u32[]{:S(2)}, u32[]{:S(2)}) %collective-permute-start.3) | collective-permute-done | bytes 131104 | tf_op jit(solution)/shard_map/ppermute | solution.py:65
  57.4 2.1 %all-to-all-done.1.rows = bf16[16,2,16,1024]{3,2,1,0:T(8,128)(2,1)S(1)} async-done(((bf16[16,2,16,1024]{3,2,1,0:T(8,128)(2,1)}), bf16[16,2,16,1024]{3,2,1,0:T(8,128)(2,1)S(1)}, u32[]{:S(2)}, u32[]{:S(2)}) %all-to-all-start.1) | async-done | bytes 1048608 | tf_op jit(solution)/shard_map/all_to_all | solution.py:41
  63.1 4.1 %all-to-all-start.2 = ((bf16[4,64,1024]{2,1,0:T(8,128)(2,1)}), bf16[4,64,1024]{2,1,0:T(8,128)(2,1)}, u32[]{:S(2)}, u32[]{:S(2)}) async-start(bf16[4,64,1024]{2,1,0:T(8,128)(2,1)} %bitcast.50), calls=%async_computation.2 | async-start | bytes 1048576 | tf_op jit(solution)/shard_map/all_to_all | solution.py:41
  67.3 4.8 %collective-permute-start.6 = (bf16[16,2,16,1024]{3,2,1,0:T(8,128)(2,1)S(1)}, bf16[16,2,16,1024]{3,2,1,0:T(8,128)(2,1)}, u32[]{:S(2)}, u32[]{:S(2)}) collective-permute-start(bf16[16,2,16,1024]{3,2,1,0:T(8,128)(2,1)S(1)} %all-to-all-done.rows), channel_id=1, source_target_pairs={{0,64},{64,0},{1,65},{65,1},{2,66},{66,2},{3,67},{67,3},{4,68},{68... | collective-permute-start | bytes 3145736 | tf_op jit(solution)/shard_map/ppermute | solution.py:37
  72.1 1.9 %collective-permute-start.7 = (bf16[16,2,16,1024]{3,2,1,0:T(8,128)(2,1)S(1)}, bf16[16,2,16,1024]{3,2,1,0:T(8,128)(2,1)}, u32[]{:S(2)}, u32[]{:S(2)}) collective-permute-start(bf16[16,2,16,1024]{3,2,1,0:T(8,128)(2,1)S(1)} %all-to-all-done.1.rows), channel_id=1, source_target_pairs={{0,64},{64,0},{1,65},{65,1},{2,66},{66,2},{3,67},{67,3},{4,68},{68... | collective-permute-start | bytes 3145736 | tf_op jit(solution)/shard_map/ppermute | solution.py:37
  75.1 6.4 %collective-permute-start.5 = (bf16[64,1024]{1,0:T(8,128)(2,1)S(1)}, bf16[64,1024]{1,0:T(8,128)(2,1)S(1)}, u32[]{:S(2)}, u32[]{:S(2)}) collective-permute-start(bf16[64,1024]{1,0:T(8,128)(2,1)S(1)} %convert_element_type.84), channel_id=1, source_target_pairs={{0,32},{32,0},{1,33},{33,1},{2,34},{34,2},{3,35},{35,3},{4,36},{36... | collective-permute-start | bytes 393224 | tf_op jit(solution)/shard_map/ppermute | solution.py:37
  82.6 3.3 %collective-permute-done.5 = bf16[64,1024]{1,0:T(8,128)(2,1)S(1)} collective-permute-done((bf16[64,1024]{1,0:T(8,128)(2,1)S(1)}, bf16[64,1024]{1,0:T(8,128)(2,1)S(1)}, u32[]{:S(2)}, u32[]{:S(2)}) %collective-permute-start.5) | collective-permute-done | bytes 131104 | tf_op jit(solution)/shard_map/ppermute | solution.py:37
  87.9 5.9 %collective-permute-start.8 = (bf16[64,1024]{1,0:T(8,128)(2,1)S(1)}, bf16[64,1024]{1,0:T(8,128)(2,1)S(1)}, u32[]{:S(2)}, u32[]{:S(2)}) collective-permute-start(bf16[64,1024]{1,0:T(8,128)(2,1)S(1)} %convert_element_type.87), channel_id=1, source_target_pairs={{0,32},{32,0},{1,33},{33,1},{2,34},{34,2},{3,35},{35,3},{4,36},{36... | collective-permute-start | bytes 393224 | tf_op jit(solution)/shard_map/ppermute | solution.py:37
  94.9 10.6 %collective-permute-start.9 = (bf16[64,1024]{1,0:T(8,128)(2,1)S(1)}, bf16[64,1024]{1,0:T(8,128)(2,1)S(1)}, u32[]{:S(2)}, u32[]{:S(2)}) collective-permute-start(bf16[64,1024]{1,0:T(8,128)(2,1)S(1)} %pad_maximum_fusion.5), channel_id=1, source_target_pairs={{0,16},{8,24},{16,0},{24,8},{1,17},{9,25},{17,1},{25,9},{2,18},{10... | collective-permute-start | bytes 393224 | tf_op jit(solution)/shard_map/ppermute | solution.py:70
  111.4 6.7 %all-to-all-start.3 = ((bf16[4,64,1024]{2,1,0:T(8,128)(2,1)}), bf16[4,64,1024]{2,1,0:T(8,128)(2,1)S(1)}, u32[]{:S(2)}, u32[]{:S(2)}) async-start(bf16[4,64,1024]{2,1,0:T(8,128)(2,1)} %broadcast_in_dim.8), calls=%async_computation.3 | async-start | bytes 1048576 | tf_op jit(solution)/shard_map/all_to_all | solution.py:41
  118.2 4.1 %collective-permute-start.10 = (bf16[2,64,1024]{2,1,0:T(8,128)(2,1)S(1)}, bf16[2,64,1024]{2,1,0:T(8,128)(2,1)S(1)}, u32[]{:S(2)}, u32[]{:S(2)}) collective-permute-start(bf16[2,64,1024]{2,1,0:T(8,128)(2,1)S(1)} %pad_maximum_fusion.4), channel_id=1, source_target_pairs={{0,8},{8,0},{16,24},{24,16},{1,9},{9,1},{17,25},{25,17},{2,10},{10... | collective-permute-start | bytes 786440 | tf_op jit(solution)/shard_map/ppermute | solution.py:70
  122.3 12.9 %collective-permute-done.10 = bf16[2,64,1024]{2,1,0:T(8,128)(2,1)S(1)} collective-permute-done((bf16[2,64,1024]{2,1,0:T(8,128)(2,1)S(1)}, bf16[2,64,1024]{2,1,0:T(8,128)(2,1)S(1)}, u32[]{:S(2)}, u32[]{:S(2)}) %collective-permute-start.10) | collective-permute-done | bytes 262176 | tf_op jit(solution)/shard_map/ppermute | solution.py:70
  137.0 4.3 %all-to-all-start.4 = ((bf16[16,2,16,1024]{3,2,1,0:T(8,128)(2,1)}), bf16[16,2,16,1024]{3,2,1,0:T(8,128)(2,1)}, u32[]{:S(2)}, u32[]{:S(2)}) async-start(bf16[16,2,16,1024]{3,2,1,0:T(8,128)(2,1)} %copy-done.9), calls=%async_computation.4 | async-start | bytes 2097152 | tf_op jit(solution)/shard_map/all_to_all | solution.py:41
  142.2 2.9 %collective-permute-start.11 = (bf16[512,512]{1,0:T(8,128)(2,1)}, bf16[512,512]{1,0:T(8,128)(2,1)}, u32[]{:S(2)}, u32[]{:S(2)}) collective-permute-start(bf16[512,512]{1,0:T(8,128)(2,1)} %fusion), channel_id=1, source_target_pairs={{0,64},{64,0},{1,65},{65,1},{2,66},{66,2},{3,67},{67,3},{4,68},{68... | collective-permute-start | bytes 1572872 | tf_op jit(solution)/shard_map/ppermute | solution.py:37
  148.0 9.3 %all-to-all-done.4 = bf16[16,2,16,1024]{3,2,1,0:T(8,128)(2,1)} async-done(((bf16[16,2,16,1024]{3,2,1,0:T(8,128)(2,1)}), bf16[16,2,16,1024]{3,2,1,0:T(8,128)(2,1)}, u32[]{:S(2)}, u32[]{:S(2)}) %all-to-all-start.4) | async-done | bytes 1048608 | tf_op jit(solution)/shard_map/all_to_all | solution.py:41
  158.7 4.3 %all-to-all-start.5 = ((bf16[16,2,16,1024]{3,2,1,0:T(8,128)(2,1)}), bf16[16,2,16,1024]{3,2,1,0:T(8,128)(2,1)S(1)}, u32[]{:S(2)}, u32[]{:S(2)}) async-start(bf16[16,2,16,1024]{3,2,1,0:T(8,128)(2,1)} %copy-done.8), calls=%async_computation.5 | async-start | bytes 2097152 | tf_op jit(solution)/shard_map/all_to_all | solution.py:41
  163.0 8.4 %collective-permute-start.12 = (bf16[2,16,1024]{2,1,0:T(8,128)(2,1)S(1)}, bf16[2,16,1024]{2,1,0:T(8,128)(2,1)S(1)}, u32[]{:S(2)}, u32[]{:S(2)}) collective-permute-start(bf16[2,16,1024]{2,1,0:T(8,128)(2,1)S(1)} %convert_reduce_fusion.1), channel_id=1, source_target_pairs={{0,1},{1,0},{2,3},{3,2},{4,5},{5,4},{6,7},{7,6},{8,9},{9,8},{10,11... | collective-permute-start | bytes 196616 | tf_op jit(solution)/shard_map/ppermute | solution.py:37
  (92 shorter events, 37.6 us)
Async XLA Ops:
  0.6 14.5 %copy-start.1 = (bf16[256,1024]{1,0:T(8,128)(2,1)S(1)}, bf16[256,1024]{1,0:T(8,128)(2,1)}, u32[]{:S(2)}) copy-start(bf16[256,1024]{1,0:T(8,128)(2,1)} %out_a.7) | copy-start | bytes 1572868
  2.6 27.9 %all-to-all-start = ((bf16[16,2,16,1024]{3,2,1,0:T(8,128)(2,1)}), bf16[16,2,16,1024]{3,2,1,0:T(8,128)(2,1)S(1)}, u32[]{:S(2)}, u32[]{:S(2)}) async-start(bf16[16,2,16,1024]{3,2,1,0:T(8,128)(2,1)} %broadcast_in_dim.6), calls=%async_computation | async-start | bytes 2097152 | tf_op jit(solution)/shard_map/all_to_all | solution.py:41
  10.2 20.3 %collective-permute-start = (bf16[1024,256]{1,0:T(8,128)(2,1)S(1)}, bf16[1024,256]{1,0:T(8,128)(2,1)S(1)}, u32[]{:S(2)}, u32[]{:S(2)}) collective-permute-start(bf16[1024,256]{1,0:T(8,128)(2,1)S(1)} %copy-done), channel_id=1, source_target_pairs={{0,64},{64,0},{1,65},{65,1},{2,66},{66,2},{3,67},{67,3},{4,68},{68... | collective-permute-start | bytes 1572872 | tf_op jit(solution)/shard_map/ppermute | solution.py:37
  15.1 15.4 %collective-permute-start.1 = (bf16[256,1024]{1,0:T(8,128)(2,1)S(1)}, bf16[256,1024]{1,0:T(8,128)(2,1)S(1)}, u32[]{:S(2)}, u32[]{:S(2)}) collective-permute-start(bf16[256,1024]{1,0:T(8,128)(2,1)S(1)} %copy-done.1), channel_id=1, source_target_pairs={{0,64},{64,0},{1,65},{65,1},{2,66},{66,2},{3,67},{67,3},{4,68},{68... | collective-permute-start | bytes 1572872 | tf_op jit(solution)/shard_map/ppermute | solution.py:37
  17.1 18.8 %collective-permute-start.4 = (bf16[2,16,1024]{2,1,0:T(8,128)(2,1)S(1)}, bf16[2,16,1024]{2,1,0:T(8,128)(2,1)S(1)}, u32[]{:S(2)}, u32[]{:S(2)}) collective-permute-start(bf16[2,16,1024]{2,1,0:T(8,128)(2,1)S(1)} %pad_maximum_fusion.7), channel_id=1, source_target_pairs={{0,1},{1,0},{2,3},{3,2},{4,5},{5,4},{6,7},{7,6},{8,9},{9,8},{10,11... | collective-permute-start | bytes 196616 | tf_op jit(solution)/shard_map/ppermute | solution.py:37
  33.2 10.7 %collective-permute-start.2 = (bf16[2,64,1024]{2,1,0:T(8,128)(2,1)}, bf16[2,64,1024]{2,1,0:T(8,128)(2,1)S(1)}, u32[]{:S(2)}, u32[]{:S(2)}) collective-permute-start(bf16[2,64,1024]{2,1,0:T(8,128)(2,1)} %fusion.7), channel_id=1, source_target_pairs={{0,8},{8,0},{16,24},{24,16},{1,9},{9,1},{17,25},{25,17},{2,10},{10... | collective-permute-start | bytes 786440 | tf_op jit(solution)/shard_map/ppermute | solution.py:65
  37.0 22.5 %all-to-all-start.1 = ((bf16[16,2,16,1024]{3,2,1,0:T(8,128)(2,1)}), bf16[16,2,16,1024]{3,2,1,0:T(8,128)(2,1)S(1)}, u32[]{:S(2)}, u32[]{:S(2)}) async-start(bf16[16,2,16,1024]{3,2,1,0:T(8,128)(2,1)} %broadcast_in_dim.7), calls=%async_computation.1 | async-start | bytes 2097152 | tf_op jit(solution)/shard_map/all_to_all | solution.py:41
  45.9 10.5 %collective-permute-start.3 = (bf16[64,1024]{1,0:T(8,128)(2,1)S(1)}, bf16[64,1024]{1,0:T(8,128)(2,1)S(1)}, u32[]{:S(2)}, u32[]{:S(2)}) collective-permute-start(bf16[64,1024]{1,0:T(8,128)(2,1)S(1)} %fusion.8), channel_id=1, source_target_pairs={{0,16},{8,24},{16,0},{24,8},{1,17},{9,25},{17,1},{25,9},{2,18},{10... | collective-permute-start | bytes 393224 | tf_op jit(solution)/shard_map/ppermute | solution.py:65
  63.1 23.6 %all-to-all-start.2 = ((bf16[4,64,1024]{2,1,0:T(8,128)(2,1)}), bf16[4,64,1024]{2,1,0:T(8,128)(2,1)}, u32[]{:S(2)}, u32[]{:S(2)}) async-start(bf16[4,64,1024]{2,1,0:T(8,128)(2,1)} %bitcast.50), calls=%async_computation.2 | async-start | bytes 1048576 | tf_op jit(solution)/shard_map/all_to_all | solution.py:41
  67.3 20.6 %collective-permute-start.6 = (bf16[16,2,16,1024]{3,2,1,0:T(8,128)(2,1)S(1)}, bf16[16,2,16,1024]{3,2,1,0:T(8,128)(2,1)}, u32[]{:S(2)}, u32[]{:S(2)}) collective-permute-start(bf16[16,2,16,1024]{3,2,1,0:T(8,128)(2,1)S(1)} %all-to-all-done.rows), channel_id=1, source_target_pairs={{0,64},{64,0},{1,65},{65,1},{2,66},{66,2},{3,67},{67,3},{4,68},{68... | collective-permute-start | bytes 3145736 | tf_op jit(solution)/shard_map/ppermute | solution.py:37
  72.1 15.7 %collective-permute-start.7 = (bf16[16,2,16,1024]{3,2,1,0:T(8,128)(2,1)S(1)}, bf16[16,2,16,1024]{3,2,1,0:T(8,128)(2,1)}, u32[]{:S(2)}, u32[]{:S(2)}) collective-permute-start(bf16[16,2,16,1024]{3,2,1,0:T(8,128)(2,1)S(1)} %all-to-all-done.1.rows), channel_id=1, source_target_pairs={{0,64},{64,0},{1,65},{65,1},{2,66},{66,2},{3,67},{67,3},{4,68},{68... | collective-permute-start | bytes 3145736 | tf_op jit(solution)/shard_map/ppermute | solution.py:37
  75.1 10.8 %collective-permute-start.5 = (bf16[64,1024]{1,0:T(8,128)(2,1)S(1)}, bf16[64,1024]{1,0:T(8,128)(2,1)S(1)}, u32[]{:S(2)}, u32[]{:S(2)}) collective-permute-start(bf16[64,1024]{1,0:T(8,128)(2,1)S(1)} %convert_element_type.84), channel_id=1, source_target_pairs={{0,32},{32,0},{1,33},{33,1},{2,34},{34,2},{3,35},{35,3},{4,36},{36... | collective-permute-start | bytes 393224 | tf_op jit(solution)/shard_map/ppermute | solution.py:37
  87.9 22.5 %collective-permute-start.8 = (bf16[64,1024]{1,0:T(8,128)(2,1)S(1)}, bf16[64,1024]{1,0:T(8,128)(2,1)S(1)}, u32[]{:S(2)}, u32[]{:S(2)}) collective-permute-start(bf16[64,1024]{1,0:T(8,128)(2,1)S(1)} %convert_element_type.87), channel_id=1, source_target_pairs={{0,32},{32,0},{1,33},{33,1},{2,34},{34,2},{3,35},{35,3},{4,36},{36... | collective-permute-start | bytes 393224 | tf_op jit(solution)/shard_map/ppermute | solution.py:37
  94.9 12.5 %copy-start.15 = (bf16[16,1,16,1024]{3,2,1,0:T(8,128)(2,1)S(1)}, bf16[16,1,16,1024]{3,2,1,0:T(8,128)(2,1)}, u32[]{:S(2)}) copy-start(bf16[16,1,16,1024]{3,2,1,0:T(8,128)(2,1)} %get-tuple-element.43) | copy-start | bytes 1572868
  94.9 15.6 %collective-permute-start.9 = (bf16[64,1024]{1,0:T(8,128)(2,1)S(1)}, bf16[64,1024]{1,0:T(8,128)(2,1)S(1)}, u32[]{:S(2)}, u32[]{:S(2)}) collective-permute-start(bf16[64,1024]{1,0:T(8,128)(2,1)S(1)} %pad_maximum_fusion.5), channel_id=1, source_target_pairs={{0,16},{8,24},{16,0},{24,8},{1,17},{9,25},{17,1},{25,9},{2,18},{10... | collective-permute-start | bytes 393224 | tf_op jit(solution)/shard_map/ppermute | solution.py:70
  111.4 23.9 %copy-start.4 = (bf16[1024,256]{1,0:T(8,128)(2,1)S(1)}, bf16[1024,256]{1,0:T(8,128)(2,1)}, u32[]{:S(2)}) copy-start(bf16[1024,256]{1,0:T(8,128)(2,1)} %copy-done.2) | copy-start | bytes 1572868
  111.4 23.9 %copy-start.7 = (bf16[256,1024]{1,0:T(8,128)(2,1)S(1)}, bf16[256,1024]{1,0:T(8,128)(2,1)}, u32[]{:S(2)}) copy-start(bf16[256,1024]{1,0:T(8,128)(2,1)} %copy-done.5) | copy-start | bytes 1572868
  111.4 23.9 %all-to-all-start.3 = ((bf16[4,64,1024]{2,1,0:T(8,128)(2,1)}), bf16[4,64,1024]{2,1,0:T(8,128)(2,1)S(1)}, u32[]{:S(2)}, u32[]{:S(2)}) async-start(bf16[4,64,1024]{2,1,0:T(8,128)(2,1)} %broadcast_in_dim.8), calls=%async_computation.3 | async-start | bytes 1048576 | tf_op jit(solution)/shard_map/all_to_all | solution.py:41
  118.2 17.0 %collective-permute-start.10 = (bf16[2,64,1024]{2,1,0:T(8,128)(2,1)S(1)}, bf16[2,64,1024]{2,1,0:T(8,128)(2,1)S(1)}, u32[]{:S(2)}, u32[]{:S(2)}) collective-permute-start(bf16[2,64,1024]{2,1,0:T(8,128)(2,1)S(1)} %pad_maximum_fusion.4), channel_id=1, source_target_pairs={{0,8},{8,0},{16,24},{24,16},{1,9},{9,1},{17,25},{25,17},{2,10},{10... | collective-permute-start | bytes 786440 | tf_op jit(solution)/shard_map/ppermute | solution.py:70
  137.0 20.3 %all-to-all-start.4 = ((bf16[16,2,16,1024]{3,2,1,0:T(8,128)(2,1)}), bf16[16,2,16,1024]{3,2,1,0:T(8,128)(2,1)}, u32[]{:S(2)}, u32[]{:S(2)}) async-start(bf16[16,2,16,1024]{3,2,1,0:T(8,128)(2,1)} %copy-done.9), calls=%async_computation.4 | async-start | bytes 2097152 | tf_op jit(solution)/shard_map/all_to_all | solution.py:41
  142.2 16.5 %collective-permute-start.11 = (bf16[512,512]{1,0:T(8,128)(2,1)}, bf16[512,512]{1,0:T(8,128)(2,1)}, u32[]{:S(2)}, u32[]{:S(2)}) collective-permute-start(bf16[512,512]{1,0:T(8,128)(2,1)} %fusion), channel_id=1, source_target_pairs={{0,64},{64,0},{1,65},{65,1},{2,66},{66,2},{3,67},{67,3},{4,68},{68... | collective-permute-start | bytes 1572872 | tf_op jit(solution)/shard_map/ppermute | solution.py:37
  158.7 15.1 %copy-start.12 = (bf16[1024,1024]{1,0:T(8,128)(2,1)S(1)}, bf16[1024,1024]{1,0:T(8,128)(2,1)}, u32[]{:S(2)}) copy-start(bf16[1024,1024]{1,0:T(8,128)(2,1)} %pad_maximum_fusion.1) | copy-start | bytes 6291460
  158.7 19.5 %all-to-all-start.5 = ((bf16[16,2,16,1024]{3,2,1,0:T(8,128)(2,1)}), bf16[16,2,16,1024]{3,2,1,0:T(8,128)(2,1)S(1)}, u32[]{:S(2)}, u32[]{:S(2)}) async-start(bf16[16,2,16,1024]{3,2,1,0:T(8,128)(2,1)} %copy-done.8), calls=%async_computation.5 | async-start | bytes 2097152 | tf_op jit(solution)/shard_map/all_to_all | solution.py:41
  163.0 15.3 %collective-permute-start.12 = (bf16[2,16,1024]{2,1,0:T(8,128)(2,1)S(1)}, bf16[2,16,1024]{2,1,0:T(8,128)(2,1)S(1)}, u32[]{:S(2)}, u32[]{:S(2)}) collective-permute-start(bf16[2,16,1024]{2,1,0:T(8,128)(2,1)S(1)} %convert_reduce_fusion.1), channel_id=1, source_target_pairs={{0,1},{1,0},{2,3},{3,2},{4,5},{5,4},{6,7},{7,6},{8,9},{9,8},{10,11... | collective-permute-start | bytes 196616 | tf_op jit(solution)/shard_map/ppermute | solution.py:37
  (14 other events, 36.4 us)

commit v6 on v5

--- a/solution.py
+++ b/solution.py
@@ -152,24 +152,29 @@
     far_4 = jnp.sum(
         exchange(far_1.reshape(4, 64, 4 * u), ("zr",)).astype(f32), axis=0
     )
+    near_8, far_4, near_c = both(cross(near_4), far_4, near_c)
+    mid_near = middle(near_8)
+    far_8, mid_near, other, far = both(
+        cross(far_4), mid_near, partner(mid_near, 2), far
+    )
     far_c = swap(far, "c")
-    near_8, far_4, near_c, far_c = both(cross(near_4), far_4, near_c, far_c)
+    mid_near = joined(mid_near, other, 2, 0)
+    mid_far, mid_near, far_c = both(
+        gather_four(middle(far_8)), double(mid_near, 1, 1), far_c
+    )
+    parts_far = last(mid_far)
+    mid_near = mid_near.reshape(256, 4 * u)
+    far_parts = exchange(parts_far)
+    parts_near = last(mid_near)
+
     x_all = jnp.concatenate([r[:, 0].reshape(256, n) for r in (near, far, near_c, far_c)])
     dy_all = jnp.concatenate([r[:, 1].reshape(256, n) for r in (near, far, near_c, far_c)])
-    mid_near = middle(near_8)
-    far_8, mid_near, other, x_all, dy_all = both(
-        cross(far_4), mid_near, partner(mid_near, 2), x_all, dy_all
-    )
-    mid_near = joined(mid_near, other, 2, 0)
-    mid_far, mid_near = both(gather_four(middle(far_8)), double(mid_near, 1, 1))
-    parts_far = last(mid_far)
-    mid_near = mid_near.reshape(256, 4 * u)
-    far_sum = total_of(parts_far)
-    parts_near = last(mid_near)
-
     mids = jnp.concatenate([mid_near, mid_far])
     theirs = swap(mids[:, 2 * u :], "c")
-    far_sum, parts_near, mids, theirs = both(far_sum, parts_near, mids, theirs)
+    far_parts, parts_near, mids, theirs, x_all, dy_all = both(
+        far_parts, parts_near, mids, theirs, x_all, dy_all
+    )
+    far_sum = jnp.sum(far_parts.astype(f32), axis=0)
     act_all = jnp.concatenate([mids[:, :u], theirs[:, :u]])
     grad_all = jnp.concatenate([mids[:, u : 2 * u], theirs[:, u:]])
     grad_w_in = dot_tn(x_all, grad_all).astype(bf16)

time: 181 us -> 181 us (level)
  waiting for transfers between devices: 36.4 us -> 32.9 us
  other arithmetic: 12.7 us -> 10.7 us
  starting transfers between devices: 105 us -> 107 us
  local copies, waits for them, and re-layouts: 17.6 us -> 19.5 us
    ppermute x2, waiting for transfers between devices: 12.9 us -> 10.5 us  [partner(): return lax.ppermute(value, 'zr', [(i, i ^ stride) for i in range(4)])]
    all_to_all x6, waiting for transfers between devices: 12.8 us -> 10.7 us  [exchange(): return lax.all_to_all(value, axes, 0, 0, tiled=True)]
    unnamed x38 -> x40, local copies, waits for them, and re-layouts: 6.87 us -> 7.95 us
    slice x3 -> x4, local copies, waits for them, and re-layouts: 4.02 us -> 4.8 us  [shards(): r[:, 1].reshape(256, n)]
  transfers between devices with their start and end apart: 19 -> 19, of which waited for: 6 -> 7; matrix products, arithmetic and copies ran while one was open for 13% -> 12% of each run, Pallas kernels for 1% -> 1%
where the time goes in v6:
time: 181 us; the launch traced here: 178 us
  starting transfers between devices  107 us (59%)
  waiting for transfers between devices  32.9 us (18%)
  local copies, waits for them, and re-layouts  19.5 us (11%)
  other arithmetic  10.7 us (6%)
  Pallas kernels  3.82 us (2%)
  matrix products  3.08 us (2%)
    ppermute x9, starting transfers between devices, swap(): return lax.ppermute(value, axis, [(0, 1), (1, 0)])  52.1 us
    all_to_all x6, starting transfers between devices, exchange(): return lax.all_to_all(value, axes, 0, 0, tiled=True)  35.3 us
    ppermute x2, starting transfers between devices, partner(): return lax.ppermute(value, 'zr', [(i, i ^ stride) for i in range(4)])  14 us
    all_to_all x6, waiting for transfers between devices, exchange(): return lax.all_to_all(value, axes, 0, 0, tiled=True)  10.7 us
    ppermute x2, waiting for transfers between devices, partner(): return lax.ppermute(value, 'zr', [(i, i ^ stride) for i in range(4)])  10.5 us
    unnamed x40, local copies, waits for them, and re-layouts  7.95 us
    ppermute x2, waiting for transfers between devices, halve(): lax.ppermute(send.astype(bf16), 'zr', [(i, i ^ stride) for i in range(4)])  7.4 us
    ppermute x2, starting transfers between devices, halve(): lax.ppermute(send.astype(bf16), 'zr', [(i, i ^ stride) for i in range(4)])  5.74 us
  transfers between devices with their start and end apart: 19, of which 7 were waited for; matrix products, arithmetic and copies ran while one was open for 12% of the time, Pallas kernels for 1%

profile of v6, /device:TPU:1, one launch (start us, length us, event | category | flops | bytes accessed | tf_op | source)
XLA Modules:
  0.0 178.3 jit_solution(3903189161958715409)
XLA Ops:
  2.6 7.6 %all-to-all-start = ((bf16[16,2,16,1024]{3,2,1,0:T(8,128)(2,1)}), bf16[16,2,16,1024]{3,2,1,0:T(8,128)(2,1)S(1)}, u32[]{:S(2)}, u32[]{:S(2)}) async-start(bf16[16,2,16,1024]{3,2,1,0:T(8,128)(2,1)} %broadcast_in_dim.6), calls=%async_computation | async-start | bytes 2097152 | tf_op jit(solution)/shard_map/all_to_all | solution.py:41
  10.2 4.9 %collective-permute-start = (bf16[1024,256]{1,0:T(8,128)(2,1)S(1)}, bf16[1024,256]{1,0:T(8,128)(2,1)S(1)}, u32[]{:S(2)}, u32[]{:S(2)}) collective-permute-start(bf16[1024,256]{1,0:T(8,128)(2,1)S(1)} %copy-done), channel_id=1, source_target_pairs={{0,64},{64,0},{1,65},{65,1},{2,66},{66,2},{3,67},{67,3},{4,68},{68... | collective-permute-start | bytes 1572872 | tf_op jit(solution)/shard_map/ppermute | solution.py:37
  17.0 13.5 %collective-permute-start.4 = (bf16[2,16,1024]{2,1,0:T(8,128)(2,1)S(1)}, bf16[2,16,1024]{2,1,0:T(8,128)(2,1)S(1)}, u32[]{:S(2)}, u32[]{:S(2)}) collective-permute-start(bf16[2,16,1024]{2,1,0:T(8,128)(2,1)S(1)} %pad_maximum_fusion.7), channel_id=1, source_target_pairs={{0,1},{1,0},{2,3},{3,2},{4,5},{5,4},{6,7},{7,6},{8,9},{9,8},{10,11... | collective-permute-start | bytes 196616 | tf_op jit(solution)/shard_map/ppermute | solution.py:37
  33.2 2.6 %collective-permute-start.2 = (bf16[2,64,1024]{2,1,0:T(8,128)(2,1)}, bf16[2,64,1024]{2,1,0:T(8,128)(2,1)S(1)}, u32[]{:S(2)}, u32[]{:S(2)}) collective-permute-start(bf16[2,64,1024]{2,1,0:T(8,128)(2,1)} %fusion.7), channel_id=1, source_target_pairs={{0,8},{8,0},{16,24},{24,16},{1,9},{9,1},{17,25},{25,17},{2,10},{10... | collective-permute-start | bytes 786440 | tf_op jit(solution)/shard_map/ppermute | solution.py:65
  37.0 6.9 %all-to-all-start.1 = ((bf16[16,2,16,1024]{3,2,1,0:T(8,128)(2,1)}), bf16[16,2,16,1024]{3,2,1,0:T(8,128)(2,1)S(1)}, u32[]{:S(2)}, u32[]{:S(2)}) async-start(bf16[16,2,16,1024]{3,2,1,0:T(8,128)(2,1)} %broadcast_in_dim.7), calls=%async_computation.1 | async-start | bytes 2097152 | tf_op jit(solution)/shard_map/all_to_all | solution.py:41
  45.9 3.1 %collective-permute-start.3 = (bf16[64,1024]{1,0:T(8,128)(2,1)S(1)}, bf16[64,1024]{1,0:T(8,128)(2,1)S(1)}, u32[]{:S(2)}, u32[]{:S(2)}) collective-permute-start(bf16[64,1024]{1,0:T(8,128)(2,1)S(1)} %fusion.8), channel_id=1, source_target_pairs={{0,16},{8,24},{16,0},{24,8},{1,17},{9,25},{17,1},{25,9},{2,18},{10... | collective-permute-start | bytes 393224 | tf_op jit(solution)/shard_map/ppermute | solution.py:65
  49.0 7.4 %collective-permute-done.3 = bf16[64,1024]{1,0:T(8,128)(2,1)S(1)} collective-permute-done((bf16[64,1024]{1,0:T(8,128)(2,1)S(1)}, bf16[64,1024]{1,0:T(8,128)(2,1)S(1)}, u32[]{:S(2)}, u32[]{:S(2)}) %collective-permute-start.3) | collective-permute-done | bytes 131104 | tf_op jit(solution)/shard_map/ppermute | solution.py:65
  63.1 3.5 %all-to-all-start.2 = ((bf16[4,64,1024]{2,1,0:T(8,128)(2,1)}), bf16[4,64,1024]{2,1,0:T(8,128)(2,1)S(1)}, u32[]{:S(2)}, u32[]{:S(2)}) async-start(bf16[4,64,1024]{2,1,0:T(8,128)(2,1)} %bitcast.50), calls=%async_computation.2 | async-start | bytes 1048576 | tf_op jit(solution)/shard_map/all_to_all | solution.py:41
  66.6 4.8 %collective-permute-start.6 = (bf16[16,2,16,1024]{3,2,1,0:T(8,128)(2,1)S(1)}, bf16[16,2,16,1024]{3,2,1,0:T(8,128)(2,1)}, u32[]{:S(2)}, u32[]{:S(2)}) collective-permute-start(bf16[16,2,16,1024]{3,2,1,0:T(8,128)(2,1)S(1)} %all-to-all-done.rows), channel_id=1, source_target_pairs={{0,64},{64,0},{1,65},{65,1},{2,66},{66,2},{3,67},{67,3},{4,68},{68... | collective-permute-start | bytes 3145736 | tf_op jit(solution)/shard_map/ppermute | solution.py:37
  71.5 7.0 %collective-permute-start.5 = (bf16[64,1024]{1,0:T(8,128)(2,1)S(1)}, bf16[64,1024]{1,0:T(8,128)(2,1)S(1)}, u32[]{:S(2)}, u32[]{:S(2)}) collective-permute-start(bf16[64,1024]{1,0:T(8,128)(2,1)S(1)} %convert_element_type.80), channel_id=1, source_target_pairs={{0,32},{32,0},{1,33},{33,1},{2,34},{34,2},{3,35},{35,3},{4,36},{36... | collective-permute-start | bytes 393224 | tf_op jit(solution)/shard_map/ppermute | solution.py:37
  78.5 4.3 %collective-permute-done.5 = bf16[64,1024]{1,0:T(8,128)(2,1)S(1)} collective-permute-done((bf16[64,1024]{1,0:T(8,128)(2,1)S(1)}, bf16[64,1024]{1,0:T(8,128)(2,1)S(1)}, u32[]{:S(2)}, u32[]{:S(2)}) %collective-permute-start.5) | collective-permute-done | bytes 131104 | tf_op jit(solution)/shard_map/ppermute | solution.py:37
  83.7 6.6 %collective-permute-start.7 = (bf16[64,1024]{1,0:T(8,128)(2,1)S(1)}, bf16[64,1024]{1,0:T(8,128)(2,1)S(1)}, u32[]{:S(2)}, u32[]{:S(2)}) collective-permute-start(bf16[64,1024]{1,0:T(8,128)(2,1)S(1)} %convert_element_type.83), channel_id=1, source_target_pairs={{0,32},{32,0},{1,33},{33,1},{2,34},{34,2},{3,35},{35,3},{4,36},{36... | collective-permute-start | bytes 393224 | tf_op jit(solution)/shard_map/ppermute | solution.py:37
  91.4 10.0 %collective-permute-start.8 = (bf16[64,1024]{1,0:T(8,128)(2,1)S(1)}, bf16[64,1024]{1,0:T(8,128)(2,1)S(1)}, u32[]{:S(2)}, u32[]{:S(2)}) collective-permute-start(bf16[64,1024]{1,0:T(8,128)(2,1)S(1)} %pad_maximum_fusion.5), channel_id=1, source_target_pairs={{0,16},{8,24},{16,0},{24,8},{1,17},{9,25},{17,1},{25,9},{2,18},{10... | collective-permute-start | bytes 393224 | tf_op jit(solution)/shard_map/ppermute | solution.py:70
  101.4 3.4 %collective-permute-done.8 = bf16[64,1024]{1,0:T(8,128)(2,1)S(1)} collective-permute-done((bf16[64,1024]{1,0:T(8,128)(2,1)S(1)}, bf16[64,1024]{1,0:T(8,128)(2,1)S(1)}, u32[]{:S(2)}, u32[]{:S(2)}) %collective-permute-start.8) | collective-permute-done | bytes 131104 | tf_op jit(solution)/shard_map/ppermute | solution.py:70
  105.8 8.4 %all-to-all-start.3 = ((bf16[4,64,1024]{2,1,0:T(8,128)(2,1)}), bf16[4,64,1024]{2,1,0:T(8,128)(2,1)S(1)}, u32[]{:S(2)}, u32[]{:S(2)}) async-start(bf16[4,64,1024]{2,1,0:T(8,128)(2,1)} %broadcast_in_dim.8), calls=%async_computation.3 | async-start | bytes 1048576 | tf_op jit(solution)/shard_map/all_to_all | solution.py:41
  114.2 3.0 %collective-permute-start.10 = (bf16[16,2,16,1024]{3,2,1,0:T(8,128)(2,1)S(1)}, bf16[16,2,16,1024]{3,2,1,0:T(8,128)(2,1)}, u32[]{:S(2)}, u32[]{:S(2)}) collective-permute-start(bf16[16,2,16,1024]{3,2,1,0:T(8,128)(2,1)S(1)} %all-to-all-done.1.rows), channel_id=1, source_target_pairs={{0,64},{64,0},{1,65},{65,1},{2,66},{66,2},{3,67},{67,3},{4,68},{68... | collective-permute-start | bytes 3145736 | tf_op jit(solution)/shard_map/ppermute | solution.py:37
  118.3 4.0 %collective-permute-start.9 = (bf16[2,64,1024]{2,1,0:T(8,128)(2,1)S(1)}, bf16[2,64,1024]{2,1,0:T(8,128)(2,1)S(1)}, u32[]{:S(2)}, u32[]{:S(2)}) collective-permute-start(bf16[2,64,1024]{2,1,0:T(8,128)(2,1)S(1)} %pad_maximum_fusion.4), channel_id=1, source_target_pairs={{0,8},{8,0},{16,24},{24,16},{1,9},{9,1},{17,25},{25,17},{2,10},{10... | collective-permute-start | bytes 786440 | tf_op jit(solution)/shard_map/ppermute | solution.py:70
  122.3 2.3 %fusion.38 = (bf16[16,1,16,1024]{3,2,1,0:T(8,128)(2,1)}, bf16[16,1,16,1024]{3,2,1,0:T(8,128)(2,1)}) fusion(bf16[16,2,16,1024]{3,2,1,0:T(8,128)(2,1)} %collective-permute-done.6), kind=kLoop, calls=%fused_computation.77 | loop fusion | bytes 2097152 | tf_op jit(solution)/shard_map/slice | solution.py:171
  124.6 7.1 %collective-permute-done.9 = bf16[2,64,1024]{2,1,0:T(8,128)(2,1)S(1)} collective-permute-done((bf16[2,64,1024]{2,1,0:T(8,128)(2,1)S(1)}, bf16[2,64,1024]{2,1,0:T(8,128)(2,1)S(1)}, u32[]{:S(2)}, u32[]{:S(2)}) %collective-permute-start.9) | collective-permute-done | bytes 262176 | tf_op jit(solution)/shard_map/ppermute | solution.py:70
  135.6 4.3 %all-to-all-start.4 = ((bf16[16,2,16,1024]{3,2,1,0:T(8,128)(2,1)}), bf16[16,2,16,1024]{3,2,1,0:T(8,128)(2,1)}, u32[]{:S(2)}, u32[]{:S(2)}) async-start(bf16[16,2,16,1024]{3,2,1,0:T(8,128)(2,1)} %copy-done.11), calls=%async_computation.4 | async-start | bytes 2097152 | tf_op jit(solution)/shard_map/all_to_all | solution.py:41
  140.1 2.6 %collective-permute-start.11 = (bf16[512,512]{1,0:T(8,128)(2,1)S(1)}, bf16[512,512]{1,0:T(8,128)(2,1)}, u32[]{:S(2)}, u32[]{:S(2)}) collective-permute-start(bf16[512,512]{1,0:T(8,128)(2,1)S(1)} %fusion), channel_id=1, source_target_pairs={{0,64},{64,0},{1,65},{65,1},{2,66},{66,2},{3,67},{67,3},{4,68},{68... | collective-permute-start | bytes 1572872 | tf_op jit(solution)/shard_map/ppermute | solution.py:37
  148.5 7.9 %all-to-all-done.4 = bf16[16,2,16,1024]{3,2,1,0:T(8,128)(2,1)} async-done(((bf16[16,2,16,1024]{3,2,1,0:T(8,128)(2,1)}), bf16[16,2,16,1024]{3,2,1,0:T(8,128)(2,1)}, u32[]{:S(2)}, u32[]{:S(2)}) %all-to-all-start.4) | async-done | bytes 1048608 | tf_op jit(solution)/shard_map/all_to_all | solution.py:41
  156.4 4.5 %all-to-all-start.5 = ((bf16[16,2,16,1024]{3,2,1,0:T(8,128)(2,1)}), bf16[16,2,16,1024]{3,2,1,0:T(8,128)(2,1)}, u32[]{:S(2)}, u32[]{:S(2)}) async-start(bf16[16,2,16,1024]{3,2,1,0:T(8,128)(2,1)} %shard_map.78), calls=%async_computation.5 | async-start | bytes 2097152 | tf_op jit(solution)/shard_map/all_to_all | solution.py:41
  162.3 7.8 %collective-permute-start.12 = (bf16[2,16,1024]{2,1,0:T(8,128)(2,1)S(1)}, bf16[2,16,1024]{2,1,0:T(8,128)(2,1)S(1)}, u32[]{:S(2)}, u32[]{:S(2)}) collective-permute-start(bf16[2,16,1024]{2,1,0:T(8,128)(2,1)S(1)} %reduce_sum.32), channel_id=1, source_target_pairs={{0,1},{1,0},{2,3},{3,2},{4,5},{5,4},{6,7},{7,6},{8,9},{9,8},{10,11... | collective-permute-start | bytes 196616 | tf_op jit(solution)/shard_map/ppermute | solution.py:37
  (94 shorter events, 39.5 us)
Async XLA Ops:
  0.6 9.6 %copy-start = (bf16[1024,256]{1,0:T(8,128)(2,1)S(1)}, bf16[1024,256]{1,0:T(8,128)(2,1)}, u32[]{:S(2)}) copy-start(bf16[1024,256]{1,0:T(8,128)(2,1)} %in_a.7) | copy-start | bytes 1572868
  0.6 14.5 %copy-start.1 = (bf16[256,1024]{1,0:T(8,128)(2,1)S(1)}, bf16[256,1024]{1,0:T(8,128)(2,1)}, u32[]{:S(2)}) copy-start(bf16[256,1024]{1,0:T(8,128)(2,1)} %out_a.7) | copy-start | bytes 1572868
  2.6 27.9 %all-to-all-start = ((bf16[16,2,16,1024]{3,2,1,0:T(8,128)(2,1)}), bf16[16,2,16,1024]{3,2,1,0:T(8,128)(2,1)S(1)}, u32[]{:S(2)}, u32[]{:S(2)}) async-start(bf16[16,2,16,1024]{3,2,1,0:T(8,128)(2,1)} %broadcast_in_dim.6), calls=%async_computation | async-start | bytes 2097152 | tf_op jit(solution)/shard_map/all_to_all | solution.py:41
  10.2 20.3 %collective-permute-start = (bf16[1024,256]{1,0:T(8,128)(2,1)S(1)}, bf16[1024,256]{1,0:T(8,128)(2,1)S(1)}, u32[]{:S(2)}, u32[]{:S(2)}) collective-permute-start(bf16[1024,256]{1,0:T(8,128)(2,1)S(1)} %copy-done), channel_id=1, source_target_pairs={{0,64},{64,0},{1,65},{65,1},{2,66},{66,2},{3,67},{67,3},{4,68},{68... | collective-permute-start | bytes 1572872 | tf_op jit(solution)/shard_map/ppermute | solution.py:37
  15.1 15.4 %collective-permute-start.1 = (bf16[256,1024]{1,0:T(8,128)(2,1)S(1)}, bf16[256,1024]{1,0:T(8,128)(2,1)S(1)}, u32[]{:S(2)}, u32[]{:S(2)}) collective-permute-start(bf16[256,1024]{1,0:T(8,128)(2,1)S(1)} %copy-done.1), channel_id=1, source_target_pairs={{0,64},{64,0},{1,65},{65,1},{2,66},{66,2},{3,67},{67,3},{4,68},{68... | collective-permute-start | bytes 1572872 | tf_op jit(solution)/shard_map/ppermute | solution.py:37
  17.0 18.8 %collective-permute-start.4 = (bf16[2,16,1024]{2,1,0:T(8,128)(2,1)S(1)}, bf16[2,16,1024]{2,1,0:T(8,128)(2,1)S(1)}, u32[]{:S(2)}, u32[]{:S(2)}) collective-permute-start(bf16[2,16,1024]{2,1,0:T(8,128)(2,1)S(1)} %pad_maximum_fusion.7), channel_id=1, source_target_pairs={{0,1},{1,0},{2,3},{3,2},{4,5},{5,4},{6,7},{7,6},{8,9},{9,8},{10,11... | collective-permute-start | bytes 196616 | tf_op jit(solution)/shard_map/ppermute | solution.py:37
  33.2 10.7 %collective-permute-start.2 = (bf16[2,64,1024]{2,1,0:T(8,128)(2,1)}, bf16[2,64,1024]{2,1,0:T(8,128)(2,1)S(1)}, u32[]{:S(2)}, u32[]{:S(2)}) collective-permute-start(bf16[2,64,1024]{2,1,0:T(8,128)(2,1)} %fusion.7), channel_id=1, source_target_pairs={{0,8},{8,0},{16,24},{24,16},{1,9},{9,1},{17,25},{25,17},{2,10},{10... | collective-permute-start | bytes 786440 | tf_op jit(solution)/shard_map/ppermute | solution.py:65
  37.0 22.5 %all-to-all-start.1 = ((bf16[16,2,16,1024]{3,2,1,0:T(8,128)(2,1)}), bf16[16,2,16,1024]{3,2,1,0:T(8,128)(2,1)S(1)}, u32[]{:S(2)}, u32[]{:S(2)}) async-start(bf16[16,2,16,1024]{3,2,1,0:T(8,128)(2,1)} %broadcast_in_dim.7), calls=%async_computation.1 | async-start | bytes 2097152 | tf_op jit(solution)/shard_map/all_to_all | solution.py:41
  45.9 10.5 %collective-permute-start.3 = (bf16[64,1024]{1,0:T(8,128)(2,1)S(1)}, bf16[64,1024]{1,0:T(8,128)(2,1)S(1)}, u32[]{:S(2)}, u32[]{:S(2)}) collective-permute-start(bf16[64,1024]{1,0:T(8,128)(2,1)S(1)} %fusion.8), channel_id=1, source_target_pairs={{0,16},{8,24},{16,0},{24,8},{1,17},{9,25},{17,1},{25,9},{2,18},{10... | collective-permute-start | bytes 393224 | tf_op jit(solution)/shard_map/ppermute | solution.py:65
  63.1 20.4 %all-to-all-start.2 = ((bf16[4,64,1024]{2,1,0:T(8,128)(2,1)}), bf16[4,64,1024]{2,1,0:T(8,128)(2,1)S(1)}, u32[]{:S(2)}, u32[]{:S(2)}) async-start(bf16[4,64,1024]{2,1,0:T(8,128)(2,1)} %bitcast.50), calls=%async_computation.2 | async-start | bytes 1048576 | tf_op jit(solution)/shard_map/all_to_all | solution.py:41
  66.6 17.1 %collective-permute-start.6 = (bf16[16,2,16,1024]{3,2,1,0:T(8,128)(2,1)S(1)}, bf16[16,2,16,1024]{3,2,1,0:T(8,128)(2,1)}, u32[]{:S(2)}, u32[]{:S(2)}) collective-permute-start(bf16[16,2,16,1024]{3,2,1,0:T(8,128)(2,1)S(1)} %all-to-all-done.rows), channel_id=1, source_target_pairs={{0,64},{64,0},{1,65},{65,1},{2,66},{66,2},{3,67},{67,3},{4,68},{68... | collective-permute-start | bytes 3145736 | tf_op jit(solution)/shard_map/ppermute | solution.py:37
  71.5 11.3 %collective-permute-start.5 = (bf16[64,1024]{1,0:T(8,128)(2,1)S(1)}, bf16[64,1024]{1,0:T(8,128)(2,1)S(1)}, u32[]{:S(2)}, u32[]{:S(2)}) collective-permute-start(bf16[64,1024]{1,0:T(8,128)(2,1)S(1)} %convert_element_type.80), channel_id=1, source_target_pairs={{0,32},{32,0},{1,33},{33,1},{2,34},{34,2},{3,35},{35,3},{4,36},{36... | collective-permute-start | bytes 393224 | tf_op jit(solution)/shard_map/ppermute | solution.py:37
  83.7 17.7 %collective-permute-start.7 = (bf16[64,1024]{1,0:T(8,128)(2,1)S(1)}, bf16[64,1024]{1,0:T(8,128)(2,1)S(1)}, u32[]{:S(2)}, u32[]{:S(2)}) collective-permute-start(bf16[64,1024]{1,0:T(8,128)(2,1)S(1)} %convert_element_type.83), channel_id=1, source_target_pairs={{0,32},{32,0},{1,33},{33,1},{2,34},{34,2},{3,35},{35,3},{4,36},{36... | collective-permute-start | bytes 393224 | tf_op jit(solution)/shard_map/ppermute | solution.py:37
  91.4 13.4 %collective-permute-start.8 = (bf16[64,1024]{1,0:T(8,128)(2,1)S(1)}, bf16[64,1024]{1,0:T(8,128)(2,1)S(1)}, u32[]{:S(2)}, u32[]{:S(2)}) collective-permute-start(bf16[64,1024]{1,0:T(8,128)(2,1)S(1)} %pad_maximum_fusion.5), channel_id=1, source_target_pairs={{0,16},{8,24},{16,0},{24,8},{1,17},{9,25},{17,1},{25,9},{2,18},{10... | collective-permute-start | bytes 393224 | tf_op jit(solution)/shard_map/ppermute | solution.py:70
  105.8 26.1 %all-to-all-start.3 = ((bf16[4,64,1024]{2,1,0:T(8,128)(2,1)}), bf16[4,64,1024]{2,1,0:T(8,128)(2,1)S(1)}, u32[]{:S(2)}, u32[]{:S(2)}) async-start(bf16[4,64,1024]{2,1,0:T(8,128)(2,1)} %broadcast_in_dim.8), calls=%async_computation.3 | async-start | bytes 1048576 | tf_op jit(solution)/shard_map/all_to_all | solution.py:41
  114.2 17.6 %collective-permute-start.10 = (bf16[16,2,16,1024]{3,2,1,0:T(8,128)(2,1)S(1)}, bf16[16,2,16,1024]{3,2,1,0:T(8,128)(2,1)}, u32[]{:S(2)}, u32[]{:S(2)}) collective-permute-start(bf16[16,2,16,1024]{3,2,1,0:T(8,128)(2,1)S(1)} %all-to-all-done.1.rows), channel_id=1, source_target_pairs={{0,64},{64,0},{1,65},{65,1},{2,66},{66,2},{3,67},{67,3},{4,68},{68... | collective-permute-start | bytes 3145736 | tf_op jit(solution)/shard_map/ppermute | solution.py:37
  118.3 13.5 %copy-start.2 = (bf16[256,1024]{1,0:T(8,128)(2,1)S(1)}, bf16[256,1024]{1,0:T(8,128)(2,1)}, u32[]{:S(2)}) copy-start(bf16[256,1024]{1,0:T(8,128)(2,1)} %out_a.7) | copy-start | bytes 1572868
  118.3 13.4 %collective-permute-start.9 = (bf16[2,64,1024]{2,1,0:T(8,128)(2,1)S(1)}, bf16[2,64,1024]{2,1,0:T(8,128)(2,1)S(1)}, u32[]{:S(2)}, u32[]{:S(2)}) collective-permute-start(bf16[2,64,1024]{2,1,0:T(8,128)(2,1)S(1)} %pad_maximum_fusion.4), channel_id=1, source_target_pairs={{0,8},{8,0},{16,24},{24,16},{1,9},{9,1},{17,25},{25,17},{2,10},{10... | collective-permute-start | bytes 786440 | tf_op jit(solution)/shard_map/ppermute | solution.py:70
  135.6 20.8 %all-to-all-start.4 = ((bf16[16,2,16,1024]{3,2,1,0:T(8,128)(2,1)}), bf16[16,2,16,1024]{3,2,1,0:T(8,128)(2,1)}, u32[]{:S(2)}, u32[]{:S(2)}) async-start(bf16[16,2,16,1024]{3,2,1,0:T(8,128)(2,1)} %copy-done.11), calls=%async_computation.4 | async-start | bytes 2097152 | tf_op jit(solution)/shard_map/all_to_all | solution.py:41
  140.1 4.0 %copy-start.6 = (bf16[1024,256]{1,0:T(8,128)(2,1)S(1)}, bf16[1024,256]{1,0:T(8,128)(2,1)}, u32[]{:S(2)}) copy-start(bf16[1024,256]{1,0:T(8,128)(2,1)} %copy-done.3) | copy-start | bytes 1572868
  140.1 4.0 %copy-start.10 = (bf16[256,1024]{1,0:T(8,128)(2,1)S(1)}, bf16[256,1024]{1,0:T(8,128)(2,1)}, u32[]{:S(2)}) copy-start(bf16[256,1024]{1,0:T(8,128)(2,1)} %copy-done.7) | copy-start | bytes 1572868
  140.1 8.4 %collective-permute-start.11 = (bf16[512,512]{1,0:T(8,128)(2,1)S(1)}, bf16[512,512]{1,0:T(8,128)(2,1)}, u32[]{:S(2)}, u32[]{:S(2)}) collective-permute-start(bf16[512,512]{1,0:T(8,128)(2,1)S(1)} %fusion), channel_id=1, source_target_pairs={{0,64},{64,0},{1,65},{65,1},{2,66},{66,2},{3,67},{67,3},{4,68},{68... | collective-permute-start | bytes 1572872 | tf_op jit(solution)/shard_map/ppermute | solution.py:37
  156.4 19.8 %all-to-all-start.5 = ((bf16[16,2,16,1024]{3,2,1,0:T(8,128)(2,1)}), bf16[16,2,16,1024]{3,2,1,0:T(8,128)(2,1)}, u32[]{:S(2)}, u32[]{:S(2)}) async-start(bf16[16,2,16,1024]{3,2,1,0:T(8,128)(2,1)} %shard_map.78), calls=%async_computation.5 | async-start | bytes 2097152 | tf_op jit(solution)/shard_map/all_to_all | solution.py:41
  162.3 15.3 %collective-permute-start.12 = (bf16[2,16,1024]{2,1,0:T(8,128)(2,1)S(1)}, bf16[2,16,1024]{2,1,0:T(8,128)(2,1)S(1)}, u32[]{:S(2)}, u32[]{:S(2)}) collective-permute-start(bf16[2,16,1024]{2,1,0:T(8,128)(2,1)S(1)} %reduce_sum.32), channel_id=1, source_target_pairs={{0,1},{1,0},{2,3},{3,2},{4,5},{5,4},{6,7},{7,6},{8,9},{9,8},{10,11... | collective-permute-start | bytes 196616 | tf_op jit(solution)/shard_map/ppermute | solution.py:37
  (15 other events, 23.3 us)

commit v7 on v5

--- a/solution.py
+++ b/solution.py
@@ -164,12 +164,13 @@
     mid_far, mid_near = both(gather_four(middle(far_8)), double(mid_near, 1, 1))
     parts_far = last(mid_far)
     mid_near = mid_near.reshape(256, 4 * u)
-    far_sum = total_of(parts_far)
+    far_parts = exchange(parts_far)
     parts_near = last(mid_near)
 
     mids = jnp.concatenate([mid_near, mid_far])
     theirs = swap(mids[:, 2 * u :], "c")
-    far_sum, parts_near, mids, theirs = both(far_sum, parts_near, mids, theirs)
+    far_parts, parts_near, mids, theirs = both(far_parts, parts_near, mids, theirs)
+    far_sum = jnp.sum(far_parts.astype(f32), axis=0)
     act_all = jnp.concatenate([mids[:, :u], theirs[:, :u]])
     grad_all = jnp.concatenate([mids[:, u : 2 * u], theirs[:, u:]])
     grad_w_in = dot_tn(x_all, grad_all).astype(bf16)

time: 181 us -> 181 us (level)
  transfers between devices with their start and end apart: 19 -> 19, of which waited for: 6 -> 5; matrix products, arithmetic and copies ran while one was open for 13% -> 13% of each run, Pallas kernels for 1% -> 1%
where the time goes in v7:
time: 181 us; the launch traced here: 178 us
  starting transfers between devices  105 us (58%)
  waiting for transfers between devices  36.6 us (20%)
  local copies, waits for them, and re-layouts  16.9 us (9%)
  other arithmetic  12.2 us (7%)
  matrix products  3.08 us (2%)
  Pallas kernels  2.85 us (2%)
    ppermute x9, starting transfers between devices, swap(): return lax.ppermute(value, axis, [(0, 1), (1, 0)])  50.6 us
    all_to_all x6, starting transfers between devices, exchange(): return lax.all_to_all(value, axes, 0, 0, tiled=True)  33.9 us
    ppermute x2, starting transfers between devices, partner(): return lax.ppermute(value, 'zr', [(i, i ^ stride) for i in range(4)])  14.8 us
    all_to_all x6, waiting for transfers between devices, exchange(): return lax.all_to_all(value, axes, 0, 0, tiled=True)  13 us
    ppermute x2, waiting for transfers between devices, partner(): return lax.ppermute(value, 'zr', [(i, i ^ stride) for i in range(4)])  12.9 us
    ppermute x2, waiting for transfers between devices, halve(): lax.ppermute(send.astype(bf16), 'zr', [(i, i ^ stride) for i in range(4)])  7.4 us
    unnamed x38, local copies, waits for them, and re-layouts  6.08 us
    ppermute x2, starting transfers between devices, halve(): lax.ppermute(send.astype(bf16), 'zr', [(i, i ^ stride) for i in range(4)])  5.74 us
  transfers between devices with their start and end apart: 19, of which 5 were waited for; matrix products, arithmetic and copies ran while one was open for 13% of the time, Pallas kernels for 1%

profile of v7, /device:TPU:1, one launch (start us, length us, event | category | flops | bytes accessed | tf_op | source)
XLA Modules:
  0.0 177.8 jit_solution(10429642870456369639)
XLA Ops:
  2.6 7.6 %all-to-all-start = ((bf16[16,2,16,1024]{3,2,1,0:T(8,128)(2,1)}), bf16[16,2,16,1024]{3,2,1,0:T(8,128)(2,1)S(1)}, u32[]{:S(2)}, u32[]{:S(2)}) async-start(bf16[16,2,16,1024]{3,2,1,0:T(8,128)(2,1)} %broadcast_in_dim.6), calls=%async_computation | async-start | bytes 2097152 | tf_op jit(solution)/shard_map/all_to_all | solution.py:41
  10.2 4.9 %collective-permute-start = (bf16[1024,256]{1,0:T(8,128)(2,1)S(1)}, bf16[1024,256]{1,0:T(8,128)(2,1)S(1)}, u32[]{:S(2)}, u32[]{:S(2)}) collective-permute-start(bf16[1024,256]{1,0:T(8,128)(2,1)S(1)} %copy-done), channel_id=1, source_target_pairs={{0,64},{64,0},{1,65},{65,1},{2,66},{66,2},{3,67},{67,3},{4,68},{68... | collective-permute-start | bytes 1572872 | tf_op jit(solution)/shard_map/ppermute | solution.py:37
  15.1 1.9 %collective-permute-start.1 = (bf16[256,1024]{1,0:T(8,128)(2,1)S(1)}, bf16[256,1024]{1,0:T(8,128)(2,1)S(1)}, u32[]{:S(2)}, u32[]{:S(2)}) collective-permute-start(bf16[256,1024]{1,0:T(8,128)(2,1)S(1)} %copy-done.1), channel_id=1, source_target_pairs={{0,64},{64,0},{1,65},{65,1},{2,66},{66,2},{3,67},{67,3},{4,68},{68... | collective-permute-start | bytes 1572872 | tf_op jit(solution)/shard_map/ppermute | solution.py:37
  17.1 13.5 %collective-permute-start.4 = (bf16[2,16,1024]{2,1,0:T(8,128)(2,1)S(1)}, bf16[2,16,1024]{2,1,0:T(8,128)(2,1)S(1)}, u32[]{:S(2)}, u32[]{:S(2)}) collective-permute-start(bf16[2,16,1024]{2,1,0:T(8,128)(2,1)S(1)} %pad_maximum_fusion.7), channel_id=1, source_target_pairs={{0,1},{1,0},{2,3},{3,2},{4,5},{5,4},{6,7},{7,6},{8,9},{9,8},{10,11... | collective-permute-start | bytes 196616 | tf_op jit(solution)/shard_map/ppermute | solution.py:37
  33.2 2.6 %collective-permute-start.2 = (bf16[2,64,1024]{2,1,0:T(8,128)(2,1)}, bf16[2,64,1024]{2,1,0:T(8,128)(2,1)S(1)}, u32[]{:S(2)}, u32[]{:S(2)}) collective-permute-start(bf16[2,64,1024]{2,1,0:T(8,128)(2,1)} %fusion.7), channel_id=1, source_target_pairs={{0,8},{8,0},{16,24},{24,16},{1,9},{9,1},{17,25},{25,17},{2,10},{10... | collective-permute-start | bytes 786440 | tf_op jit(solution)/shard_map/ppermute | solution.py:65
  37.0 6.9 %all-to-all-start.1 = ((bf16[16,2,16,1024]{3,2,1,0:T(8,128)(2,1)}), bf16[16,2,16,1024]{3,2,1,0:T(8,128)(2,1)S(1)}, u32[]{:S(2)}, u32[]{:S(2)}) async-start(bf16[16,2,16,1024]{3,2,1,0:T(8,128)(2,1)} %broadcast_in_dim.7), calls=%async_computation.1 | async-start | bytes 2097152 | tf_op jit(solution)/shard_map/all_to_all | solution.py:41
  45.9 3.1 %collective-permute-start.3 = (bf16[64,1024]{1,0:T(8,128)(2,1)S(1)}, bf16[64,1024]{1,0:T(8,128)(2,1)S(1)}, u32[]{:S(2)}, u32[]{:S(2)}) collective-permute-start(bf16[64,1024]{1,0:T(8,128)(2,1)S(1)} %fusion.8), channel_id=1, source_target_pairs={{0,16},{8,24},{16,0},{24,8},{1,17},{9,25},{17,1},{25,9},{2,18},{10... | collective-permute-start | bytes 393224 | tf_op jit(solution)/shard_map/ppermute | solution.py:65
  49.0 7.4 %collective-permute-done.3 = bf16[64,1024]{1,0:T(8,128)(2,1)S(1)} collective-permute-done((bf16[64,1024]{1,0:T(8,128)(2,1)S(1)}, bf16[64,1024]{1,0:T(8,128)(2,1)S(1)}, u32[]{:S(2)}, u32[]{:S(2)}) %collective-permute-start.3) | collective-permute-done | bytes 131104 | tf_op jit(solution)/shard_map/ppermute | solution.py:65
  57.4 2.1 %all-to-all-done.1.rows = bf16[16,2,16,1024]{3,2,1,0:T(8,128)(2,1)S(1)} async-done(((bf16[16,2,16,1024]{3,2,1,0:T(8,128)(2,1)}), bf16[16,2,16,1024]{3,2,1,0:T(8,128)(2,1)S(1)}, u32[]{:S(2)}, u32[]{:S(2)}) %all-to-all-start.1) | async-done | bytes 1048608 | tf_op jit(solution)/shard_map/all_to_all | solution.py:41
  63.1 4.1 %all-to-all-start.2 = ((bf16[4,64,1024]{2,1,0:T(8,128)(2,1)}), bf16[4,64,1024]{2,1,0:T(8,128)(2,1)}, u32[]{:S(2)}, u32[]{:S(2)}) async-start(bf16[4,64,1024]{2,1,0:T(8,128)(2,1)} %bitcast.50), calls=%async_computation.2 | async-start | bytes 1048576 | tf_op jit(solution)/shard_map/all_to_all | solution.py:41
  67.3 4.8 %collective-permute-start.6 = (bf16[16,2,16,1024]{3,2,1,0:T(8,128)(2,1)S(1)}, bf16[16,2,16,1024]{3,2,1,0:T(8,128)(2,1)}, u32[]{:S(2)}, u32[]{:S(2)}) collective-permute-start(bf16[16,2,16,1024]{3,2,1,0:T(8,128)(2,1)S(1)} %all-to-all-done.rows), channel_id=1, source_target_pairs={{0,64},{64,0},{1,65},{65,1},{2,66},{66,2},{3,67},{67,3},{4,68},{68... | collective-permute-start | bytes 3145736 | tf_op jit(solution)/shard_map/ppermute | solution.py:37
  72.1 1.9 %collective-permute-start.7 = (bf16[16,2,16,1024]{3,2,1,0:T(8,128)(2,1)S(1)}, bf16[16,2,16,1024]{3,2,1,0:T(8,128)(2,1)}, u32[]{:S(2)}, u32[]{:S(2)}) collective-permute-start(bf16[16,2,16,1024]{3,2,1,0:T(8,128)(2,1)S(1)} %all-to-all-done.1.rows), channel_id=1, source_target_pairs={{0,64},{64,0},{1,65},{65,1},{2,66},{66,2},{3,67},{67,3},{4,68},{68... | collective-permute-start | bytes 3145736 | tf_op jit(solution)/shard_map/ppermute | solution.py:37
  75.1 6.4 %collective-permute-start.5 = (bf16[64,1024]{1,0:T(8,128)(2,1)S(1)}, bf16[64,1024]{1,0:T(8,128)(2,1)S(1)}, u32[]{:S(2)}, u32[]{:S(2)}) collective-permute-start(bf16[64,1024]{1,0:T(8,128)(2,1)S(1)} %convert_element_type.80), channel_id=1, source_target_pairs={{0,32},{32,0},{1,33},{33,1},{2,34},{34,2},{3,35},{35,3},{4,36},{36... | collective-permute-start | bytes 393224 | tf_op jit(solution)/shard_map/ppermute | solution.py:37
  82.6 3.3 %collective-permute-done.5 = bf16[64,1024]{1,0:T(8,128)(2,1)S(1)} collective-permute-done((bf16[64,1024]{1,0:T(8,128)(2,1)S(1)}, bf16[64,1024]{1,0:T(8,128)(2,1)S(1)}, u32[]{:S(2)}, u32[]{:S(2)}) %collective-permute-start.5) | collective-permute-done | bytes 131104 | tf_op jit(solution)/shard_map/ppermute | solution.py:37
  87.9 5.9 %collective-permute-start.8 = (bf16[64,1024]{1,0:T(8,128)(2,1)S(1)}, bf16[64,1024]{1,0:T(8,128)(2,1)S(1)}, u32[]{:S(2)}, u32[]{:S(2)}) collective-permute-start(bf16[64,1024]{1,0:T(8,128)(2,1)S(1)} %convert_element_type.83), channel_id=1, source_target_pairs={{0,32},{32,0},{1,33},{33,1},{2,34},{34,2},{3,35},{35,3},{4,36},{36... | collective-permute-start | bytes 393224 | tf_op jit(solution)/shard_map/ppermute | solution.py:37
  94.9 10.6 %collective-permute-start.9 = (bf16[64,1024]{1,0:T(8,128)(2,1)S(1)}, bf16[64,1024]{1,0:T(8,128)(2,1)S(1)}, u32[]{:S(2)}, u32[]{:S(2)}) collective-permute-start(bf16[64,1024]{1,0:T(8,128)(2,1)S(1)} %pad_maximum_fusion.5), channel_id=1, source_target_pairs={{0,16},{8,24},{16,0},{24,8},{1,17},{9,25},{17,1},{25,9},{2,18},{10... | collective-permute-start | bytes 393224 | tf_op jit(solution)/shard_map/ppermute | solution.py:70
  111.4 6.7 %all-to-all-start.3 = ((bf16[4,64,1024]{2,1,0:T(8,128)(2,1)}), bf16[4,64,1024]{2,1,0:T(8,128)(2,1)S(1)}, u32[]{:S(2)}, u32[]{:S(2)}) async-start(bf16[4,64,1024]{2,1,0:T(8,128)(2,1)} %broadcast_in_dim.8), calls=%async_computation.3 | async-start | bytes 1048576 | tf_op jit(solution)/shard_map/all_to_all | solution.py:41
  118.2 4.1 %collective-permute-start.10 = (bf16[2,64,1024]{2,1,0:T(8,128)(2,1)S(1)}, bf16[2,64,1024]{2,1,0:T(8,128)(2,1)S(1)}, u32[]{:S(2)}, u32[]{:S(2)}) collective-permute-start(bf16[2,64,1024]{2,1,0:T(8,128)(2,1)S(1)} %pad_maximum_fusion.4), channel_id=1, source_target_pairs={{0,8},{8,0},{16,24},{24,16},{1,9},{9,1},{17,25},{25,17},{2,10},{10... | collective-permute-start | bytes 786440 | tf_op jit(solution)/shard_map/ppermute | solution.py:70
  122.3 12.9 %collective-permute-done.10 = bf16[2,64,1024]{2,1,0:T(8,128)(2,1)S(1)} collective-permute-done((bf16[2,64,1024]{2,1,0:T(8,128)(2,1)S(1)}, bf16[2,64,1024]{2,1,0:T(8,128)(2,1)S(1)}, u32[]{:S(2)}, u32[]{:S(2)}) %collective-permute-start.10) | collective-permute-done | bytes 262176 | tf_op jit(solution)/shard_map/ppermute | solution.py:70
  137.0 4.3 %all-to-all-start.4 = ((bf16[16,2,16,1024]{3,2,1,0:T(8,128)(2,1)}), bf16[16,2,16,1024]{3,2,1,0:T(8,128)(2,1)}, u32[]{:S(2)}, u32[]{:S(2)}) async-start(bf16[16,2,16,1024]{3,2,1,0:T(8,128)(2,1)} %copy-done.9), calls=%async_computation.4 | async-start | bytes 2097152 | tf_op jit(solution)/shard_map/all_to_all | solution.py:41
  141.4 2.9 %collective-permute-start.11 = (bf16[512,512]{1,0:T(8,128)(2,1)S(1)}, bf16[512,512]{1,0:T(8,128)(2,1)}, u32[]{:S(2)}, u32[]{:S(2)}) collective-permute-start(bf16[512,512]{1,0:T(8,128)(2,1)S(1)} %fusion), channel_id=1, source_target_pairs={{0,64},{64,0},{1,65},{65,1},{2,66},{66,2},{3,67},{67,3},{4,68},{68... | collective-permute-start | bytes 1572872 | tf_op jit(solution)/shard_map/ppermute | solution.py:37
  146.5 10.8 %all-to-all-done.4 = bf16[16,2,16,1024]{3,2,1,0:T(8,128)(2,1)} async-done(((bf16[16,2,16,1024]{3,2,1,0:T(8,128)(2,1)}), bf16[16,2,16,1024]{3,2,1,0:T(8,128)(2,1)}, u32[]{:S(2)}, u32[]{:S(2)}) %all-to-all-start.4) | async-done | bytes 1048608 | tf_op jit(solution)/shard_map/all_to_all | solution.py:41
  157.3 4.2 %all-to-all-start.5 = ((bf16[16,2,16,1024]{3,2,1,0:T(8,128)(2,1)}), bf16[16,2,16,1024]{3,2,1,0:T(8,128)(2,1)S(1)}, u32[]{:S(2)}, u32[]{:S(2)}) async-start(bf16[16,2,16,1024]{3,2,1,0:T(8,128)(2,1)} %copy-done.8), calls=%async_computation.5 | async-start | bytes 2097152 | tf_op jit(solution)/shard_map/all_to_all | solution.py:41
  163.1 8.4 %collective-permute-start.12 = (bf16[2,16,1024]{2,1,0:T(8,128)(2,1)S(1)}, bf16[2,16,1024]{2,1,0:T(8,128)(2,1)S(1)}, u32[]{:S(2)}, u32[]{:S(2)}) collective-permute-start(bf16[2,16,1024]{2,1,0:T(8,128)(2,1)S(1)} %reduce_sum.32), channel_id=1, source_target_pairs={{0,1},{1,0},{2,3},{3,2},{4,5},{5,4},{6,7},{7,6},{8,9},{9,8},{10,11... | collective-permute-start | bytes 196616 | tf_op jit(solution)/shard_map/ppermute | solution.py:37
  (92 shorter events, 35.0 us)
Async XLA Ops:
  0.6 14.5 %copy-start.1 = (bf16[256,1024]{1,0:T(8,128)(2,1)S(1)}, bf16[256,1024]{1,0:T(8,128)(2,1)}, u32[]{:S(2)}) copy-start(bf16[256,1024]{1,0:T(8,128)(2,1)} %out_a.7) | copy-start | bytes 1572868
  2.6 27.9 %all-to-all-start = ((bf16[16,2,16,1024]{3,2,1,0:T(8,128)(2,1)}), bf16[16,2,16,1024]{3,2,1,0:T(8,128)(2,1)S(1)}, u32[]{:S(2)}, u32[]{:S(2)}) async-start(bf16[16,2,16,1024]{3,2,1,0:T(8,128)(2,1)} %broadcast_in_dim.6), calls=%async_computation | async-start | bytes 2097152 | tf_op jit(solution)/shard_map/all_to_all | solution.py:41
  10.2 20.3 %collective-permute-start = (bf16[1024,256]{1,0:T(8,128)(2,1)S(1)}, bf16[1024,256]{1,0:T(8,128)(2,1)S(1)}, u32[]{:S(2)}, u32[]{:S(2)}) collective-permute-start(bf16[1024,256]{1,0:T(8,128)(2,1)S(1)} %copy-done), channel_id=1, source_target_pairs={{0,64},{64,0},{1,65},{65,1},{2,66},{66,2},{3,67},{67,3},{4,68},{68... | collective-permute-start | bytes 1572872 | tf_op jit(solution)/shard_map/ppermute | solution.py:37
  15.1 15.4 %collective-permute-start.1 = (bf16[256,1024]{1,0:T(8,128)(2,1)S(1)}, bf16[256,1024]{1,0:T(8,128)(2,1)S(1)}, u32[]{:S(2)}, u32[]{:S(2)}) collective-permute-start(bf16[256,1024]{1,0:T(8,128)(2,1)S(1)} %copy-done.1), channel_id=1, source_target_pairs={{0,64},{64,0},{1,65},{65,1},{2,66},{66,2},{3,67},{67,3},{4,68},{68... | collective-permute-start | bytes 1572872 | tf_op jit(solution)/shard_map/ppermute | solution.py:37
  17.1 18.8 %collective-permute-start.4 = (bf16[2,16,1024]{2,1,0:T(8,128)(2,1)S(1)}, bf16[2,16,1024]{2,1,0:T(8,128)(2,1)S(1)}, u32[]{:S(2)}, u32[]{:S(2)}) collective-permute-start(bf16[2,16,1024]{2,1,0:T(8,128)(2,1)S(1)} %pad_maximum_fusion.7), channel_id=1, source_target_pairs={{0,1},{1,0},{2,3},{3,2},{4,5},{5,4},{6,7},{7,6},{8,9},{9,8},{10,11... | collective-permute-start | bytes 196616 | tf_op jit(solution)/shard_map/ppermute | solution.py:37
  33.2 10.7 %collective-permute-start.2 = (bf16[2,64,1024]{2,1,0:T(8,128)(2,1)}, bf16[2,64,1024]{2,1,0:T(8,128)(2,1)S(1)}, u32[]{:S(2)}, u32[]{:S(2)}) collective-permute-start(bf16[2,64,1024]{2,1,0:T(8,128)(2,1)} %fusion.7), channel_id=1, source_target_pairs={{0,8},{8,0},{16,24},{24,16},{1,9},{9,1},{17,25},{25,17},{2,10},{10... | collective-permute-start | bytes 786440 | tf_op jit(solution)/shard_map/ppermute | solution.py:65
  37.0 22.5 %all-to-all-start.1 = ((bf16[16,2,16,1024]{3,2,1,0:T(8,128)(2,1)}), bf16[16,2,16,1024]{3,2,1,0:T(8,128)(2,1)S(1)}, u32[]{:S(2)}, u32[]{:S(2)}) async-start(bf16[16,2,16,1024]{3,2,1,0:T(8,128)(2,1)} %broadcast_in_dim.7), calls=%async_computation.1 | async-start | bytes 2097152 | tf_op jit(solution)/shard_map/all_to_all | solution.py:41
  45.9 10.5 %collective-permute-start.3 = (bf16[64,1024]{1,0:T(8,128)(2,1)S(1)}, bf16[64,1024]{1,0:T(8,128)(2,1)S(1)}, u32[]{:S(2)}, u32[]{:S(2)}) collective-permute-start(bf16[64,1024]{1,0:T(8,128)(2,1)S(1)} %fusion.8), channel_id=1, source_target_pairs={{0,16},{8,24},{16,0},{24,8},{1,17},{9,25},{17,1},{25,9},{2,18},{10... | collective-permute-start | bytes 393224 | tf_op jit(solution)/shard_map/ppermute | solution.py:65
  63.1 23.6 %all-to-all-start.2 = ((bf16[4,64,1024]{2,1,0:T(8,128)(2,1)}), bf16[4,64,1024]{2,1,0:T(8,128)(2,1)}, u32[]{:S(2)}, u32[]{:S(2)}) async-start(bf16[4,64,1024]{2,1,0:T(8,128)(2,1)} %bitcast.50), calls=%async_computation.2 | async-start | bytes 1048576 | tf_op jit(solution)/shard_map/all_to_all | solution.py:41
  67.3 20.6 %collective-permute-start.6 = (bf16[16,2,16,1024]{3,2,1,0:T(8,128)(2,1)S(1)}, bf16[16,2,16,1024]{3,2,1,0:T(8,128)(2,1)}, u32[]{:S(2)}, u32[]{:S(2)}) collective-permute-start(bf16[16,2,16,1024]{3,2,1,0:T(8,128)(2,1)S(1)} %all-to-all-done.rows), channel_id=1, source_target_pairs={{0,64},{64,0},{1,65},{65,1},{2,66},{66,2},{3,67},{67,3},{4,68},{68... | collective-permute-start | bytes 3145736 | tf_op jit(solution)/shard_map/ppermute | solution.py:37
  72.1 15.7 %collective-permute-start.7 = (bf16[16,2,16,1024]{3,2,1,0:T(8,128)(2,1)S(1)}, bf16[16,2,16,1024]{3,2,1,0:T(8,128)(2,1)}, u32[]{:S(2)}, u32[]{:S(2)}) collective-permute-start(bf16[16,2,16,1024]{3,2,1,0:T(8,128)(2,1)S(1)} %all-to-all-done.1.rows), channel_id=1, source_target_pairs={{0,64},{64,0},{1,65},{65,1},{2,66},{66,2},{3,67},{67,3},{4,68},{68... | collective-permute-start | bytes 3145736 | tf_op jit(solution)/shard_map/ppermute | solution.py:37
  75.1 10.8 %collective-permute-start.5 = (bf16[64,1024]{1,0:T(8,128)(2,1)S(1)}, bf16[64,1024]{1,0:T(8,128)(2,1)S(1)}, u32[]{:S(2)}, u32[]{:S(2)}) collective-permute-start(bf16[64,1024]{1,0:T(8,128)(2,1)S(1)} %convert_element_type.80), channel_id=1, source_target_pairs={{0,32},{32,0},{1,33},{33,1},{2,34},{34,2},{3,35},{35,3},{4,36},{36... | collective-permute-start | bytes 393224 | tf_op jit(solution)/shard_map/ppermute | solution.py:37
  87.9 22.5 %collective-permute-start.8 = (bf16[64,1024]{1,0:T(8,128)(2,1)S(1)}, bf16[64,1024]{1,0:T(8,128)(2,1)S(1)}, u32[]{:S(2)}, u32[]{:S(2)}) collective-permute-start(bf16[64,1024]{1,0:T(8,128)(2,1)S(1)} %convert_element_type.83), channel_id=1, source_target_pairs={{0,32},{32,0},{1,33},{33,1},{2,34},{34,2},{3,35},{35,3},{4,36},{36... | collective-permute-start | bytes 393224 | tf_op jit(solution)/shard_map/ppermute | solution.py:37
  94.9 12.5 %copy-start.15 = (bf16[16,1,16,1024]{3,2,1,0:T(8,128)(2,1)S(1)}, bf16[16,1,16,1024]{3,2,1,0:T(8,128)(2,1)}, u32[]{:S(2)}) copy-start(bf16[16,1,16,1024]{3,2,1,0:T(8,128)(2,1)} %get-tuple-element.43) | copy-start | bytes 1572868
  94.9 12.5 %copy-start.17 = (bf16[16,1,16,1024]{3,2,1,0:T(8,128)(2,1)S(1)}, bf16[16,1,16,1024]{3,2,1,0:T(8,128)(2,1)}, u32[]{:S(2)}) copy-start(bf16[16,1,16,1024]{3,2,1,0:T(8,128)(2,1)} %get-tuple-element.45) | copy-start | bytes 1572868
  94.9 15.6 %collective-permute-start.9 = (bf16[64,1024]{1,0:T(8,128)(2,1)S(1)}, bf16[64,1024]{1,0:T(8,128)(2,1)S(1)}, u32[]{:S(2)}, u32[]{:S(2)}) collective-permute-start(bf16[64,1024]{1,0:T(8,128)(2,1)S(1)} %pad_maximum_fusion.5), channel_id=1, source_target_pairs={{0,16},{8,24},{16,0},{24,8},{1,17},{9,25},{17,1},{25,9},{2,18},{10... | collective-permute-start | bytes 393224 | tf_op jit(solution)/shard_map/ppermute | solution.py:70
  111.4 23.9 %copy-start.4 = (bf16[1024,256]{1,0:T(8,128)(2,1)S(1)}, bf16[1024,256]{1,0:T(8,128)(2,1)}, u32[]{:S(2)}) copy-start(bf16[1024,256]{1,0:T(8,128)(2,1)} %copy-done.2) | copy-start | bytes 1572868
  111.4 23.9 %copy-start.7 = (bf16[256,1024]{1,0:T(8,128)(2,1)S(1)}, bf16[256,1024]{1,0:T(8,128)(2,1)}, u32[]{:S(2)}) copy-start(bf16[256,1024]{1,0:T(8,128)(2,1)} %copy-done.5) | copy-start | bytes 1572868
  111.4 23.9 %all-to-all-start.3 = ((bf16[4,64,1024]{2,1,0:T(8,128)(2,1)}), bf16[4,64,1024]{2,1,0:T(8,128)(2,1)S(1)}, u32[]{:S(2)}, u32[]{:S(2)}) async-start(bf16[4,64,1024]{2,1,0:T(8,128)(2,1)} %broadcast_in_dim.8), calls=%async_computation.3 | async-start | bytes 1048576 | tf_op jit(solution)/shard_map/all_to_all | solution.py:41
  118.2 17.0 %collective-permute-start.10 = (bf16[2,64,1024]{2,1,0:T(8,128)(2,1)S(1)}, bf16[2,64,1024]{2,1,0:T(8,128)(2,1)S(1)}, u32[]{:S(2)}, u32[]{:S(2)}) collective-permute-start(bf16[2,64,1024]{2,1,0:T(8,128)(2,1)S(1)} %pad_maximum_fusion.4), channel_id=1, source_target_pairs={{0,8},{8,0},{16,24},{24,16},{1,9},{9,1},{17,25},{25,17},{2,10},{10... | collective-permute-start | bytes 786440 | tf_op jit(solution)/shard_map/ppermute | solution.py:70
  137.0 20.3 %all-to-all-start.4 = ((bf16[16,2,16,1024]{3,2,1,0:T(8,128)(2,1)}), bf16[16,2,16,1024]{3,2,1,0:T(8,128)(2,1)}, u32[]{:S(2)}, u32[]{:S(2)}) async-start(bf16[16,2,16,1024]{3,2,1,0:T(8,128)(2,1)} %copy-done.9), calls=%async_computation.4 | async-start | bytes 2097152 | tf_op jit(solution)/shard_map/all_to_all | solution.py:41
  141.4 5.1 %collective-permute-start.11 = (bf16[512,512]{1,0:T(8,128)(2,1)S(1)}, bf16[512,512]{1,0:T(8,128)(2,1)}, u32[]{:S(2)}, u32[]{:S(2)}) collective-permute-start(bf16[512,512]{1,0:T(8,128)(2,1)S(1)} %fusion), channel_id=1, source_target_pairs={{0,64},{64,0},{1,65},{65,1},{2,66},{66,2},{3,67},{67,3},{4,68},{68... | collective-permute-start | bytes 1572872 | tf_op jit(solution)/shard_map/ppermute | solution.py:37
  157.3 19.6 %all-to-all-start.5 = ((bf16[16,2,16,1024]{3,2,1,0:T(8,128)(2,1)}), bf16[16,2,16,1024]{3,2,1,0:T(8,128)(2,1)S(1)}, u32[]{:S(2)}, u32[]{:S(2)}) async-start(bf16[16,2,16,1024]{3,2,1,0:T(8,128)(2,1)} %copy-done.8), calls=%async_computation.5 | async-start | bytes 2097152 | tf_op jit(solution)/shard_map/all_to_all | solution.py:41
  163.1 14.0 %collective-permute-start.12 = (bf16[2,16,1024]{2,1,0:T(8,128)(2,1)S(1)}, bf16[2,16,1024]{2,1,0:T(8,128)(2,1)S(1)}, u32[]{:S(2)}, u32[]{:S(2)}) collective-permute-start(bf16[2,16,1024]{2,1,0:T(8,128)(2,1)S(1)} %reduce_sum.32), channel_id=1, source_target_pairs={{0,1},{1,0},{2,3},{3,2},{4,5},{5,4},{6,7},{7,6},{8,9},{9,8},{10,11... | collective-permute-start | bytes 196616 | tf_op jit(solution)/shard_map/ppermute | solution.py:37
  (14 other events, 36.6 us)
